TPU v7x, 256 devices: a whole 4x4x8 slice. The times are simulated.
256 devices in a mesh: dp: 16 (over z_hi, x), seq: 16 (over y, z_lo, core).
Axes of the slice: x: 4, y: 4, z: 8 (z_hi: 4, z_lo: 2; z = z_hi * 2 + z_lo), core: 2. Of those that a mesh axis runs over, the one named last changes fastest.
Arguments:
- queries: bfloat16 [16, 4096, 1024], P('dp', 'seq'), may hold values from -4.5 to 4.5
- keys: bfloat16 [16, 4096, 1024], P('dp', 'seq'), may hold values from -4.5 to 4.5
- values: bfloat16 [16, 4096, 1024], P('dp', 'seq'), may hold values from -6 to 6
- d_out: bfloat16 [16, 4096, 2048], P('dp', 'seq'), may hold values from -6 to 6
- w_out: bfloat16 [2048, 1024], replicated, may hold values from -0.1875 to 0.1875
Outputs:
- d_queries: bfloat16 [16, 4096, 1024], P('dp', 'seq')
- d_keys: bfloat16 [16, 4096, 1024], P('dp', 'seq')
- d_values: bfloat16 [16, 4096, 1024], P('dp', 'seq')
- d_weight: float32 [2048, 1024], P('seq')
All inputs are finite; a program needn't handle non-finite values.
Results may differ from a plain program's by a relative error of at most 0.024.
Values may be sent and summed in bfloat16 or wider, within the bound.
No kernel may reach another device: no remote copies, remote signals or barrier semaphores. Data moves between devices by JAX's collectives and lax.ppermute only.
A program may use at most 128 MiB of HBM per device.

v0:
```python
import jax
import jax.numpy as jnp
from jax import lax
from jax.sharding import PartitionSpec as P

HEADS = 8
HDIM = 128
BLOCK = 128


def from_partner(value, axis, stride):
    mask = 2**stride
    pairs = [(source, source ^ mask) for source in range(lax.axis_size(axis))]
    return lax.ppermute(value, axis, pairs)


def coarsen(matrix):
    paired_rows = matrix.astype(jnp.float32).reshape(matrix.shape[0] // 2, 2, matrix.shape[1])
    return ((paired_rows[:, 0] + paired_rows[:, 1]) * 0.5).astype(jnp.bfloat16)


def flip_pairs(tensor):
    layout = tensor.shape
    return tensor.reshape((layout[0] // 2, 2) + layout[1:])[:, ::-1].reshape(layout)


def to_tokens(tensor):
    return jnp.transpose(tensor, (1, 0, 2)).reshape(tensor.shape[1], -1)


def to_groups(tensor, groups):
    return jnp.transpose(tensor.reshape(tensor.shape[0], groups, -1), (1, 0, 2))


def spread(gradient):
    return jnp.repeat(gradient * 0.5, 2, axis=0)


def level_weights(raw_scores, height, row_peak, groups):
    return 2.0**height * jnp.exp(
        jnp.repeat(raw_scores, 2**height, axis=2) - to_groups(row_peak, groups)[..., None]
    )


def per_device(queries, keys, values, d_out, w_out):
    tok_q = queries[0]
    tok_k = keys[0]
    tok_v = values[0]
    grad_out = d_out[0]
    tok_count = tok_q.shape[0]
    width = tok_q.shape[1]
    seq_size = lax.axis_size("seq")
    cross_levels = seq_size.bit_length() - 1
    local_levels = (tok_count // BLOCK).bit_length() - 1
    levels = local_levels + cross_levels
    score_scale = HDIM ** (-0.5)
    position = lax.axis_index("seq")
    coarse_q = [tok_q]
    for height in range(1, levels):
        coarse_q.append(coarsen(coarse_q[-1]))
    coarse_k = [tok_k]
    coarse_v = [tok_v]
    height = 1
    coarse_k.append(coarsen(coarse_k[-1]))
    coarse_v.append(coarsen(coarse_v[-1]))
    far_k = []
    far_v = []
    own_k = coarse_k[local_levels]
    own_v = coarse_v[local_levels]
    for bit_idx in range(cross_levels):
        sib_k, sib_v = from_partner((own_k, own_v), "seq", bit_idx)
        far_k.append(sib_k)
        far_v.append(sib_v)
        if bit_idx + 1 < cross_levels:
            is_lower = position // 2**bit_idx % 2 == 0
            own_k = coarsen(
                jnp.where(
                    is_lower, jnp.concatenate([own_k, sib_k]), jnp.concatenate([sib_k, own_k])
                )
            )
            own_v = coarsen(
                jnp.where(
                    is_lower, jnp.concatenate([own_v, sib_v]), jnp.concatenate([sib_v, own_v])
                )
            )
    level_data = []
    for height in range(levels):
        if height < local_levels:
            groups = tok_count // (BLOCK * 2**height)
            q_heads = coarse_q[height].reshape(groups, BLOCK, HEADS, HDIM)
            k_heads = coarse_k[height].reshape(groups, BLOCK, HEADS, HDIM)
            v_heads = coarse_v[height].reshape(groups, BLOCK, HEADS, HDIM)
            k_group = jnp.concatenate([k_heads, flip_pairs(k_heads)], axis=1)
            v_group = jnp.concatenate([v_heads, flip_pairs(v_heads)], axis=1)
        else:
            q_heads = coarse_q[height].reshape(1, -1, HEADS, HDIM)
            k_group = far_k[height - local_levels].reshape(1, BLOCK, HEADS, HDIM)
            v_group = far_v[height - local_levels].reshape(1, BLOCK, HEADS, HDIM)
        level_data.append((q_heads, k_group, v_group))
    raw_list = []
    row_peak = None
    for height, (q_heads, k_group, v_group) in enumerate(level_data):
        raw_scores = (
            jnp.einsum("grhd,gjhd->ghrj", q_heads, k_group, preferred_element_type=jnp.float32)
            * score_scale
        )
        level_peak = to_tokens(jnp.repeat(jnp.max(raw_scores, axis=3), 2**height, axis=2))
        row_peak = level_peak if height == 0 else jnp.maximum(row_peak, level_peak)
        raw_list.append(raw_scores)
    normaliser = jnp.zeros((HEADS, tok_count), jnp.float32)
    numerator = jnp.zeros((tok_count, HEADS, HDIM), jnp.float32)
    for height, (q_heads, k_group, v_group) in enumerate(level_data):
        groups = q_heads.shape[0]
        weights = level_weights(raw_list[height], height, row_peak, groups)
        normaliser = normaliser + to_tokens(jnp.sum(weights, axis=3))
        numerator = numerator + jnp.einsum(
            "ghfj,gjhd->gfhd",
            weights.astype(jnp.bfloat16),
            v_group,
            preferred_element_type=jnp.float32,
        ).reshape(tok_count, HEADS, HDIM)
    attended = (
        (numerator / jnp.transpose(normaliser)[:, :, None])
        .astype(jnp.bfloat16)
        .reshape(tok_count, width)
    )
    d_attended = jnp.dot(grad_out, w_out, preferred_element_type=jnp.float32).astype(jnp.bfloat16)
    dout_heads = d_attended.reshape(tok_count, HEADS, HDIM)
    row_delta = jnp.transpose(
        jnp.sum(
            dout_heads.astype(jnp.float32)
            * attended.astype(jnp.float32).reshape(tok_count, HEADS, HDIM),
            axis=2,
        )
    )
    grad_q = []
    grad_k = []
    grad_v = []
    part_k = []
    part_v = []
    for height, (q_heads, k_group, v_group) in enumerate(level_data):
        groups = q_heads.shape[0]
        q_rows = q_heads.shape[1]
        repeats = 2**height
        key_count = k_group.shape[1]
        probability = (
            level_weights(raw_list[height], height, row_peak, groups)
            / to_groups(normaliser, groups)[..., None]
        )
        dout_group = dout_heads.reshape(groups, -1, HEADS, HDIM)
        prob_grad = jnp.einsum(
            "gfhd,gjhd->ghfj", dout_group, v_group, preferred_element_type=jnp.float32
        )
        score_grad = probability * (prob_grad - to_groups(row_delta, groups)[..., None])
        value_part = jnp.einsum(
            "ghfj,gfhd->gjhd",
            probability.astype(jnp.bfloat16),
            dout_group,
            preferred_element_type=jnp.float32,
        )
        coarse_grad = jnp.sum(
            score_grad.reshape(groups, HEADS, q_rows, repeats, key_count), axis=3
        ).astype(jnp.bfloat16)
        grad_q.append(
            (
                jnp.einsum(
                    "ghrj,gjhd->grhd", coarse_grad, k_group, preferred_element_type=jnp.float32
                )
                * score_scale
            ).reshape(-1, width)
        )
        key_part = (
            jnp.einsum("ghrj,grhd->gjhd", coarse_grad, q_heads, preferred_element_type=jnp.float32)
            * score_scale
        )
        if height == 0:
            grad_k.append(
                (key_part[:, :BLOCK] + flip_pairs(key_part[:, BLOCK:])).reshape(-1, width)
            )
            grad_v.append(
                (value_part[:, :BLOCK] + flip_pairs(value_part[:, BLOCK:])).reshape(-1, width)
            )
        else:
            part_k.append(key_part[0].reshape(BLOCK, width))
            part_v.append(value_part[0].reshape(BLOCK, width))
    carry_k = None
    carry_v = None
    for bit_idx in reversed(range(cross_levels)):
        send_k = part_k[bit_idx]
        send_v = part_v[bit_idx]
        keep_k = None
        keep_v = None
        if carry_k is not None:
            is_lower = position // 2**bit_idx % 2 == 0
            wide_k = spread(carry_k)
            wide_v = spread(carry_v)
            keep_k = jnp.where(is_lower, wide_k[:BLOCK], wide_k[BLOCK:])
            keep_v = jnp.where(is_lower, wide_v[:BLOCK], wide_v[BLOCK:])
            send_k = send_k + jnp.where(is_lower, wide_k[BLOCK:], wide_k[:BLOCK])
            send_v = send_v + jnp.where(is_lower, wide_v[BLOCK:], wide_v[:BLOCK])
        got_k, got_v = from_partner((send_k, send_v), "seq", bit_idx)
        carry_k = got_k if keep_k is None else got_k + keep_k
        carry_v = got_v if keep_v is None else got_v + keep_v
    grad_k.append(carry_k)
    grad_v.append(carry_v)
    height = 1
    grad_k[height - 1] = grad_k[height - 1] + spread(grad_k[height])
    grad_v[height - 1] = grad_v[height - 1] + spread(grad_v[height])
    for height in range(levels - 1, 0, -1):
        grad_q[height - 1] = grad_q[height - 1] + spread(grad_q[height])
    shares = lax.psum_scatter(
        jnp.einsum("tr,te->re", grad_out, attended, preferred_element_type=jnp.float32),
        "seq",
        scatter_dimension=0,
        tiled=True,
    )
    d_weight = lax.psum(shares, "dp")
    d_queries = grad_q[0].astype(jnp.bfloat16)[None]
    d_keys = grad_k[0].astype(jnp.bfloat16)[None]
    d_values = grad_v[0].astype(jnp.bfloat16)[None]
    return (d_queries, d_keys, d_values, d_weight)


def solution(mesh):
    in_specs = (
        P("dp", "seq", None),
        P("dp", "seq", None),
        P("dp", "seq", None),
        P("dp", "seq", None),
        P(),
    )
    out_specs = (P("dp", "seq", None), P("dp", "seq", None), P("dp", "seq", None), P("seq", None))
    return jax.shard_map(
        per_device, mesh=mesh, in_specs=in_specs, out_specs=out_specs, check_vma=False
    )
```

profile of v0, /device:TPU:32, one launch (start us, length us, event | category | flops | bytes accessed | tf_op | source)
XLA Modules:
  0.0 474.3 jit_solution(9442952296988886307)
XLA Ops:
  7.2 1.8 reshape.917
  20.2 2.0 copy-done.91
  23.6 1.8 bitcast_reduce_fusion
  30.9 3.0 fusion.50
  33.8 2.8 reshape.919
  36.7 2.4 fusion.158
  40.0 2.0 collective-permute-start.1
  42.0 1.6 reshape.925
  43.7 3.5 fusion.162
  53.3 1.8 copy.1031
  55.1 2.4 fusion.51
  57.5 1.8 reshape.921
  62.6 2.2 fusion.54
  64.8 1.8 reshape.926
  66.6 1.8 fusion.161
  69.6 1.9 fusion.165
  77.2 1.8 copy.1038
  78.9 2.4 fusion.52
  81.3 1.8 reshape.923
  84.9 3.6 collective-permute-start.3
  88.5 2.3 fusion.55
  90.8 1.8 reshape.927
  92.7 1.8 fusion.160
  95.6 1.8 fusion.164
  99.7 2.1 fusion.102
  120.4 2.0 fusion.14
  122.5 1.7 convolution_bitcast_fusion.6
  126.4 2.2 fusion.28
  128.6 2.4 convolution_bitcast_fusion.3
  138.0 4.6 convolution_bitcast_fusion
  144.6 2.7 multiply_convert_fusion
  148.8 2.6 copy.1052
  151.4 2.4 reshape.898
  155.1 2.8 fusion.16
  159.8 3.1 fusion.4
  162.9 1.9 reduce_sum.101
  166.7 2.0 copy.1069
  168.7 3.1 fusion.5
  171.8 2.5 reduce_sum.100
  175.4 2.0 copy.1056
  177.5 2.0 fusion.74
  179.5 2.0 copy.1070
  181.6 2.4 broadcast_in_dim.215
  183.9 2.9 reshape.909
  190.2 2.4 reshape.911
  193.9 3.4 collective-permute-start.8
  200.4 2.3 convolution_bitcast_fusion.1
  204.3 2.4 reshape.914
  208.1 1.7 fusion.77
  211.3 1.8 fusion.79
  216.3 10.5 %collective-permute-start.9 = (f32[128,1024]{0,1:T(8,128)}, f32[128,1024]{0,1:T(8,128)}, u32[]{:S(2)}, u32[]{:S(2)}) collective-permute-start(f32[128,1024]{0,1:T(8,128)} %bitcast_add_fusion.3), channel_id=1, source_target_pairs={{0,4},{1,5},{2,6},{3,7},{4,0},{5,1},{6,2},{7,3},{8,12},{9,13},{10,... | collective-permute-start | bytes 1572872 | tf_op jit(solution)/shard_map/ppermute | solution.py:14
  230.9 17.8 %collective-permute-start.13 = (f32[128,1024]{0,1:T(8,128)}, f32[128,1024]{0,1:T(8,128)}, u32[]{:S(2)}, u32[]{:S(2)}) collective-permute-start(f32[128,1024]{0,1:T(8,128)} %bitcast_add_fusion), channel_id=1, source_target_pairs={{0,4},{1,5},{2,6},{3,7},{4,0},{5,1},{6,2},{7,3},{8,12},{9,13},{10,... | collective-permute-start | bytes 1572872 | tf_op jit(solution)/shard_map/ppermute | solution.py:14
  249.6 5.5 %collective-permute-done.9 = f32[128,1024]{0,1:T(8,128)} collective-permute-done((f32[128,1024]{0,1:T(8,128)}, f32[128,1024]{0,1:T(8,128)}, u32[]{:S(2)}, u32[]{:S(2)}) %collective-permute-start.9) | collective-permute-done | bytes 524320 | tf_op jit(solution)/shard_map/ppermute | solution.py:14
  259.5 5.5 %collective-permute-done.13 = f32[128,1024]{0,1:T(8,128)} collective-permute-done((f32[128,1024]{0,1:T(8,128)}, f32[128,1024]{0,1:T(8,128)}, u32[]{:S(2)}, u32[]{:S(2)}) %collective-permute-start.13) | collective-permute-done | bytes 524320 | tf_op jit(solution)/shard_map/ppermute | solution.py:14
  273.4 7.9 %collective-permute-done.14 = f32[128,1024]{0,1:T(8,128)S(1)} collective-permute-done((f32[128,1024]{0,1:T(8,128)}, f32[128,1024]{0,1:T(8,128)S(1)}, u32[]{:S(2)}, u32[]{:S(2)}) %collective-permute-start.14) | collective-permute-done | bytes 524320 | tf_op jit(solution)/shard_map/ppermute | solution.py:14
  282.7 2.2 select_n.218
  284.9 2.0 copy.1113
  286.9 2.0 bitcast_add_fusion.2
  293.5 1.7 reshape.912
  296.9 1.7 reshape.915
  298.6 2.3 add_convert_fusion.1
  300.9 2.1 add_convert_fusion
  303.1 161.9 %all-reduce.2.cloned.1.call-done = f32[128,1024]{0,1:T(8,128)} async-done(((f32[128,1024]{0,1:T(8,128)}), f32[128,1024]{0,1:T(8,128)}) %all-reduce.2.cloned.1.call-update) | async-done | bytes 524304 | tf_op jit(solution)/shard_map/psum | solution.py:217
  465.0 2.0 copy.1117
  (426 shorter events, 117.1 us)
Async XLA Ops:
  7.2 13.1 %copy-start = (bf16[1,256,2048]{2,1,0:T(8,128)(2,1)S(1)}, bf16[1,256,2048]{2,1,0:T(8,128)(2,1)}, u32[]{:S(2)}) copy-start(bf16[1,256,2048]{2,1,0:T(8,128)(2,1)} %param.8) | copy-start | bytes 3145732
  7.2 291.4 %reduce-scatter.2.cloned.1.call-start = ((), (), s32[]{:S(2)}) async-start(), calls=%async_computation.1 | async-start | bytes 8912896 | tf_op jit(solution)/shard_map/reduce_scatter | solution.py:211
  10.7 20.2 %collective-permute-start = (bf16[128,1024]{1,0:T(8,128)(2,1)}, bf16[128,1024]{1,0:T(8,128)(2,1)}, u32[]{:S(2)}, u32[]{:S(2)}) collective-permute-start(bf16[128,1024]{1,0:T(8,128)(2,1)} %fusion.95), channel_id=1, source_target_pairs={{0,1},{1,0},{2,3},{3,2},{4,5},{5,4},{6,7},{7,6},{8,9},{9,8},{10,11... | collective-permute-start | bytes 786440 | tf_op jit(solution)/shard_map/ppermute | solution.py:14
  13.1 17.8 %collective-permute-start.4 = (bf16[128,1024]{1,0:T(8,128)(2,1)}, bf16[128,1024]{1,0:T(8,128)(2,1)}, u32[]{:S(2)}, u32[]{:S(2)}) collective-permute-start(bf16[128,1024]{1,0:T(8,128)(2,1)} %fusion.99), channel_id=1, source_target_pairs={{0,1},{1,0},{2,3},{3,2},{4,5},{5,4},{6,7},{7,6},{8,9},{9,8},{10,11... | collective-permute-start | bytes 786440 | tf_op jit(solution)/shard_map/ppermute | solution.py:14
  15.4 4.1 copy-start.24
  19.5 4.1 copy-start.26
  19.7 3.8 copy-start.31
  19.8 3.7 copy-start.33
  23.5 4.3 copy-start.29
  25.5 22.8 %copy-start.19 = (bf16[128,1,1024]{0,2,1:T(8,128)(2,1)}, bf16[128,1,1024]{0,2,1:T(8,128)(2,1)S(1)}, u32[]{:S(2)}) copy-start(bf16[128,1,1024]{0,2,1:T(8,128)(2,1)S(1)} %copy.972) | copy-start | bytes 786436
  40.0 15.1 %collective-permute-start.1 = (bf16[128,1024]{1,0:T(8,128)(2,1)}, bf16[128,1024]{1,0:T(8,128)(2,1)}, u32[]{:S(2)}, u32[]{:S(2)}) collective-permute-start(bf16[128,1024]{1,0:T(8,128)(2,1)} %fusion.96), channel_id=1, source_target_pairs={{0,2},{1,3},{2,0},{3,1},{4,6},{5,7},{6,4},{7,5},{8,10},{9,11},{10,... | collective-permute-start | bytes 786440 | tf_op jit(solution)/shard_map/ppermute | solution.py:14
  48.7 6.4 %copy-start.53 = (f32[8,128]{0,1:T(8,128)}, f32[8,128]{0,1:T(8,128)S(1)}, u32[]{:S(2)}) copy-start(f32[8,128]{0,1:T(8,128)S(1)} %copy.978) | copy-start | bytes 12292
  52.3 10.2 %collective-permute-start.5 = (bf16[128,1024]{1,0:T(8,128)(2,1)S(1)}, bf16[128,1024]{1,0:T(8,128)(2,1)}, u32[]{:S(2)}, u32[]{:S(2)}) collective-permute-start(bf16[128,1024]{1,0:T(8,128)(2,1)S(1)} %fusion.100), channel_id=1, source_target_pairs={{0,2},{1,3},{2,0},{3,1},{4,6},{5,7},{6,4},{7,5},{8,10},{9,11},{10,... | collective-permute-start | bytes 786440 | tf_op jit(solution)/shard_map/ppermute | solution.py:14
  61.0 17.9 %collective-permute-start.2 = (bf16[128,1024]{1,0:T(8,128)(2,1)}, bf16[128,1024]{1,0:T(8,128)(2,1)}, u32[]{:S(2)}, u32[]{:S(2)}) collective-permute-start(bf16[128,1024]{1,0:T(8,128)(2,1)} %fusion.97), channel_id=1, source_target_pairs={{0,4},{1,5},{2,6},{3,7},{4,0},{5,1},{6,2},{7,3},{8,12},{9,13},{10,... | collective-permute-start | bytes 786440 | tf_op jit(solution)/shard_map/ppermute | solution.py:14
  68.4 6.8 %copy-start.36 = (f32[128,1,1024]{2,1,0:T(1,128)S(1)}, f32[128,1,1024]{2,1,0:T(1,128)}, u32[]{:S(2)}) copy-start(f32[128,1,1024]{2,1,0:T(1,128)} %get-tuple-element.56) | copy-start | bytes 1572868
  68.4 6.8 %copy-start.37 = (f32[128,1,1024]{2,1,0:T(1,128)S(1)}, f32[128,1,1024]{2,1,0:T(1,128)}, u32[]{:S(2)}) copy-start(f32[128,1,1024]{2,1,0:T(1,128)} %get-tuple-element.57) | copy-start | bytes 1572868
  76.1 12.5 %collective-permute-start.6 = (bf16[128,1024]{1,0:T(8,128)(2,1)}, bf16[128,1024]{1,0:T(8,128)(2,1)S(1)}, u32[]{:S(2)}, u32[]{:S(2)}) collective-permute-start(bf16[128,1024]{1,0:T(8,128)(2,1)} %fusion.101), channel_id=1, source_target_pairs={{0,4},{1,5},{2,6},{3,7},{4,0},{5,1},{6,2},{7,3},{8,12},{9,13},{10,... | collective-permute-start | bytes 786440 | tf_op jit(solution)/shard_map/ppermute | solution.py:14
  84.9 18.1 %collective-permute-start.3 = (bf16[128,1024]{1,0:T(8,128)(2,1)}, bf16[128,1024]{1,0:T(8,128)(2,1)}, u32[]{:S(2)}, u32[]{:S(2)}) collective-permute-start(bf16[128,1024]{1,0:T(8,128)(2,1)} %fusion.98), channel_id=1, source_target_pairs={{0,8},{1,9},{2,10},{3,11},{4,12},{5,13},{6,14},{7,15},{8,0},{9,1},... | collective-permute-start | bytes 786440 | tf_op jit(solution)/shard_map/ppermute | solution.py:14
  88.5 5.9 %copy-start.50 = (bf16[128,1024]{1,0:T(8,128)(2,1)}, bf16[128,1024]{1,0:T(8,128)(2,1)S(1)}, u32[]{:S(2)}) copy-start(bf16[128,1024]{1,0:T(8,128)(2,1)S(1)} %collective-permute-done.6) | copy-start | bytes 786436
  94.4 9.7 %copy-start.66 = (bf16[16,1024]{1,0:T(8,128)(2,1)S(1)}, bf16[16,1024]{1,0:T(8,128)(2,1)}, u32[]{:S(2)}) copy-start(bf16[16,1024]{1,0:T(8,128)(2,1)} %convert_reduce_fusion.4) | copy-start | bytes 98308
  95.6 13.2 %copy-start.13 = (bf16[128,1024]{0,1:T(8,128)(2,1)}, bf16[128,1024]{0,1:T(8,128)(2,1)S(1)}, u32[]{:S(2)}) copy-start(bf16[128,1024]{0,1:T(8,128)(2,1)S(1)} %copy.989) | copy-start | bytes 786436
  95.6 6.5 %copy-start.51 = (bf16[128,1024]{1,0:T(8,128)(2,1)S(1)}, bf16[128,1024]{1,0:T(8,128)(2,1)}, u32[]{:S(2)}) copy-start(bf16[128,1024]{1,0:T(8,128)(2,1)} %copy-done.50) | copy-start | bytes 786436
  99.0 12.7 %copy-start.59 = (f32[8,32,8]{2,1,0:T(8,128)S(1)}, f32[8,32,8]{2,1,0:T(8,128)}, u32[]{:S(2)}) copy-start(f32[8,32,8]{2,1,0:T(8,128)} %reshape.882) | copy-start | bytes 24580
  99.0 12.7 %copy-start.60 = (f32[8,32,8]{2,1,0:T(8,128)S(1)}, f32[8,32,8]{2,1,0:T(8,128)}, u32[]{:S(2)}) copy-start(f32[8,32,8]{2,1,0:T(8,128)} %copy.1014) | copy-start | bytes 24580
  101.8 13.3 %copy-start.42 = (f32[8,2,128]{0,2,1:T(8,128)S(1)}, f32[8,2,128]{0,2,1:T(8,128)}, u32[]{:S(2)}) copy-start(f32[8,2,128]{0,2,1:T(8,128)} %copy.1000) | copy-start | bytes 24580
  101.8 13.3 %copy-start.63 = (f32[8,64]{0,1:T(8,128)S(1)}, f32[8,64]{0,1:T(8,128)}, u32[]{:S(2)}) copy-start(f32[8,64]{0,1:T(8,128)} %copy.985) | copy-start | bytes 6148
  101.8 29.2 %collective-permute-start.7 = (bf16[128,1024]{1,0:T(8,128)(2,1)}, bf16[128,1024]{1,0:T(8,128)(2,1)}, u32[]{:S(2)}, u32[]{:S(2)}) collective-permute-start(bf16[128,1024]{1,0:T(8,128)(2,1)} %fusion.102), channel_id=1, source_target_pairs={{0,8},{1,9},{2,10},{3,11},{4,12},{5,13},{6,14},{7,15},{8,0},{9,1},... | collective-permute-start | bytes 786440 | tf_op jit(solution)/shard_map/ppermute | solution.py:14
  102.9 12.3 %copy-start.47 = (f32[8,64,128]{2,1,0:T(8,128)S(1)}, f32[8,64,128]{2,1,0:T(8,128)}, u32[]{:S(2)}) copy-start(f32[8,64,128]{2,1,0:T(8,128)} %get-tuple-element.79) | copy-start | bytes 786436
  104.1 12.6 %copy-start.17 = (bf16[128,1024]{0,1:T(8,128)(2,1)}, bf16[128,1024]{0,1:T(8,128)(2,1)S(1)}, u32[]{:S(2)}) copy-start(bf16[128,1024]{0,1:T(8,128)(2,1)S(1)} %copy.995) | copy-start | bytes 786436
  110.3 5.0 %copy-start.70 = (f32[8,16,16]{2,1,0:T(8,128)}, f32[8,16,16]{2,1,0:T(8,128)S(1)}, u32[]{:S(2)}) copy-start(f32[8,16,16]{2,1,0:T(8,128)S(1)} %multiply_reduce_fusion.1) | copy-start | bytes 24580
  114.3 8.1 %copy-start.57 = (f32[8,32,8]{2,1,0:T(8,128)}, f32[8,32,8]{2,1,0:T(8,128)S(1)}, u32[]{:S(2)}) copy-start(f32[8,32,8]{2,1,0:T(8,128)S(1)} %multiply_reduce_fusion.2) | copy-start | bytes 24580
  115.9 6.5 %copy-start.38 = (bf16[2,128,8,128]{3,1,2,0:T(8,128)(2,1)S(1)}, bf16[2,128,8,128]{3,1,2,0:T(8,128)(2,1)}, u32[]{:S(2)}) copy-start(bf16[2,128,8,128]{3,1,2,0:T(8,128)(2,1)} %copy.1024) | copy-start | bytes 1572868
  119.4 4.8 %copy-start.40 = (f32[8,128,2]{0,2,1:T(2,128)}, f32[8,128,2]{0,2,1:T(2,128)S(1)}, u32[]{:S(2)}) copy-start(f32[8,128,2]{0,2,1:T(2,128)S(1)} %copy.1005) | copy-start | bytes 24580
  120.4 3.8 copy-start.74
  125.0 3.6 copy-start.49
  142.7 322.3 %all-reduce.2.cloned.1.call-start = ((), (), s32[]{:S(2)}) async-start(), calls=%async_computation.2 | async-start | bytes 1048576 | tf_op jit(solution)/shard_map/psum | solution.py:217
  144.1 3.1 copy-start.55
  148.8 5.0 %copy-start.80 = (f32[256,8]{0,1:T(8,128)S(1)}, f32[256,8]{0,1:T(8,128)}, u32[]{:S(2)}) copy-start(f32[256,8]{0,1:T(8,128)} %get-tuple-element.86) | copy-start | bytes 24580
  151.4 2.9 copy-start.18
  151.4 3.7 copy-start.61
  155.0 3.4 copy-start.14
  155.0 4.8 %copy-start.46 = (bf16[128,1024]{0,1:T(8,128)(2,1)S(1)}, bf16[128,1024]{0,1:T(8,128)(2,1)}, u32[]{:S(2)}) copy-start(bf16[128,1024]{0,1:T(8,128)(2,1)} %copy.1038) | copy-start | bytes 786436
  155.0 4.8 %copy-start.81 = (f32[256,8]{0,1:T(8,128)S(1)}, f32[256,8]{0,1:T(8,128)}, u32[]{:S(2)}) copy-start(f32[256,8]{0,1:T(8,128)} %get-tuple-element.86) | copy-start | bytes 24580
  159.8 5.0 %copy-start.16 = (bf16[128,1024]{0,1:T(8,128)(2,1)S(1)}, bf16[128,1024]{0,1:T(8,128)(2,1)}, u32[]{:S(2)}) copy-start(bf16[128,1024]{0,1:T(8,128)(2,1)} %copy-done.15) | copy-start | bytes 786436
  165.1 3.7 copy-start.44
  168.7 5.6 %copy-start.22 = (bf16[128,1024]{0,1:T(8,128)(2,1)S(1)}, bf16[128,1024]{0,1:T(8,128)(2,1)}, u32[]{:S(2)}) copy-start(bf16[128,1024]{0,1:T(8,128)(2,1)} %copy-done.21) | copy-start | bytes 786436
  188.6 4.0 copy-start.65
  188.6 4.0 copy-start.67
  190.2 7.1 %copy-start.52 = (bf16[32,1024]{1,0:T(8,128)(2,1)S(1)}, bf16[32,1024]{1,0:T(8,128)(2,1)}, u32[]{:S(2)}) copy-start(bf16[32,1024]{1,0:T(8,128)(2,1)} %get-tuple-element.42) | copy-start | bytes 196612
  190.2 7.1 %copy-start.69 = (bf16[8,32,128]{2,1,0:T(8,128)(2,1)S(1)}, bf16[8,32,128]{2,1,0:T(8,128)(2,1)}, u32[]{:S(2)}) copy-start(bf16[8,32,128]{2,1,0:T(8,128)(2,1)} %copy-done.68) | copy-start | bytes 196612
  192.6 6.0 %copy-start.39 = (bf16[64,1024]{1,0:T(8,128)(2,1)S(1)}, bf16[64,1024]{1,0:T(8,128)(2,1)}, u32[]{:S(2)}) copy-start(bf16[64,1024]{1,0:T(8,128)(2,1)} %get-tuple-element.40) | copy-start | bytes 393220
  192.9 7.0 %copy-start.20 = (bf16[128,1,1024]{0,2,1:T(8,128)(2,1)S(1)}, bf16[128,1,1024]{0,2,1:T(8,128)(2,1)}, u32[]{:S(2)}) copy-start(bf16[128,1,1024]{0,2,1:T(8,128)(2,1)} %copy-done.19) | copy-start | bytes 786436
  193.9 19.2 %collective-permute-start.8 = (f32[128,1024]{0,1:T(8,128)}, f32[128,1024]{0,1:T(8,128)}, u32[]{:S(2)}, u32[]{:S(2)}) collective-permute-start(f32[128,1024]{0,1:T(8,128)} %bitcast.460), channel_id=1, source_target_pairs={{0,8},{1,9},{2,10},{3,11},{4,12},{5,13},{6,14},{7,15},{8,0},{9,1},... | collective-permute-start | bytes 1572872 | tf_op jit(solution)/shard_map/ppermute | solution.py:14
  204.3 3.9 copy-start.8
  207.8 20.0 %collective-permute-start.12 = (f32[128,1024]{0,1:T(8,128)}, f32[128,1024]{0,1:T(8,128)}, u32[]{:S(2)}, u32[]{:S(2)}) collective-permute-start(f32[128,1024]{0,1:T(8,128)} %bitcast.109), channel_id=1, source_target_pairs={{0,8},{1,9},{2,10},{3,11},{4,12},{5,13},{6,14},{7,15},{8,0},{9,1},... | collective-permute-start | bytes 1572872 | tf_op jit(solution)/shard_map/ppermute | solution.py:14
  216.3 38.9 %collective-permute-start.9 = (f32[128,1024]{0,1:T(8,128)}, f32[128,1024]{0,1:T(8,128)}, u32[]{:S(2)}, u32[]{:S(2)}) collective-permute-start(f32[128,1024]{0,1:T(8,128)} %bitcast_add_fusion.3), channel_id=1, source_target_pairs={{0,4},{1,5},{2,6},{3,7},{4,0},{5,1},{6,2},{7,3},{8,12},{9,13},{10,... | collective-permute-start | bytes 1572872 | tf_op jit(solution)/shard_map/ppermute | solution.py:14
  230.9 34.2 %collective-permute-start.13 = (f32[128,1024]{0,1:T(8,128)}, f32[128,1024]{0,1:T(8,128)}, u32[]{:S(2)}, u32[]{:S(2)}) collective-permute-start(f32[128,1024]{0,1:T(8,128)} %bitcast_add_fusion), channel_id=1, source_target_pairs={{0,4},{1,5},{2,6},{3,7},{4,0},{5,1},{6,2},{7,3},{8,12},{9,13},{10,... | collective-permute-start | bytes 1572872 | tf_op jit(solution)/shard_map/ppermute | solution.py:14
  258.4 11.9 %collective-permute-start.10 = (f32[128,1024]{0,1:T(8,128)}, f32[128,1024]{0,1:T(8,128)}, u32[]{:S(2)}, u32[]{:S(2)}) collective-permute-start(f32[128,1024]{0,1:T(8,128)} %bitcast_add_fusion.4), channel_id=1, source_target_pairs={{0,2},{1,3},{2,0},{3,1},{4,6},{5,7},{6,4},{7,5},{8,10},{9,11},{10,... | collective-permute-start | bytes 1572872 | tf_op jit(solution)/shard_map/ppermute | solution.py:14
  268.2 13.0 %collective-permute-start.14 = (f32[128,1024]{0,1:T(8,128)}, f32[128,1024]{0,1:T(8,128)S(1)}, u32[]{:S(2)}, u32[]{:S(2)}) collective-permute-start(f32[128,1024]{0,1:T(8,128)} %bitcast_add_fusion.1), channel_id=1, source_target_pairs={{0,2},{1,3},{2,0},{3,1},{4,6},{5,7},{6,4},{7,5},{8,10},{9,11},{10,... | collective-permute-start | bytes 1572872 | tf_op jit(solution)/shard_map/ppermute | solution.py:14
  273.4 18.4 %collective-permute-start.11 = (f32[128,1024]{0,1:T(8,128)}, f32[128,1024]{0,1:T(8,128)}, u32[]{:S(2)}, u32[]{:S(2)}) collective-permute-start(f32[128,1024]{0,1:T(8,128)} %bitcast_add_fusion.5), channel_id=1, source_target_pairs={{0,1},{1,0},{2,3},{3,2},{4,5},{5,4},{6,7},{7,6},{8,9},{9,8},{10,11... | collective-permute-start | bytes 1572872 | tf_op jit(solution)/shard_map/ppermute | solution.py:14
  281.7 7.3 %copy-start.9 = (f32[1,256,1024]{2,1,0:T(8,128)S(1)}, f32[1,256,1024]{2,1,0:T(8,128)}, u32[]{:S(2)}) copy-start(f32[1,256,1024]{2,1,0:T(8,128)} %reshape.898) | copy-start | bytes 3145732
  281.7 7.3 %copy-start.11 = (f32[1,256,1024]{2,1,0:T(8,128)S(1)}, f32[1,256,1024]{2,1,0:T(8,128)}, u32[]{:S(2)}) copy-start(f32[1,256,1024]{2,1,0:T(8,128)} %reshape.909) | copy-start | bytes 3145732
  289.0 6.2 %collective-permute-start.15 = (f32[128,1024]{0,1:T(8,128)}, f32[128,1024]{0,1:T(8,128)}, u32[]{:S(2)}, u32[]{:S(2)}) collective-permute-start(f32[128,1024]{0,1:T(8,128)} %bitcast_add_fusion.2), channel_id=1, source_target_pairs={{0,1},{1,0},{2,3},{3,2},{4,5},{5,4},{6,7},{7,6},{8,9},{9,8},{10,11... | collective-permute-start | bytes 1572872 | tf_op jit(solution)/shard_map/ppermute | solution.py:14
  298.6 168.4 %copy-start.1 = (bf16[1,256,2048]{2,1,0:T(8,128)(2,1)S(1)}, bf16[1,256,2048]{2,1,0:T(8,128)(2,1)}, u32[]{:S(2)}) copy-start(bf16[1,256,2048]{2,1,0:T(8,128)(2,1)} %param.8) | copy-start | bytes 3145732
  (46 other events, 84.2 us)
Sparse Core Ops, SparseCore 0:
  142.8 99.1 reduce-scatter.1
  298.7 166.1 all-reduce.1
where the time goes:
time: 482 us; the launch traced here: 474 us
  waiting for transfers between devices  182 us (38%)
  local copies, waits for them, and re-layouts  122 us (25%)
  other arithmetic  65.6 us (14%)
  matrix products  46.5 us (10%)
  starting transfers between devices  41.5 us (9%)
  between operations  16.5 us (3%)
    psum x1, waiting for transfers between devices, per_device(): d_weight = lax.psum(shares, 'dp')  162 us
    ppermute x16, starting transfers between devices, from_partner(): return lax.ppermute(value, axis, pairs)  41.2 us
    ppermute x16, waiting for transfers between devices, from_partner(): return lax.ppermute(value, axis, pairs)  20 us
    convert_element_type x12, local copies, waits for them, and re-layouts, coarsen(): matrix.astype(jnp.float32).reshape(matrix.shape[0] // 2, 2, matrix.shape[1])  15.5 us
    slice x9, local copies, waits for them, and re-layouts, coarsen(): return ((paired_rows[:, 0] + paired_rows[:, 1]) * 0.5).astype(jnp.bfloat16)  13.5 us
    convert_element_type x7, other arithmetic, coarsen(): matrix.astype(jnp.float32).reshape(matrix.shape[0] // 2, 2, matrix.shape[1])  13.3 us
    broadcast_in_dim x24, local copies, waits for them, and re-layouts, per_device(): jnp.repeat(jnp.max(raw_scores, axis=3), 2 ** height, axis=2)  12.4 us
    convert_element_type x12, other arithmetic, coarsen(): return ((paired_rows[:, 0] + paired_rows[:, 1]) * 0.5).astype(jnp.bfloat16)  12.3 us
  transfers between devices with their start and end apart: 18, of which 5 were waited for; matrix products, arithmetic and copies ran while one was open for 43% of the time, Pallas kernels for 0%

commit v1 on v0

v1 whole, which is shorter than its diff:
```python
import functools

import jax
import jax.numpy as jnp
from jax import lax
from jax.experimental import pallas as pl
from jax.experimental.pallas import tpu as pltpu
from jax.sharding import PartitionSpec as P

HEADS = 8
HDIM = 128
ROWS = 256
WIDTH = 1024
DMODEL = 2048
SCALE = HDIM**-0.5
LEVEL_ROWS = (128, 64, 32, 16)
LEVEL_AT = (0, 128, 192, 224)
COARSE = 240
BF = jnp.bfloat16
F32 = jnp.float32
VMEM = pltpu.CompilerParams(vmem_limit_bytes=48 * 1024 * 1024)

CORE, ZLO, Y1, Y2, Y3 = 1, 2, 4, 8, 12
X1, X2, X3, ZH1, ZH3 = 1, 2, 3, 4, 12


def swap(value, axis, mask):
    pairs = [(source, source ^ mask) for source in range(16)]
    return lax.ppermute(value, axis, pairs)


def dot(a, b):
    return jnp.dot(a, b, preferred_element_type=F32)


def dot_nt(a, b):
    return lax.dot_general(a, b, (((1,), (1,)), ((), ())), preferred_element_type=F32)


def dot_tn(a, b):
    return lax.dot_general(a, b, (((0,), (0,)), ((), ())), preferred_element_type=F32)


def pool_matrix(rows):
    r = lax.broadcasted_iota(jnp.int32, (rows, 2 * rows), 0)
    c = lax.broadcasted_iota(jnp.int32, (rows, 2 * rows), 1)
    return jnp.where((c == 2 * r) | (c == 2 * r + 1), 0.5, 0.0).astype(BF)


def coarse_levels(x):
    levels = []
    for rows in LEVEL_ROWS:
        x = dot(pool_matrix(rows), x).astype(BF)
        levels.append(x)
    return levels


def rep2(buf, x):
    rows, cols = x.shape
    buf[pl.ds(0, rows, stride=2), 0:cols] = x
    buf[pl.ds(1, rows, stride=2), 0:cols] = x
    return buf[0 : 2 * rows, 0:cols]


def pairsum(buf, x):
    rows, cols = x.shape
    buf[0:rows, 0:cols] = x
    half = rows // 2
    return buf[pl.ds(0, half, stride=2), 0:cols] + buf[pl.ds(1, half, stride=2), 0:cols]


def wide(column):
    return jnp.broadcast_to(column, (column.shape[0], HDIM))


def coarsen_kernel(k_ref, v_ref, o1, o2, o3, o4):
    ks = coarse_levels(k_ref[...])
    vs = coarse_levels(v_ref[...])
    for out, rows, k, v in zip((o1, o2, o3, o4), LEVEL_ROWS, ks, vs):
        out[0:rows, :] = k
        out[rows : 2 * rows, :] = v


def arrange_kernel(at_ref, dout_ref, own_ref, other_ref):
    y, zl, c = at_ref[0], at_ref[1], at_ref[2]
    for n in range(8):
        jy, iz = n // 2, n % 2
        base = (y ^ jy) * 4 + (zl ^ iz) * 2
        for ref, core in ((own_ref, c), (other_ref, 1 - c)):
            at = pl.multiple_of((base + core) * 128, 128)
            block = dout_ref[:, pl.ds(at, 128)]
            ref[n * 128 : (n + 1) * 128, :] = block.T


def local_kernel(q_ref, k_ref, v_ref, dout_ref, w_ref, datt_ref, qc_ref, n_ref, m_ref, l_ref):
    datt_ref[...] = dot(dout_ref[...], w_ref[...]).astype(BF)
    q = q_ref[...]
    for x, at, rows in zip(coarse_levels(q), LEVEL_AT, LEVEL_ROWS):
        qc_ref[at : at + rows, :] = x
    for h in range(q.shape[1] // HDIM):
        cols = slice(h * HDIM, (h + 1) * HDIM)
        s = dot_nt(q_ref[:, cols], k_ref[:, cols]) * SCALE
        m = jnp.max(s, axis=1, keepdims=True)
        e = jnp.exp(s - m)
        l_ref[:, cols] = wide(jnp.sum(e, axis=1, keepdims=True))
        m_ref[:, cols] = wide(m)
        n_ref[:, cols] = dot(e.astype(BF), v_ref[:, cols])


def sibling(level, a_ref, u_ref, e_ref, cols):
    if level == 1:
        return a_ref[0:128, cols], a_ref[128:256, cols]
    spans = {
        2: ((0, 64),),
        3: ((128, 32), (256, 32)),
        4: ((192, 16), (224, 16), (320, 16), (352, 16)),
    }[level]
    keys = [ref[at : at + n, cols] for ref in (u_ref, e_ref) for at, n in spans]
    vals = [ref[at + n : at + 2 * n, cols] for ref in (u_ref, e_ref) for at, n in spans]
    return jnp.concatenate(keys, axis=0), jnp.concatenate(vals, axis=0)


def forward_kernel(
    qc_ref, a_ref, u_ref, e_ref, n_ref, m_ref, l_ref,
    att_ref, lse_ref, w_ref, f_ref, c_ref, bufs,
):
    for h in range(qc_ref.shape[1] // HDIM):
        cols = slice(h * HDIM, (h + 1) * HDIM)
        per = []
        for level in range(1, 5):
            at, rows = LEVEL_AT[level - 1], LEVEL_ROWS[level - 1]
            keys, vals = sibling(level, a_ref, u_ref, e_ref, cols)
            s = dot_nt(qc_ref[at : at + rows, cols], keys) * SCALE
            m = jnp.max(s, axis=1, keepdims=True)
            e = jnp.exp(s - m)
            w_ref[at : at + rows, cols] = e
            per.append((wide(m), wide(jnp.sum(e, axis=1, keepdims=True)), dot(e.astype(BF), vals)))
        top, total, num = per[3]
        total, num = total * 16.0, num * 16.0
        for level in (3, 2, 1):
            at, rows = LEVEL_AT[level - 1], LEVEL_ROWS[level - 1]
            m, lsum, n = per[level - 1]
            up_m = rep2(bufs.at[3 * h], top)
            up_l = rep2(bufs.at[3 * h + 1], total)
            up_n = rep2(bufs.at[3 * h + 2], num)
            top = jnp.maximum(m, up_m)
            own = jnp.exp(m - top) * 2.0**level
            far = jnp.exp(up_m - top)
            total = own * lsum + far * up_l
            num = own * n + far * up_n
            c_ref[at : at + rows, cols] = own
            f_ref[256 + at : 256 + at + rows, cols] = far
        up_m = rep2(bufs.at[3 * h], top)
        up_l = rep2(bufs.at[3 * h + 1], total)
        up_n = rep2(bufs.at[3 * h + 2], num)
        m = m_ref[:, cols]
        top = jnp.maximum(m, up_m)
        own = jnp.exp(m - top)
        far = jnp.exp(up_m - top)
        total = own * l_ref[:, cols] + far * up_l
        inv = 1.0 / total
        att_ref[:, cols] = ((own * n_ref[:, cols] + far * up_n) * inv).astype(BF)
        f_ref[0:256, cols] = far * inv
        lse_ref[:, cols] = top + jnp.log(total)


def coarse_back_kernel(
    qc_ref, a_ref, u_ref, e_ref, datt_ref, att_ref, w_ref, f_ref, c_ref,
    send_ref, keep_ref, gq_ref, bufs,
):
    spans = {
        2: ((0, 64),),
        3: ((128, 32), (256, 32)),
        4: ((192, 16), (224, 16), (320, 16), (352, 16)),
    }
    for h in range(qc_ref.shape[1] // HDIM):
        cols = slice(h * HDIM, (h + 1) * HDIM)
        datt = datt_ref[:, cols].astype(F32)
        delta = wide(jnp.sum(datt * att_ref[:, cols].astype(F32), axis=1, keepdims=True))
        far = f_ref[0:256, cols]
        d, dl = far * datt, far * delta
        gqs = []
        for level in range(1, 5):
            at, rows = LEVEL_AT[level - 1], LEVEL_ROWS[level - 1]
            d = pairsum(bufs.at[2 * h], d)
            dl = pairsum(bufs.at[2 * h + 1], dl)
            keys, vals = sibling(level, a_ref, u_ref, e_ref, cols)
            if level < 4:
                own = c_ref[at : at + rows, cols]
                da, dd = (own * d).astype(BF), own * dl
                far = f_ref[256 + at : 256 + at + rows, cols]
                d, dl = far * d, far * dl
            else:
                da, dd = (16.0 * d).astype(BF), 16.0 * dl
            w = w_ref[at : at + rows, cols]
            ds = (w * (dot_nt(da, vals) - dd)).astype(BF)
            gqs.append(dot(ds, keys) * SCALE)
            gk = dot_tn(ds, qc_ref[at : at + rows, cols]) * SCALE
            gv = dot_tn(w.astype(BF), da)
            if level == 1:
                send_ref[0:128, cols] = gk.astype(BF)
                send_ref[128:256, cols] = gv.astype(BF)
            else:
                row = 0
                for ref, off in ((keep_ref, 0), (send_ref, 256)):
                    for start, n in spans[level]:
                        to = off + start
                        ref[to : to + n, cols] = gk[row : row + n].astype(ref.dtype)
                        ref[to + n : to + 2 * n, cols] = gv[row : row + n].astype(ref.dtype)
                        row += n
        g = gqs[3]
        for level in (3, 2, 1):
            g = gqs[level - 1] + rep2(bufs.at[2 * h], 0.5 * g)
        gq_ref[:, cols] = rep2(bufs.at[2 * h], 0.5 * g)


def weight_kernel(at_ref, own_ref, other_ref, att_ref, attp_ref, *outs):
    x = at_ref[3]

    def heads(ref, half):
        blocks = []
        for jx in range(4):
            col = pl.multiple_of(((x ^ jx) * 2 + half) * 128, 128)
            blocks.append(ref[:, pl.ds(col, 128)])
        return jnp.concatenate(blocks, axis=1)

    mine, theirs = heads(att_ref, 0), heads(attp_ref, 0)
    for j in range(4):
        rows = slice(j * 256, (j + 1) * 256)
        outs[j][...] = (dot(own_ref[rows, :], mine) + dot(other_ref[rows, :], theirs)).astype(BF)
    mine, theirs = heads(att_ref, 1), heads(attp_ref, 1)
    for j in range(4):
        rows = slice(j * 256, (j + 1) * 256)
        part = (dot(own_ref[rows, :], mine) + dot(other_ref[rows, :], theirs)).astype(BF)
        for jx in range(4):
            outs[4 + jx][rows, :] = part[:, jx * 128 : (jx + 1) * 128]


def sum_first_kernel(*refs):
    ins, outs = refs[:8], refs[8:]
    for j in range(4):
        cols = slice(j * 128, (j + 1) * 128)
        outs[j][...] = sum(r[:, cols].astype(F32) for r in ins[:4]).astype(BF)
    for j in range(4):
        rows = slice(j * 256, (j + 1) * 256)
        outs[4 + j][...] = sum(r[rows, :].astype(F32) for r in ins[4:]).astype(BF)


def sum_second_kernel(*refs):
    ins, (keep_ref, send_ref) = refs[:8], refs[8:]
    for half in range(2):
        cols = slice(half * 128, (half + 1) * 128)
        total = sum(r[...].astype(F32) for r in ins[4 * half : 4 * half + 4])
        keep_ref[:, cols] = total[0:128].astype(BF)
        send_ref[:, cols] = total[128:256].astype(BF)


def place_kernel(at_ref, a, b, c, d, out_ref):
    x = at_ref[3]
    for j, ref in enumerate((a, b, c, d)):
        col = pl.multiple_of((x ^ j) * 256, 256)
        out_ref[:, pl.ds(col, 256)] = ref[...].astype(F32)


def local_back_kernel(
    q_ref, k_ref, v_ref, datt_ref, att_ref, lse_ref, gqc_ref, dq_ref, gk_ref, gv_ref
):
    for h in range(q_ref.shape[1] // HDIM):
        cols = slice(h * HDIM, (h + 1) * HDIM)
        q, k, v, datt = q_ref[:, cols], k_ref[:, cols], v_ref[:, cols], datt_ref[:, cols]
        delta = jnp.sum(datt.astype(F32) * att_ref[:, cols].astype(F32), axis=1, keepdims=True)
        p = jnp.exp(dot_nt(q, k) * SCALE - lse_ref[:, cols][:, 0:1])
        ds = (p * (dot_nt(datt, v) - delta)).astype(BF)
        dq_ref[:, cols] = (dot(ds, k) * SCALE + gqc_ref[:, cols]).astype(BF)
        gk_ref[:, cols] = dot_tn(ds, q) * SCALE
        gv_ref[:, cols] = dot_tn(p.astype(BF), datt)


def finish_kernel(gk_ref, gv_ref, r1, r2, r3, r4, dk_ref, dv_ref, bufs):
    for h in range(gk_ref.shape[1] // HDIM):
        cols = slice(h * HDIM, (h + 1) * HDIM)
        for which, (g0_ref, out_ref) in enumerate(((gk_ref, dk_ref), (gv_ref, dv_ref))):
            g = None
            for ref, rows in ((r4, 16), (r3, 32), (r2, 64), (r1, 128)):
                own = ref[which * rows : (which + 1) * rows, cols].astype(F32)
                g = own if g is None else own + rep2(bufs.at[2 * h + which], 0.5 * g)
            g = g0_ref[:, cols] + rep2(bufs.at[2 * h + which], 0.5 * g)
            out_ref[:, cols] = g.astype(BF)


def shape(rows, cols, dtype=BF):
    return jax.ShapeDtypeStruct((rows, cols), dtype)


SMEM = pl.BlockSpec(memory_space=pltpu.SMEM)


def by_heads(rows, step):
    return pl.BlockSpec((rows, step), lambda i: (0, i))


def whole(rows, cols):
    return pl.BlockSpec((rows, cols), lambda i: (0, 0))


def call(kernel, out, **kw):
    return pl.pallas_call(kernel, out_shape=out, compiler_params=VMEM, **kw)


def per_device(queries, keys, values, d_out, w_out):
    q, k, v, dout = queries[0], keys[0], values[0], d_out[0]
    seq, dp = lax.axis_index("seq"), lax.axis_index("dp")
    place = jnp.stack([seq // 4, seq // 2 % 2, seq % 2, dp % 4]).astype(jnp.int32)
    step = 2 * HDIM
    grid = (WIDTH // step,)
    hs = functools.partial(by_heads, step=step)

    l1, l2, l3, l4 = call(
        coarsen_kernel,
        [shape(2 * rows, WIDTH) for rows in LEVEL_ROWS],
    )(k, v)
    a1 = swap(l1, "seq", CORE)
    b2 = swap(l2, "seq", ZLO)
    b4 = swap(l4, "seq", Y3)
    b3 = swap(l3, "seq", Y1)
    c4 = swap(b4, "seq", Y1)
    t = jnp.concatenate([b3, c4, b4])
    d = swap(t, "seq", ZLO)
    u = jnp.concatenate([b2, t, d])
    e = swap(u, "seq", CORE)

    own_t, other_t = call(
        arrange_kernel,
        [shape(1024, ROWS)] * 2,
        in_specs=[SMEM, pl.BlockSpec(memory_space=pltpu.VMEM)],
    )(place, dout)
    rec_t = swap(other_t, "seq", CORE)

    datt, qc, n0, m0, l0 = call(
        local_kernel,
        [shape(ROWS, WIDTH), shape(COARSE, WIDTH)] + [shape(ROWS, WIDTH, F32)] * 3,
        grid=grid,
        in_specs=[hs(ROWS)] * 3 + [whole(ROWS, DMODEL), hs(DMODEL)],
        out_specs=[hs(ROWS), hs(COARSE)] + [hs(ROWS)] * 3,
    )(q, k, v, dout, w_out)

    att, lse, w, f, c = call(
        forward_kernel,
        [
            shape(ROWS, WIDTH),
            shape(ROWS, WIDTH, F32),
            shape(COARSE, WIDTH, F32),
            shape(480, WIDTH, F32),
            shape(224, WIDTH, F32),
        ],
        grid=grid,
        in_specs=[hs(COARSE), hs(256), hs(384), hs(384)] + [hs(ROWS)] * 3,
        out_specs=[hs(ROWS), hs(ROWS), hs(COARSE), hs(480), hs(224)],
        scratch_shapes=[pltpu.VMEM((6, ROWS, HDIM), F32)],
    )(qc, a1, u, e, n0, m0, l0)

    attp = swap(att, "seq", CORE)

    send, keep, gqc = call(
        coarse_back_kernel,
        [shape(640, WIDTH), shape(384, WIDTH, F32), shape(ROWS, WIDTH, F32)],
        grid=grid,
        in_specs=[hs(COARSE), hs(256), hs(384), hs(384), hs(ROWS), hs(ROWS)]
        + [hs(COARSE), hs(480), hs(224)],
        out_specs=[hs(640), hs(384), hs(ROWS)],
        scratch_shapes=[pltpu.VMEM((4, ROWS, HDIM), F32)],
    )(qc, a1, u, e, datt, att, w, f, c)

    o = call(
        weight_kernel,
        [shape(256, 512)] * 4 + [shape(1024, 128)] * 4,
        in_specs=[SMEM] + [pl.BlockSpec(memory_space=pltpu.VMEM)] * 4,
    )(place, own_t, rec_t, att, attp)
    first = [
        o[0], swap(o[1], "seq", Y1), swap(o[2], "seq", Y2), swap(o[3], "seq", Y3),
        o[4], swap(o[5], "dp", X1), swap(o[6], "dp", X2), swap(o[7], "dp", X3),
    ]

    rc = swap(send, "seq", CORE)
    dq, gk0, gv0 = call(
        local_back_kernel,
        [shape(ROWS, WIDTH), shape(ROWS, WIDTH, F32), shape(ROWS, WIDTH, F32)],
        grid=grid,
        in_specs=[hs(ROWS)] * 7,
        out_specs=[hs(ROWS)] * 3,
    )(q, k, v, datt, att, lse, gqc)
    s = keep + rc[256:640].astype(F32)
    rz = swap(s[256:384].astype(BF), "seq", ZLO)
    r2 = swap(s[0:128].astype(BF), "seq", ZLO)
    t = s[128:256] + rz.astype(F32)
    ry = swap(t[0:96].astype(BF), "seq", Y1)
    r4 = swap((t[96:128] + ry[64:96].astype(F32)).astype(BF), "seq", Y3)
    dk, dv = call(
        finish_kernel,
        [shape(ROWS, WIDTH)] * 2,
        grid=grid,
        in_specs=[hs(ROWS)] * 2 + [hs(256), hs(128), hs(64), hs(32)],
        out_specs=[hs(ROWS)] * 2,
        scratch_shapes=[pltpu.VMEM((4, ROWS, HDIM), F32)],
    )(gk0, gv0, rc[0:256], r2, ry[0:64], r4)

    p = call(sum_first_kernel, [shape(256, 128)] * 8)(*first)
    second = [
        p[0], swap(p[1], "dp", X1), swap(p[2], "dp", X2), swap(p[3], "dp", X3),
        p[4], swap(p[5], "seq", Y1), swap(p[6], "seq", Y2), swap(p[7], "seq", Y3),
    ]
    kept, sent = call(sum_second_kernel, [shape(128, 256)] * 2)(*second)
    g = kept.astype(F32) + swap(sent, "seq", ZLO).astype(F32)
    for mask in (ZH1, ZH3):
        g = g.astype(BF)
        g = g.astype(F32) + swap(g, "dp", mask).astype(F32)
    g = g.astype(BF)
    dw = call(
        place_kernel,
        shape(128, WIDTH, F32),
        in_specs=[SMEM] + [pl.BlockSpec(memory_space=pltpu.VMEM)] * 4,
    )(place, g, swap(g, "dp", X1), swap(g, "dp", X2), swap(g, "dp", X3))
    return dq[None], dk[None], dv[None], dw


def solution(mesh):
    rows = P("dp", "seq", None)
    return jax.shard_map(
        per_device,
        mesh=mesh,
        in_specs=(rows, rows, rows, rows, P()),
        out_specs=(rows, rows, rows, P("seq", None)),
        check_vma=False,
    )
```

time: 482 us -> 137 us (0.28); the launches traced: 474 us -> 135 us
  waiting for transfers between devices: 182 us -> 35.7 us
  local copies, waits for them, and re-layouts: 122 us -> 6.26 us
  other arithmetic: 65.6 us -> 0.52 us
  matrix products: 46.5 us -> 0 us
  Pallas kernels: 0 us -> 43.3 us
  between operations: 16.5 us -> 0.87 us
  starting transfers between devices: 41.5 us -> 48.6 us
    psum x1 -> x0, waiting for transfers between devices: 162 us -> none  [per_device(): d_weight = lax.psum(shares, 'dp')]
    dot_general x32 -> x0, matrix products: 46.5 us -> none  [the longest x5 12.1 us: per_device(): jnp.einsum('gfhd,gjhd->ghfj', dout_group, v_group, preferred_element_type...]
    pallas_call x0 -> x11, Pallas kernels: none -> 43.3 us  [the longest x1 11.3 us: per_device(): call(forward_kernel, [shape(ROWS, WIDTH), shape(ROWS, WIDTH, F32), shape(...]
    convert_element_type x22 -> x4, other arithmetic: 30.9 us -> 0.07 us  [the longest x3 0.06 us: per_device(): g = g.astype(BF)]
    reshape x16 -> x0, local copies, waits for them, and re-layouts: 21.8 us -> none  [the longest x7 10.5 us: spread(): return jnp.repeat(gradient * 0.5, 2, axis=0)]
    broadcast_in_dim x44 -> x0, local copies, waits for them, and re-layouts: 20.3 us -> none  [the longest x24 12.4 us: per_device(): jnp.repeat(jnp.max(raw_scores, axis=3), 2 ** height, axis=2)]
    ppermute x16 -> x32, waiting for transfers between devices: 20 us -> 35.7 us  [swap(): return lax.ppermute(value, axis, pairs)]
    convert_element_type x13 -> x0, local copies, waits for them, and re-layouts: 15.6 us -> none  [the longest x12 15.5 us: coarsen(): matrix.astype(jnp.float32).reshape(matrix.shape[0] // 2, 2, matrix.shape[1])]
  transfers between devices with their start and end apart: 18 -> 32, of which waited for: 5 -> 12; matrix products, arithmetic and copies ran while one was open for 43% -> 0% of each run, Pallas kernels for 0% -> 29%
where the time goes in v1:
time: 137 us; the launch traced here: 135 us
  starting transfers between devices  48.6 us (35%)
  Pallas kernels  43.3 us (32%)
  waiting for transfers between devices  35.7 us (26%)
  local copies, waits for them, and re-layouts  6.26 us (5%)
    ppermute x32, starting transfers between devices, swap(): return lax.ppermute(value, axis, pairs)  48.6 us
    ppermute x32, waiting for transfers between devices, swap(): return lax.ppermute(value, axis, pairs)  35.7 us
    pallas_call x1, Pallas kernels, per_device(): call(forward_kernel, [shape(ROWS, WIDTH), shape(ROWS, WIDTH, F32), shape(...  11.3 us
    pallas_call x1, Pallas kernels, per_device(): call(coarse_back_kernel, [shape(640, WIDTH), shape(384, WIDTH, F32), shap...  10 us
    pallas_call x1, Pallas kernels, per_device(): call(local_kernel, [shape(ROWS, WIDTH), shape(COARSE, WIDTH)] + [shape(RO...  8.37 us
    unnamed x26, local copies, waits for them, and re-layouts  6.14 us
    pallas_call x1, Pallas kernels, per_device(): call(local_back_kernel, [shape(ROWS, WIDTH), shape(ROWS, WIDTH, F32), sha...  5.43 us
  transfers between devices with their start and end apart: 32, of which 12 were waited for; matrix products, arithmetic and copies ran while one was open for 0% of the time, Pallas kernels for 29%

profile of v1, /device:TPU:32, one launch (start us, length us, event | category | flops | bytes accessed | tf_op | source)
XLA Modules:
  0.0 135.2 jit_solution(16986701232440740377)
XLA Ops:
  0.6 0.0 copy-start
  0.6 1.0 copy-done
  1.7 1.0 copy-done.2
  2.7 1.5 %shard_map.85 = (bf16[256,1024]{1,0:T(8,128)(2,1)}, bf16[128,1024]{1,0:T(8,128)(2,1)S(1)}, bf16[64,1024]{1,0:T(8,128)(2,1)S(1)}, bf16[32,1024]{1,0:T(8,128)(2,1)S(1)}) custom-call(bf16[256,1024]{1,0:T(8,128)(2,1)S(1)} %bitcast.11, bf16[256,1024]{1,0:T(8,128)(2,1)S(1)} %bitcast.14), custom_call_target="tpu_custom_call" | custom-call | tf_op jit(solution)/shard_map/pallas_call | solution.py:318
  4.3 1.8 %collective-permute-start.1 = (bf16[128,1024]{1,0:T(8,128)(2,1)S(1)}, bf16[128,1024]{1,0:T(8,128)(2,1)S(1)}, u32[]{:S(2)}, u32[]{:S(2)}) collective-permute-start(bf16[128,1024]{1,0:T(8,128)(2,1)S(1)} %get-tuple-element.49), channel_id=1, source_target_pairs={{0,2},{1,3},{2,0},{3,1},{4,6},{5,7},{6,4},{7,5},{8,10},{9,11},{10,... | collective-permute-start | bytes 786440 | tf_op jit(solution)/shard_map/ppermute | solution.py:29
  6.1 2.0 %collective-permute-start.3 = (bf16[32,1024]{1,0:T(8,128)(2,1)S(1)}, bf16[32,1024]{1,0:T(8,128)(2,1)S(1)}, u32[]{:S(2)}, u32[]{:S(2)}) collective-permute-start(bf16[32,1024]{1,0:T(8,128)(2,1)S(1)} %get-tuple-element.51), channel_id=1, source_target_pairs={{0,12},{1,13},{2,14},{3,15},{4,8},{5,9},{6,10},{7,11},{8,4},{9,5},... | collective-permute-start | bytes 196616 | tf_op jit(solution)/shard_map/ppermute | solution.py:29
  8.1 3.5 %collective-permute-done.3 = bf16[32,1024]{1,0:T(8,128)(2,1)S(1)} collective-permute-done((bf16[32,1024]{1,0:T(8,128)(2,1)S(1)}, bf16[32,1024]{1,0:T(8,128)(2,1)S(1)}, u32[]{:S(2)}, u32[]{:S(2)}) %collective-permute-start.3) | collective-permute-done | bytes 65568 | tf_op jit(solution)/shard_map/ppermute | solution.py:29
  11.6 0.8 collective-permute-start.4
  12.4 3.4 %collective-permute-done.4 = bf16[32,1024]{1,0:T(8,128)(2,1)S(1)} collective-permute-done((bf16[32,1024]{1,0:T(8,128)(2,1)S(1)}, bf16[32,1024]{1,0:T(8,128)(2,1)S(1)}, u32[]{:S(2)}, u32[]{:S(2)}) %collective-permute-start.4) | collective-permute-done | bytes 65568 | tf_op jit(solution)/shard_map/ppermute | solution.py:29
  15.9 1.8 %collective-permute-start.5 = (bf16[128,1024]{1,0:T(8,128)(2,1)S(1)}, bf16[128,1024]{1,0:T(8,128)(2,1)S(1)}, u32[]{:S(2)}, u32[]{:S(2)}) collective-permute-start(bf16[128,1024]{1,0:T(8,128)(2,1)S(1)} %pad_maximum_fusion), channel_id=1, source_target_pairs={{0,2},{1,3},{2,0},{3,1},{4,6},{5,7},{6,4},{7,5},{8,10},{9,11},{10,... | collective-permute-start | bytes 786440 | tf_op jit(solution)/shard_map/ppermute | solution.py:29
  17.8 4.5 %collective-permute-done.5 = bf16[128,1024]{1,0:T(8,128)(2,1)S(1)} collective-permute-done((bf16[128,1024]{1,0:T(8,128)(2,1)S(1)}, bf16[128,1024]{1,0:T(8,128)(2,1)S(1)}, u32[]{:S(2)}, u32[]{:S(2)}) %collective-permute-start.5) | collective-permute-done | bytes 262176 | tf_op jit(solution)/shard_map/ppermute | solution.py:29
  22.4 0.1 collective-permute-start.6
  22.5 0.5 collective-permute-start
  23.0 0.1 pad_add_fusion.at_ref
  23.0 0.9 shard_map.90
  23.9 0.2 collective-permute-start.12
  24.1 1.0 copy-done.5
  25.2 8.4 %shard_map.84 = (bf16[256,1024]{1,0:T(8,128)(2,1)S(1)}, bf16[240,1024]{1,0:T(8,128)(2,1)S(1)}, f32[256,1024]{1,0:T(8,128)S(1)}, f32[256,1024]{1,0:T(8,128)S(1)}, f32[256,1024]{1,0:T(8,128)S(1)}) custom-call(bf16[256,1024]{1,0:T(8,128)(2,1)S(1)} %bitcast.19, bf16[256,1024]{1,0:T(8,128)(2,1)S(1)} %bitcast.12, bf16[256,1024]{1,0:T(8,128)(2,1)S(1)} %bitcast.15, ...), custom_call_target="tpu_custom_call" | custom-call | tf_op jit(solution)/shard_map/pallas_call | solution.py:339
  33.5 1.0 copy-done.7
  34.5 1.0 copy-done.8
  35.5 1.0 copy-done.9
  36.5 11.3 %shard_map.86 = (bf16[256,1024]{1,0:T(8,128)(2,1)S(1)}, f32[256,1024]{1,0:T(8,128)S(1)}, f32[240,1024]{1,0:T(8,128)S(1)}, f32[480,1024]{1,0:T(8,128)}, f32[224,1024]{1,0:T(8,128)S(1)}) custom-call(bf16[240,1024]{1,0:T(8,128)(2,1)S(1)} %get-tuple-element.47.qc_ref, bf16[256,1024]{1,0:T(8,128)(2,1)S(1)} %collective-permute-done.a_ref, ...), custom_call_target="tpu_custom_call" | custom-call | tf_op jit(solution)/shard_map/pallas_call | solution.py:347
  47.8 0.4 collective-permute-start.13
  48.2 10.0 %shard_map.87 = (bf16[640,1024]{1,0:T(8,128)(2,1)}, f32[384,1024]{1,0:T(8,128)}, f32[256,1024]{1,0:T(8,128)}) custom-call(bf16[240,1024]{1,0:T(8,128)(2,1)S(1)} %get-tuple-element.47.qc_ref, bf16[256,1024]{1,0:T(8,128)(2,1)S(1)} %collective-permute-done.a_ref, bf16[384,1024]{1,0:T(8,128)(2,1)S(1)} %constant_dynamic-update-slice_fusion.u_ref, ...), custom_call_target="tpu_custom_call" | custom-call | tf_op jit(solution)/shard_map/pallas_call | solution.py:364
  58.3 0.1 collective-permute-start.7
  58.4 1.9 %shard_map.91 = (bf16[256,512]{1,0:T(8,128)(2,1)S(1)}, bf16[256,512]{1,0:T(8,128)(2,1)S(1)}, bf16[256,512]{1,0:T(8,128)(2,1)S(1)}, bf16[256,512]{1,0:T(8,128)(2,...) custom-call(s32[4]{0:T(128)S(1)} %pad_add_fusion.at_ref, ...), custom_call_target="tpu_custom_call" | custom-call | tf_op jit(solution)/shard_map/pallas_call | solution.py:374
  60.3 0.9 collective-permute-start.14
  61.2 2.7 %collective-permute-start.15 = (bf16[256,512]{1,0:T(8,128)(2,1)S(1)}, bf16[256,512]{1,0:T(8,128)(2,1)S(1)}, u32[]{:S(2)}, u32[]{:S(2)}) collective-permute-start(bf16[256,512]{1,0:T(8,128)(2,1)S(1)} %get-tuple-element.72), channel_id=1, source_target_pairs={{0,8},{1,9},{2,10},{3,11},{4,12},{5,13},{6,14},{7,15},{8,0},{9,1},... | collective-permute-start | bytes 786440 | tf_op jit(solution)/shard_map/ppermute | solution.py:29
  63.9 1.2 collective-permute-start.16
  65.1 1.3 collective-permute-start.17
  66.5 3.1 %collective-permute-done.14.refs_1_ = bf16[256,512]{1,0:T(8,128)(2,1)S(1)} collective-permute-done((bf16[256,512]{1,0:T(8,128)(2,1)S(1)}, bf16[256,512]{1,0:T(8,128)(2,1)S(1)}, u32[]{:S(2)}, u32[]{:S(2)}) %collective-permute-start.14) | collective-permute-done | bytes 262176 | tf_op jit(solution)/shard_map/ppermute | solution.py:29
  69.5 2.9 %collective-permute-start.18 = (bf16[1024,128]{1,0:T(8,128)(2,1)S(1)}, bf16[1024,128]{1,0:T(8,128)(2,1)S(1)}, u32[]{:S(2)}, u32[]{:S(2)}) collective-permute-start(bf16[1024,128]{1,0:T(8,128)(2,1)S(1)} %get-tuple-element.76), channel_id=1, source_target_pairs={{0,32},{16,48},{32,0},{48,16},{64,96},{80,112},{96,64},{112,80},{1... | collective-permute-start | bytes 786440 | tf_op jit(solution)/shard_map/ppermute | solution.py:29
  72.4 3.8 %collective-permute-done.15.refs_2_ = bf16[256,512]{1,0:T(8,128)(2,1)S(1)} collective-permute-done((bf16[256,512]{1,0:T(8,128)(2,1)S(1)}, bf16[256,512]{1,0:T(8,128)(2,1)S(1)}, u32[]{:S(2)}, u32[]{:S(2)}) %collective-permute-start.15) | collective-permute-done | bytes 262176 | tf_op jit(solution)/shard_map/ppermute | solution.py:29
  76.2 2.8 %collective-permute-start.19 = (bf16[1024,128]{1,0:T(8,128)(2,1)S(1)}, bf16[1024,128]{1,0:T(8,128)(2,1)S(1)}, u32[]{:S(2)}, u32[]{:S(2)}) collective-permute-start(bf16[1024,128]{1,0:T(8,128)(2,1)S(1)} %get-tuple-element.77), channel_id=1, source_target_pairs={{0,48},{16,32},{32,16},{48,0},{64,112},{80,96},{96,80},{112,64},{1... | collective-permute-start | bytes 786440 | tf_op jit(solution)/shard_map/ppermute | solution.py:29
  79.0 1.7 %collective-permute-done.18.refs_6_ = bf16[1024,128]{1,0:T(8,128)(2,1)S(1)} collective-permute-done((bf16[1024,128]{1,0:T(8,128)(2,1)S(1)}, bf16[1024,128]{1,0:T(8,128)(2,1)S(1)}, u32[]{:S(2)}, u32[]{:S(2)}) %collective-permute-start.18) | collective-permute-done | bytes 262176 | tf_op jit(solution)/shard_map/ppermute | solution.py:29
  80.7 5.5 %collective-permute-done.19.refs_7_ = bf16[1024,128]{1,0:T(8,128)(2,1)S(1)} collective-permute-done((bf16[1024,128]{1,0:T(8,128)(2,1)S(1)}, bf16[1024,128]{1,0:T(8,128)(2,1)S(1)}, u32[]{:S(2)}, u32[]{:S(2)}) %collective-permute-start.19) | collective-permute-done | bytes 262176 | tf_op jit(solution)/shard_map/ppermute | solution.py:29
  86.2 0.3 shard_map.92
  86.5 0.3 collective-permute-start.20
  86.8 3.0 %collective-permute-start.21 = (bf16[256,128]{1,0:T(8,128)(2,1)S(1)}, bf16[256,128]{1,0:T(8,128)(2,1)S(1)}, u32[]{:S(2)}, u32[]{:S(2)}) collective-permute-start(bf16[256,128]{1,0:T(8,128)(2,1)S(1)} %get-tuple-element.80), channel_id=1, source_target_pairs={{0,32},{16,48},{32,0},{48,16},{64,96},{80,112},{96,64},{112,80},{1... | collective-permute-start | bytes 196616 | tf_op jit(solution)/shard_map/ppermute | solution.py:29
  89.8 1.4 %collective-permute-start.22 = (bf16[256,128]{1,0:T(8,128)(2,1)S(1)}, bf16[256,128]{1,0:T(8,128)(2,1)S(1)}, u32[]{:S(2)}, u32[]{:S(2)}) collective-permute-start(bf16[256,128]{1,0:T(8,128)(2,1)S(1)} %get-tuple-element.81), channel_id=1, source_target_pairs={{0,48},{16,32},{32,16},{48,0},{64,112},{80,96},{96,80},{112,64},{1... | collective-permute-start | bytes 196616 | tf_op jit(solution)/shard_map/ppermute | solution.py:29
  91.2 3.6 %collective-permute-start.24 = (bf16[256,128]{1,0:T(8,128)(2,1)S(1)}, bf16[256,128]{1,0:T(8,128)(2,1)S(1)}, u32[]{:S(2)}, u32[]{:S(2)}) collective-permute-start(bf16[256,128]{1,0:T(8,128)(2,1)S(1)} %get-tuple-element.84), channel_id=1, source_target_pairs={{0,8},{1,9},{2,10},{3,11},{4,12},{5,13},{6,14},{7,15},{8,0},{9,1},... | collective-permute-start | bytes 196616 | tf_op jit(solution)/shard_map/ppermute | solution.py:29
  94.9 1.1 collective-permute-start.25
  96.0 1.9 %collective-permute-done.24.refs_6_ = bf16[256,128]{1,0:T(8,128)(2,1)S(1)} collective-permute-done((bf16[256,128]{1,0:T(8,128)(2,1)S(1)}, bf16[256,128]{1,0:T(8,128)(2,1)S(1)}, u32[]{:S(2)}, u32[]{:S(2)}) %collective-permute-start.24) | collective-permute-done | bytes 65568 | tf_op jit(solution)/shard_map/ppermute | solution.py:29
  97.9 2.5 %collective-permute-done.25.refs_7_ = bf16[256,128]{1,0:T(8,128)(2,1)S(1)} collective-permute-done((bf16[256,128]{1,0:T(8,128)(2,1)S(1)}, bf16[256,128]{1,0:T(8,128)(2,1)S(1)}, u32[]{:S(2)}, u32[]{:S(2)}) %collective-permute-start.25) | collective-permute-done | bytes 65568 | tf_op jit(solution)/shard_map/ppermute | solution.py:29
  100.4 0.1 shard_map.93
  100.4 2.0 %collective-permute-start.26 = (bf16[128,256]{1,0:T(8,128)(2,1)S(1)}, bf16[128,256]{1,0:T(8,128)(2,1)S(1)}, u32[]{:S(2)}, u32[]{:S(2)}) collective-permute-start(bf16[128,256]{1,0:T(8,128)(2,1)S(1)} %get-tuple-element.87), channel_id=1, source_target_pairs={{0,2},{1,3},{2,0},{3,1},{4,6},{5,7},{6,4},{7,5},{8,10},{9,11},{10,... | collective-permute-start | bytes 196616 | tf_op jit(solution)/shard_map/ppermute | solution.py:29
  102.4 2.3 %collective-permute-done.26 = bf16[128,256]{1,0:T(8,128)(2,1)S(1)} collective-permute-done((bf16[128,256]{1,0:T(8,128)(2,1)S(1)}, bf16[128,256]{1,0:T(8,128)(2,1)S(1)}, u32[]{:S(2)}, u32[]{:S(2)}) %collective-permute-start.26) | collective-permute-done | bytes 65568 | tf_op jit(solution)/shard_map/ppermute | solution.py:29
  104.8 3.4 %collective-permute-start.27 = (bf16[128,256]{1,0:T(8,128)(2,1)S(1)}, bf16[128,256]{1,0:T(8,128)(2,1)S(1)}, u32[]{:S(2)}, u32[]{:S(2)}) collective-permute-start(bf16[128,256]{1,0:T(8,128)(2,1)S(1)} %add_convert_fusion.2), channel_id=1, source_target_pairs={{0,64},{16,80},{32,96},{48,112},{64,0},{80,16},{96,32},{112,48},{1... | collective-permute-start | bytes 196616 | tf_op jit(solution)/shard_map/ppermute | solution.py:29
  108.2 0.3 fusion.1
  108.5 0.0 copy-start.6
  108.5 2.0 %collective-permute-start.9 = (bf16[128,1024]{1,0:T(8,128)(2,1)S(1)}, bf16[128,1024]{1,0:T(8,128)(2,1)S(1)}, u32[]{:S(2)}, u32[]{:S(2)}) collective-permute-start(bf16[128,1024]{1,0:T(8,128)(2,1)S(1)} %get-tuple-element.90), channel_id=1, source_target_pairs={{0,2},{1,3},{2,0},{3,1},{4,6},{5,7},{6,4},{7,5},{8,10},{9,11},{10,... | collective-permute-start | bytes 786440 | tf_op jit(solution)/shard_map/ppermute | solution.py:29
  110.6 0.6 collective-permute-done.27
  111.2 6.1 %collective-permute-start.28 = (bf16[128,256]{1,0:T(8,128)(2,1)S(1)}, bf16[128,256]{1,0:T(8,128)(2,1)S(1)}, u32[]{:S(2)}, u32[]{:S(2)}) collective-permute-start(bf16[128,256]{1,0:T(8,128)(2,1)S(1)} %add_convert_fusion.1), channel_id=1, source_target_pairs={{0,192},{16,208},{32,224},{48,240},{64,128},{80,144},{96,160},{112... | collective-permute-start | bytes 196616 | tf_op jit(solution)/shard_map/ppermute | solution.py:29
  117.3 0.1 slice_add_fusion
  117.4 0.1 collective-permute-start.10
  117.5 2.8 %collective-permute-done.28 = bf16[128,256]{1,0:T(8,128)(2,1)S(1)} collective-permute-done((bf16[128,256]{1,0:T(8,128)(2,1)S(1)}, bf16[128,256]{1,0:T(8,128)(2,1)S(1)}, u32[]{:S(2)}, u32[]{:S(2)}) %collective-permute-start.28) | collective-permute-done | bytes 65568 | tf_op jit(solution)/shard_map/ppermute | solution.py:29
  120.2 0.1 collective-permute-start.29
  120.3 1.8 %collective-permute-start.30 = (bf16[128,256]{1,0:T(8,128)(2,1)S(1)}, bf16[128,256]{1,0:T(8,128)(2,1)S(1)}, u32[]{:S(2)}, u32[]{:S(2)}) collective-permute-start(bf16[128,256]{1,0:T(8,128)(2,1)S(1)} %add_convert_fusion.a), channel_id=1, source_target_pairs={{0,32},{16,48},{32,0},{48,16},{64,96},{80,112},{96,64},{112,80},{1... | collective-permute-start | bytes 196616 | tf_op jit(solution)/shard_map/ppermute | solution.py:29
  122.1 2.9 %collective-permute-start.31 = (bf16[128,256]{1,0:T(8,128)(2,1)S(1)}, bf16[128,256]{1,0:T(8,128)(2,1)S(1)}, u32[]{:S(2)}, u32[]{:S(2)}) collective-permute-start(bf16[128,256]{1,0:T(8,128)(2,1)S(1)} %add_convert_fusion.a), channel_id=1, source_target_pairs={{0,48},{16,32},{32,16},{48,0},{64,112},{80,96},{96,80},{112,64},{1... | collective-permute-start | bytes 196616 | tf_op jit(solution)/shard_map/ppermute | solution.py:29
  125.0 0.1 collective-permute-start.8
  125.2 1.1 collective-permute-start.11
  126.3 5.4 %shard_map.88 = (bf16[256,1024]{1,0:T(8,128)(2,1)}, f32[256,1024]{1,0:T(8,128)S(1)}, f32[256,1024]{1,0:T(8,128)S(1)}) custom-call(bf16[256,1024]{1,0:T(8,128)(2,1)S(1)} %bitcast.20, bf16[256,1024]{1,0:T(8,128)(2,1)S(1)} %bitcast.13, bf16[256,1024]{1,0:T(8,128)(2,1)S(1)} %bitcast.16, bf16[256,1024]{1,0:T(8,128)(2,1)S(1)} %get-tuple-element.46.datt_ref, ...), custom_call_target="tpu_custom_call" | custom-call | tf_op jit(solution)/shard_map/pallas_call | solution.py:385
  131.7 1.4 %shard_map.94 = f32[128,1024]{1,0:T(8,128)} custom-call(s32[4]{0:T(128)S(1)} %pad_add_fusion.at_ref, bf16[128,256]{1,0:T(8,128)(2,1)S(1)} %add_convert_fusion.a, bf16[128,256]{1,0:T(8,128)(2,1)S(1)} %collective-permute-done.29.b, bf16[128,256]{1,0:T(8,128)(2,1)S(1)} %collective-permute-done.30.c, bf16[128,256]{1,0:T(8,128)(2,1)S(1)} %collective-permute-done.31.d), custom_call_target="tpu_custom_call" | custom-call | tf_op jit(solution)/shard_map/pallas_call | solution.py:418
  133.2 2.1 %shard_map.89 = (bf16[256,1024]{1,0:T(8,128)(2,1)}, bf16[256,1024]{1,0:T(8,128)(2,1)}) custom-call(f32[256,1024]{1,0:T(8,128)S(1)} %get-tuple-element.62.gk_ref, f32[256,1024]{1,0:T(8,128)S(1)} %get-tuple-element.63.gv_ref, bf16[256,1024]{1,0:T(8,128)(2,1)S(1)} %slice.39.r1, bf16[128,1024]{1,0:T(8,128)(2,1)S(1)} %collective-permute-done.8.r2, ...), custom_call_target="tpu_custom_call" | custom-call | tf_op jit(solution)/shard_map/pallas_call | solution.py:398
  (50 shorter events, 0.3 us)
Async XLA Ops:
  0.6 1.0 copy-start
  1.7 1.0 copy-start.2
  2.7 20.3 %copy-start.4 = (bf16[1,256,2048]{2,1,0:T(8,128)(2,1)S(1)}, bf16[1,256,2048]{2,1,0:T(8,128)(2,1)}, u32[]{:S(2)}) copy-start(bf16[1,256,2048]{2,1,0:T(8,128)(2,1)} %param.8) | copy-start | bytes 3145732
  4.3 13.5 %collective-permute-start.1 = (bf16[128,1024]{1,0:T(8,128)(2,1)S(1)}, bf16[128,1024]{1,0:T(8,128)(2,1)S(1)}, u32[]{:S(2)}, u32[]{:S(2)}) collective-permute-start(bf16[128,1024]{1,0:T(8,128)(2,1)S(1)} %get-tuple-element.49), channel_id=1, source_target_pairs={{0,2},{1,3},{2,0},{3,1},{4,6},{5,7},{6,4},{7,5},{8,10},{9,11},{10,... | collective-permute-start | bytes 786440 | tf_op jit(solution)/shard_map/ppermute | solution.py:29
  6.1 6.3 %collective-permute-start.2 = (bf16[64,1024]{1,0:T(8,128)(2,1)S(1)}, bf16[64,1024]{1,0:T(8,128)(2,1)S(1)}, u32[]{:S(2)}, u32[]{:S(2)}) collective-permute-start(bf16[64,1024]{1,0:T(8,128)(2,1)S(1)} %get-tuple-element.50), channel_id=1, source_target_pairs={{0,4},{1,5},{2,6},{3,7},{4,0},{5,1},{6,2},{7,3},{8,12},{9,13},{10,... | collective-permute-start | bytes 393224 | tf_op jit(solution)/shard_map/ppermute | solution.py:29
  6.1 18.0 %copy-start.1 = (bf16[1,256,1024]{2,1,0:T(8,128)(2,1)S(1)}, bf16[1,256,1024]{2,1,0:T(8,128)(2,1)}, u32[]{:S(2)}) copy-start(bf16[1,256,1024]{2,1,0:T(8,128)(2,1)} %param.6) | copy-start | bytes 1572868
  6.1 18.0 %copy-start.3 = (bf16[1,256,1024]{2,1,0:T(8,128)(2,1)S(1)}, bf16[1,256,1024]{2,1,0:T(8,128)(2,1)}, u32[]{:S(2)}) copy-start(bf16[1,256,1024]{2,1,0:T(8,128)(2,1)} %param.7) | copy-start | bytes 1572868
  6.1 5.5 %collective-permute-start.3 = (bf16[32,1024]{1,0:T(8,128)(2,1)S(1)}, bf16[32,1024]{1,0:T(8,128)(2,1)S(1)}, u32[]{:S(2)}, u32[]{:S(2)}) collective-permute-start(bf16[32,1024]{1,0:T(8,128)(2,1)S(1)} %get-tuple-element.51), channel_id=1, source_target_pairs={{0,12},{1,13},{2,14},{3,15},{4,8},{5,9},{6,10},{7,11},{8,4},{9,5},... | collective-permute-start | bytes 196616 | tf_op jit(solution)/shard_map/ppermute | solution.py:29
  11.6 4.3 %collective-permute-start.4 = (bf16[32,1024]{1,0:T(8,128)(2,1)S(1)}, bf16[32,1024]{1,0:T(8,128)(2,1)S(1)}, u32[]{:S(2)}, u32[]{:S(2)}) collective-permute-start(bf16[32,1024]{1,0:T(8,128)(2,1)S(1)} %collective-permute-done.3), channel_id=1, source_target_pairs={{0,4},{1,5},{2,6},{3,7},{4,0},{5,1},{6,2},{7,3},{8,12},{9,13},{10,... | collective-permute-start | bytes 196616 | tf_op jit(solution)/shard_map/ppermute | solution.py:29
  15.9 6.5 %collective-permute-start.5 = (bf16[128,1024]{1,0:T(8,128)(2,1)S(1)}, bf16[128,1024]{1,0:T(8,128)(2,1)S(1)}, u32[]{:S(2)}, u32[]{:S(2)}) collective-permute-start(bf16[128,1024]{1,0:T(8,128)(2,1)S(1)} %pad_maximum_fusion), channel_id=1, source_target_pairs={{0,2},{1,3},{2,0},{3,1},{4,6},{5,7},{6,4},{7,5},{8,10},{9,11},{10,... | collective-permute-start | bytes 786440 | tf_op jit(solution)/shard_map/ppermute | solution.py:29
  22.4 14.1 %collective-permute-start.6 = (bf16[384,1024]{1,0:T(8,128)(2,1)S(1)}, bf16[384,1024]{1,0:T(8,128)(2,1)}, u32[]{:S(2)}, u32[]{:S(2)}) collective-permute-start(bf16[384,1024]{1,0:T(8,128)(2,1)S(1)} %constant_dynamic-update-slice_fusion.u_ref), channel_id=1, source_target_pairs={{0,1},{1,0},{2,3},{3,2},{4,5},{5,4},{6,7},{7,6},{8,9},{9,8},{10,11... | collective-permute-start | bytes 2359304 | tf_op jit(solution)/shard_map/ppermute | solution.py:29
  22.5 14.0 %collective-permute-start = (bf16[256,1024]{1,0:T(8,128)(2,1)}, bf16[256,1024]{1,0:T(8,128)(2,1)S(1)}, u32[]{:S(2)}, u32[]{:S(2)}) collective-permute-start(bf16[256,1024]{1,0:T(8,128)(2,1)} %get-tuple-element.48), channel_id=1, source_target_pairs={{0,1},{1,0},{2,3},{3,2},{4,5},{5,4},{6,7},{7,6},{8,9},{9,8},{10,11... | collective-permute-start | bytes 1572872 | tf_op jit(solution)/shard_map/ppermute | solution.py:29
  23.9 34.5 %collective-permute-start.12 = (bf16[1024,256]{1,0:T(8,128)(2,1)S(1)}, bf16[1024,256]{1,0:T(8,128)(2,1)S(1)}, u32[]{:S(2)}, u32[]{:S(2)}) collective-permute-start(bf16[1024,256]{1,0:T(8,128)(2,1)S(1)} %get-tuple-element.69), channel_id=1, source_target_pairs={{0,1},{1,0},{2,3},{3,2},{4,5},{5,4},{6,7},{7,6},{8,9},{9,8},{10,11... | collective-permute-start | bytes 1572872 | tf_op jit(solution)/shard_map/ppermute | solution.py:29
  24.1 1.0 copy-start.5
  33.5 1.0 copy-start.7
  34.5 1.0 copy-start.8
  35.5 1.0 copy-start.9
  47.8 10.6 %collective-permute-start.13 = (bf16[256,1024]{1,0:T(8,128)(2,1)S(1)}, bf16[256,1024]{1,0:T(8,128)(2,1)S(1)}, u32[]{:S(2)}, u32[]{:S(2)}) collective-permute-start(bf16[256,1024]{1,0:T(8,128)(2,1)S(1)} %get-tuple-element.55.att_ref), channel_id=1, source_target_pairs={{0,1},{1,0},{2,3},{3,2},{4,5},{5,4},{6,7},{7,6},{8,9},{9,8},{10,11... | collective-permute-start | bytes 1572872 | tf_op jit(solution)/shard_map/ppermute | solution.py:29
  58.3 49.9 %collective-permute-start.7 = (bf16[640,1024]{1,0:T(8,128)(2,1)}, bf16[640,1024]{1,0:T(8,128)(2,1)S(1)}, u32[]{:S(2)}, u32[]{:S(2)}) collective-permute-start(bf16[640,1024]{1,0:T(8,128)(2,1)} %get-tuple-element.64), channel_id=1, source_target_pairs={{0,1},{1,0},{2,3},{3,2},{4,5},{5,4},{6,7},{7,6},{8,9},{9,8},{10,11... | collective-permute-start | bytes 3932168 | tf_op jit(solution)/shard_map/ppermute | solution.py:29
  60.3 47.9 %copy-start.10 = (f32[384,1024]{1,0:T(8,128)S(1)}, f32[384,1024]{1,0:T(8,128)}, u32[]{:S(2)}) copy-start(f32[384,1024]{1,0:T(8,128)} %get-tuple-element.65) | copy-start | bytes 4718596
  60.3 9.2 %collective-permute-start.14 = (bf16[256,512]{1,0:T(8,128)(2,1)S(1)}, bf16[256,512]{1,0:T(8,128)(2,1)S(1)}, u32[]{:S(2)}, u32[]{:S(2)}) collective-permute-start(bf16[256,512]{1,0:T(8,128)(2,1)S(1)} %get-tuple-element.71), channel_id=1, source_target_pairs={{0,4},{1,5},{2,6},{3,7},{4,0},{5,1},{6,2},{7,3},{8,12},{9,13},{10,... | collective-permute-start | bytes 786440 | tf_op jit(solution)/shard_map/ppermute | solution.py:29
  61.2 15.0 %collective-permute-start.15 = (bf16[256,512]{1,0:T(8,128)(2,1)S(1)}, bf16[256,512]{1,0:T(8,128)(2,1)S(1)}, u32[]{:S(2)}, u32[]{:S(2)}) collective-permute-start(bf16[256,512]{1,0:T(8,128)(2,1)S(1)} %get-tuple-element.72), channel_id=1, source_target_pairs={{0,8},{1,9},{2,10},{3,11},{4,12},{5,13},{6,14},{7,15},{8,0},{9,1},... | collective-permute-start | bytes 786440 | tf_op jit(solution)/shard_map/ppermute | solution.py:29
  63.9 15.1 %collective-permute-start.16 = (bf16[256,512]{1,0:T(8,128)(2,1)S(1)}, bf16[256,512]{1,0:T(8,128)(2,1)S(1)}, u32[]{:S(2)}, u32[]{:S(2)}) collective-permute-start(bf16[256,512]{1,0:T(8,128)(2,1)S(1)} %get-tuple-element.73), channel_id=1, source_target_pairs={{0,12},{1,13},{2,14},{3,15},{4,8},{5,9},{6,10},{7,11},{8,4},{9,5},... | collective-permute-start | bytes 786440 | tf_op jit(solution)/shard_map/ppermute | solution.py:29
  65.1 13.9 %collective-permute-start.17 = (bf16[1024,128]{1,0:T(8,128)(2,1)S(1)}, bf16[1024,128]{1,0:T(8,128)(2,1)S(1)}, u32[]{:S(2)}, u32[]{:S(2)}) collective-permute-start(bf16[1024,128]{1,0:T(8,128)(2,1)S(1)} %get-tuple-element.75), channel_id=1, source_target_pairs={{0,16},{16,0},{32,48},{48,32},{64,80},{80,64},{96,112},{112,96},{1... | collective-permute-start | bytes 786440 | tf_op jit(solution)/shard_map/ppermute | solution.py:29
  69.5 11.1 %collective-permute-start.18 = (bf16[1024,128]{1,0:T(8,128)(2,1)S(1)}, bf16[1024,128]{1,0:T(8,128)(2,1)S(1)}, u32[]{:S(2)}, u32[]{:S(2)}) collective-permute-start(bf16[1024,128]{1,0:T(8,128)(2,1)S(1)} %get-tuple-element.76), channel_id=1, source_target_pairs={{0,32},{16,48},{32,0},{48,16},{64,96},{80,112},{96,64},{112,80},{1... | collective-permute-start | bytes 786440 | tf_op jit(solution)/shard_map/ppermute | solution.py:29
  76.2 10.0 %collective-permute-start.19 = (bf16[1024,128]{1,0:T(8,128)(2,1)S(1)}, bf16[1024,128]{1,0:T(8,128)(2,1)S(1)}, u32[]{:S(2)}, u32[]{:S(2)}) collective-permute-start(bf16[1024,128]{1,0:T(8,128)(2,1)S(1)} %get-tuple-element.77), channel_id=1, source_target_pairs={{0,48},{16,32},{32,16},{48,0},{64,112},{80,96},{96,80},{112,64},{1... | collective-permute-start | bytes 786440 | tf_op jit(solution)/shard_map/ppermute | solution.py:29
  86.5 4.8 %collective-permute-start.20 = (bf16[256,128]{1,0:T(8,128)(2,1)S(1)}, bf16[256,128]{1,0:T(8,128)(2,1)S(1)}, u32[]{:S(2)}, u32[]{:S(2)}) collective-permute-start(bf16[256,128]{1,0:T(8,128)(2,1)S(1)} %get-tuple-element.79), channel_id=1, source_target_pairs={{0,16},{16,0},{32,48},{48,32},{64,80},{80,64},{96,112},{112,96},{1... | collective-permute-start | bytes 196616 | tf_op jit(solution)/shard_map/ppermute | solution.py:29
  86.8 8.1 %collective-permute-start.21 = (bf16[256,128]{1,0:T(8,128)(2,1)S(1)}, bf16[256,128]{1,0:T(8,128)(2,1)S(1)}, u32[]{:S(2)}, u32[]{:S(2)}) collective-permute-start(bf16[256,128]{1,0:T(8,128)(2,1)S(1)} %get-tuple-element.80), channel_id=1, source_target_pairs={{0,32},{16,48},{32,0},{48,16},{64,96},{80,112},{96,64},{112,80},{1... | collective-permute-start | bytes 196616 | tf_op jit(solution)/shard_map/ppermute | solution.py:29
  89.8 6.1 %collective-permute-start.22 = (bf16[256,128]{1,0:T(8,128)(2,1)S(1)}, bf16[256,128]{1,0:T(8,128)(2,1)S(1)}, u32[]{:S(2)}, u32[]{:S(2)}) collective-permute-start(bf16[256,128]{1,0:T(8,128)(2,1)S(1)} %get-tuple-element.81), channel_id=1, source_target_pairs={{0,48},{16,32},{32,16},{48,0},{64,112},{80,96},{96,80},{112,64},{1... | collective-permute-start | bytes 196616 | tf_op jit(solution)/shard_map/ppermute | solution.py:29
  91.2 4.7 %collective-permute-start.23 = (bf16[256,128]{1,0:T(8,128)(2,1)S(1)}, bf16[256,128]{1,0:T(8,128)(2,1)S(1)}, u32[]{:S(2)}, u32[]{:S(2)}) collective-permute-start(bf16[256,128]{1,0:T(8,128)(2,1)S(1)} %get-tuple-element.83), channel_id=1, source_target_pairs={{0,4},{1,5},{2,6},{3,7},{4,0},{5,1},{6,2},{7,3},{8,12},{9,13},{10,... | collective-permute-start | bytes 196616 | tf_op jit(solution)/shard_map/ppermute | solution.py:29
  91.2 6.6 %collective-permute-start.24 = (bf16[256,128]{1,0:T(8,128)(2,1)S(1)}, bf16[256,128]{1,0:T(8,128)(2,1)S(1)}, u32[]{:S(2)}, u32[]{:S(2)}) collective-permute-start(bf16[256,128]{1,0:T(8,128)(2,1)S(1)} %get-tuple-element.84), channel_id=1, source_target_pairs={{0,8},{1,9},{2,10},{3,11},{4,12},{5,13},{6,14},{7,15},{8,0},{9,1},... | collective-permute-start | bytes 196616 | tf_op jit(solution)/shard_map/ppermute | solution.py:29
  94.9 5.5 %collective-permute-start.25 = (bf16[256,128]{1,0:T(8,128)(2,1)S(1)}, bf16[256,128]{1,0:T(8,128)(2,1)S(1)}, u32[]{:S(2)}, u32[]{:S(2)}) collective-permute-start(bf16[256,128]{1,0:T(8,128)(2,1)S(1)} %get-tuple-element.85), channel_id=1, source_target_pairs={{0,12},{1,13},{2,14},{3,15},{4,8},{5,9},{6,10},{7,11},{8,4},{9,5},... | collective-permute-start | bytes 196616 | tf_op jit(solution)/shard_map/ppermute | solution.py:29
  100.4 4.4 %collective-permute-start.26 = (bf16[128,256]{1,0:T(8,128)(2,1)S(1)}, bf16[128,256]{1,0:T(8,128)(2,1)S(1)}, u32[]{:S(2)}, u32[]{:S(2)}) collective-permute-start(bf16[128,256]{1,0:T(8,128)(2,1)S(1)} %get-tuple-element.87), channel_id=1, source_target_pairs={{0,2},{1,3},{2,0},{3,1},{4,6},{5,7},{6,4},{7,5},{8,10},{9,11},{10,... | collective-permute-start | bytes 196616 | tf_op jit(solution)/shard_map/ppermute | solution.py:29
  104.8 6.4 %collective-permute-start.27 = (bf16[128,256]{1,0:T(8,128)(2,1)S(1)}, bf16[128,256]{1,0:T(8,128)(2,1)S(1)}, u32[]{:S(2)}, u32[]{:S(2)}) collective-permute-start(bf16[128,256]{1,0:T(8,128)(2,1)S(1)} %add_convert_fusion.2), channel_id=1, source_target_pairs={{0,64},{16,80},{32,96},{48,112},{64,0},{80,16},{96,32},{112,48},{1... | collective-permute-start | bytes 196616 | tf_op jit(solution)/shard_map/ppermute | solution.py:29
  108.5 17.8 %copy-start.6 = (bf16[1,256,1024]{2,1,0:T(8,128)(2,1)S(1)}, bf16[1,256,1024]{2,1,0:T(8,128)(2,1)}, u32[]{:S(2)}) copy-start(bf16[1,256,1024]{2,1,0:T(8,128)(2,1)} %param.5) | copy-start | bytes 1572868
  108.5 8.7 %collective-permute-start.9 = (bf16[128,1024]{1,0:T(8,128)(2,1)S(1)}, bf16[128,1024]{1,0:T(8,128)(2,1)S(1)}, u32[]{:S(2)}, u32[]{:S(2)}) collective-permute-start(bf16[128,1024]{1,0:T(8,128)(2,1)S(1)} %get-tuple-element.90), channel_id=1, source_target_pairs={{0,2},{1,3},{2,0},{3,1},{4,6},{5,7},{6,4},{7,5},{8,10},{9,11},{10,... | collective-permute-start | bytes 786440 | tf_op jit(solution)/shard_map/ppermute | solution.py:29
  111.2 9.0 %collective-permute-start.28 = (bf16[128,256]{1,0:T(8,128)(2,1)S(1)}, bf16[128,256]{1,0:T(8,128)(2,1)S(1)}, u32[]{:S(2)}, u32[]{:S(2)}) collective-permute-start(bf16[128,256]{1,0:T(8,128)(2,1)S(1)} %add_convert_fusion.1), channel_id=1, source_target_pairs={{0,192},{16,208},{32,224},{48,240},{64,128},{80,144},{96,160},{112... | collective-permute-start | bytes 196616 | tf_op jit(solution)/shard_map/ppermute | solution.py:29
  117.4 7.8 %collective-permute-start.10 = (bf16[96,1024]{1,0:T(8,128)(2,1)S(1)}, bf16[96,1024]{1,0:T(8,128)(2,1)S(1)}, u32[]{:S(2)}, u32[]{:S(2)}) collective-permute-start(bf16[96,1024]{1,0:T(8,128)(2,1)S(1)} %slice.55), channel_id=1, source_target_pairs={{0,4},{1,5},{2,6},{3,7},{4,0},{5,1},{6,2},{7,3},{8,12},{9,13},{10,... | collective-permute-start | bytes 589832 | tf_op jit(solution)/shard_map/ppermute | solution.py:29
  120.2 11.5 %collective-permute-start.29 = (bf16[128,256]{1,0:T(8,128)(2,1)S(1)}, bf16[128,256]{1,0:T(8,128)(2,1)S(1)}, u32[]{:S(2)}, u32[]{:S(2)}) collective-permute-start(bf16[128,256]{1,0:T(8,128)(2,1)S(1)} %add_convert_fusion.a), channel_id=1, source_target_pairs={{0,16},{16,0},{32,48},{48,32},{64,80},{80,64},{96,112},{112,96},{1... | collective-permute-start | bytes 196616 | tf_op jit(solution)/shard_map/ppermute | solution.py:29
  120.3 11.4 %collective-permute-start.30 = (bf16[128,256]{1,0:T(8,128)(2,1)S(1)}, bf16[128,256]{1,0:T(8,128)(2,1)S(1)}, u32[]{:S(2)}, u32[]{:S(2)}) collective-permute-start(bf16[128,256]{1,0:T(8,128)(2,1)S(1)} %add_convert_fusion.a), channel_id=1, source_target_pairs={{0,32},{16,48},{32,0},{48,16},{64,96},{80,112},{96,64},{112,80},{1... | collective-permute-start | bytes 196616 | tf_op jit(solution)/shard_map/ppermute | solution.py:29
  122.1 9.6 %collective-permute-start.31 = (bf16[128,256]{1,0:T(8,128)(2,1)S(1)}, bf16[128,256]{1,0:T(8,128)(2,1)S(1)}, u32[]{:S(2)}, u32[]{:S(2)}) collective-permute-start(bf16[128,256]{1,0:T(8,128)(2,1)S(1)} %add_convert_fusion.a), channel_id=1, source_target_pairs={{0,48},{16,32},{32,16},{48,0},{64,112},{80,96},{96,80},{112,64},{1... | collective-permute-start | bytes 196616 | tf_op jit(solution)/shard_map/ppermute | solution.py:29
  125.0 8.1 %collective-permute-start.8 = (bf16[128,1024]{1,0:T(8,128)(2,1)S(1)}, bf16[128,1024]{1,0:T(8,128)(2,1)S(1)}, u32[]{:S(2)}, u32[]{:S(2)}) collective-permute-start(bf16[128,1024]{1,0:T(8,128)(2,1)S(1)} %get-tuple-element.91), channel_id=1, source_target_pairs={{0,2},{1,3},{2,0},{3,1},{4,6},{5,7},{6,4},{7,5},{8,10},{9,11},{10,... | collective-permute-start | bytes 786440 | tf_op jit(solution)/shard_map/ppermute | solution.py:29
  125.2 8.0 %collective-permute-start.11 = (bf16[32,1024]{1,0:T(8,128)(2,1)S(1)}, bf16[32,1024]{1,0:T(8,128)(2,1)S(1)}, u32[]{:S(2)}, u32[]{:S(2)}) collective-permute-start(bf16[32,1024]{1,0:T(8,128)(2,1)S(1)} %fusion), channel_id=1, source_target_pairs={{0,12},{1,13},{2,14},{3,15},{4,8},{5,9},{6,10},{7,11},{8,4},{9,5},... | collective-permute-start | bytes 196616 | tf_op jit(solution)/shard_map/ppermute | solution.py:29

commit v2 on v1

v2 whole, which is shorter than its diff:
```python
import functools
import math

import jax
import jax.numpy as jnp
from jax import lax
from jax.experimental import pallas as pl
from jax.experimental.pallas import tpu as pltpu
from jax.sharding import PartitionSpec as P

HEADS = 8
HDIM = 128
ROWS = 256
WIDTH = 1024
DMODEL = 2048
SCALE = HDIM**-0.5
SCALE2 = SCALE * math.log2(math.e)
LEVEL_ROWS = (128, 64, 32, 16)
SPANS = {2: ((0, 64),), 3: ((128, 32), (256, 32)), 4: ((192, 16), (224, 16), (320, 16), (352, 16))}
BF = jnp.bfloat16
F32 = jnp.float32
VMEM = pltpu.CompilerParams(vmem_limit_bytes=16 * 1024 * 1024)

CORE, ZLO, Y1, Y2, Y3 = 1, 2, 4, 8, 12
X1, X2, X3, ZH1, ZH3 = 1, 2, 3, 4, 12
ORDER = (0, 3, 1, 2)


def swap(value, axis, mask):
    pairs = [(source, source ^ mask) for source in range(16)]
    return lax.ppermute(value, axis, pairs)


def dot(a, b):
    return jnp.dot(a, b, preferred_element_type=F32)


def dot_nt(a, b):
    return lax.dot_general(a, b, (((1,), (1,)), ((), ())), preferred_element_type=F32)


def dot_tn(a, b):
    return lax.dot_general(a, b, (((0,), (0,)), ((), ())), preferred_element_type=F32)


def pool_matrix(rows):
    r = lax.broadcasted_iota(jnp.int32, (rows, 2 * rows), 0)
    c = lax.broadcasted_iota(jnp.int32, (rows, 2 * rows), 1)
    return jnp.where((c == 2 * r) | (c == 2 * r + 1), 0.5, 0.0).astype(BF)


def coarse_levels(x):
    levels = []
    for rows in LEVEL_ROWS:
        x = dot(pool_matrix(rows), x).astype(BF)
        levels.append(x)
    return levels


def spread_matrix(rows):
    t = lax.broadcasted_iota(jnp.int32, (ROWS, rows), 0)
    r = lax.broadcasted_iota(jnp.int32, (ROWS, rows), 1)
    return jnp.where(t // (ROWS // rows) == r, 1.0, 0.0).astype(BF)


def average_matrix(level):
    a = lax.broadcasted_iota(jnp.int32, (ROWS, ROWS), 0)
    b = lax.broadcasted_iota(jnp.int32, (ROWS, ROWS), 1)
    return jnp.where(a // 2**level == b // 2**level, 2.0**-level, 0.0).astype(BF)


def rep2(buf, x):
    rows, cols = x.shape
    buf[pl.ds(0, rows, stride=2), 0:cols] = x
    buf[pl.ds(1, rows, stride=2), 0:cols] = x
    return buf[0 : 2 * rows, 0:cols]


def wide(column):
    return jnp.broadcast_to(column, (column.shape[0], HDIM))


def coarsen_kernel(k_ref, v_ref, o1, o2, o3, o4):
    ks = coarse_levels(k_ref[...])
    vs = coarse_levels(v_ref[...])
    for out, rows, k, v in zip((o1, o2, o3, o4), LEVEL_ROWS, ks, vs):
        out[0:rows, :] = k
        out[rows : 2 * rows, :] = v


def arrange_kernel(at_ref, dout_ref, own_ref, other_ref):
    y, zl, c = at_ref[0], at_ref[1], at_ref[2]
    for n in range(8):
        jy, iz = ORDER[n // 2], n % 2
        base = (y ^ jy) * 4 + (zl ^ iz) * 2
        for ref, core in ((own_ref, c), (other_ref, 1 - c)):
            at = pl.multiple_of((base + core) * 128, 128)
            block = dout_ref[:, pl.ds(at, 128)]
            ref[n * 128 : (n + 1) * 128, :] = block.T


def project_kernel(dout_ref, w_ref, datt_ref):
    datt_ref[...] = dot(dout_ref[...], w_ref[...]).astype(BF)


def local_kernel(q_ref, k_ref, v_ref, a_ref, qx_ref, n_ref, m_ref, l_ref):
    for n, x in enumerate(coarse_levels(q_ref[...])):
        qx_ref[n * ROWS : (n + 1) * ROWS, :] = dot(spread_matrix(x.shape[0]), x).astype(BF)
    for h in range(q_ref.shape[1] // HDIM):
        cols = slice(h * HDIM, (h + 1) * HDIM)
        s = jnp.concatenate(
            [
                dot_nt(q_ref[:, cols], k_ref[:, cols]) * SCALE2,
                dot_nt(qx_ref[0:ROWS, cols], a_ref[0:128, cols]) * SCALE2 + 1.0,
            ],
            axis=1,
        )
        m = jnp.max(s, axis=1, keepdims=True)
        e = jnp.exp2(s - m)
        l_ref[:, cols] = wide(jnp.sum(e, axis=1, keepdims=True))
        m_ref[:, cols] = wide(m)
        v = jnp.concatenate([v_ref[:, cols], a_ref[128:256, cols]], axis=0)
        n_ref[:, cols] = dot(e.astype(BF), v)


def sibling(level, a_ref, u_ref, e_ref, cols):
    if level == 1:
        return a_ref[0:128, cols], a_ref[128:256, cols]
    keys = [ref[at : at + n, cols] for ref in (u_ref, e_ref) for at, n in SPANS[level]]
    vals = [ref[at + n : at + 2 * n, cols] for ref in (u_ref, e_ref) for at, n in SPANS[level]]
    return jnp.concatenate(keys, axis=0), jnp.concatenate(vals, axis=0)


def forward_kernel(qx_ref, u_ref, e_ref, n_ref, m_ref, l_ref, att_ref, lse_ref):
    for h in range(qx_ref.shape[1] // HDIM):
        cols = slice(h * HDIM, (h + 1) * HDIM)
        scores, vals = [], []
        for level in range(2, 5):
            k, v = sibling(level, None, u_ref, e_ref, cols)
            q = qx_ref[(level - 1) * ROWS : level * ROWS, cols]
            scores.append(dot_nt(q, k) * SCALE2 + float(level))
            vals.append(v)
        s = jnp.concatenate(scores, axis=1)
        m0 = m_ref[:, cols]
        top = jnp.maximum(m0, wide(jnp.max(s, axis=1, keepdims=True)))
        e = jnp.exp2(s - jnp.concatenate([top] * 3, axis=1))
        own = jnp.exp2(m0 - top)
        total = own * l_ref[:, cols] + wide(jnp.sum(e, axis=1, keepdims=True))
        num = own * n_ref[:, cols] + dot(e.astype(BF), jnp.concatenate(vals, axis=0))
        att_ref[:, cols] = (num / total).astype(BF)
        lse_ref[:, cols] = top + jnp.log2(total)


def back_kernel(
    q_ref, k_ref, v_ref, qx_ref, a_ref, u_ref, e_ref, datt_ref, att_ref, lse_ref,
    send_ref, keep_ref, dq_ref, gk_ref, gv_ref, avg_ref,
):
    @pl.when(pl.program_id(0) == 0)
    def _():
        for level in range(1, 5):
            avg_ref[(level - 1) * ROWS : level * ROWS, :] = average_matrix(level)

    all_keys, all_ds = [], []
    for h in range(q_ref.shape[1] // HDIM):
        cols = slice(h * HDIM, (h + 1) * HDIM)
        datt = datt_ref[:, cols]
        delta = jnp.sum(datt.astype(F32) * att_ref[:, cols].astype(F32), axis=1, keepdims=True)
        delta = wide(delta).T[0:1, :]
        lse = lse_ref[:, cols].T[0:1, :]
        sides = [sibling(level, a_ref, u_ref, e_ref, cols) for level in range(1, 5)]
        queries = [qx_ref[n * ROWS : (n + 1) * ROWS, cols] for n in range(4)] + [q_ref[:, cols]]
        keys = [k for k, _ in sides] + [k_ref[:, cols]]
        vals = jnp.concatenate([v for _, v in sides] + [v_ref[:, cols]], axis=0)
        scores = [
            dot_nt(k, q) * SCALE2 + bias
            for k, q, bias in zip(keys, queries, (1.0, 2.0, 3.0, 4.0, 0.0))
        ]
        p = jnp.exp2(jnp.concatenate(scores, axis=0) - lse)
        ds = (p * (dot_nt(vals, datt) - delta)).astype(BF)
        gv = dot(p.astype(BF), datt)
        ds = [ds[n * 128 : (n + 1) * 128] for n in range(4)] + [ds[512:768]]
        all_keys.append(jnp.concatenate(keys, axis=0).T)
        all_ds.append(ds)
        for level in range(1, 5):
            gk_l = dot(ds[level - 1], queries[level - 1]) * SCALE
            gv_l = gv[(level - 1) * 128 : level * 128]
            if level == 1:
                send_ref[0:128, cols] = gk_l.astype(BF)
                send_ref[128:256, cols] = gv_l.astype(BF)
            else:
                row = 0
                for ref, off in ((keep_ref, 0), (send_ref, 256)):
                    for start, n in SPANS[level]:
                        to = off + start
                        ref[to : to + n, cols] = gk_l[row : row + n].astype(ref.dtype)
                        ref[to + n : to + 2 * n, cols] = gv_l[row : row + n].astype(ref.dtype)
                        row += n
        gk_ref[:, cols] = dot(ds[4], queries[4]) * SCALE
        gv_ref[:, cols] = gv[512:768]
    means = []
    for n in range(4):
        stacked = jnp.concatenate([ds[n] for ds in all_ds], axis=0)
        means.append(dot(stacked, avg_ref[n * ROWS : (n + 1) * ROWS, :]).astype(BF))
    for h in range(q_ref.shape[1] // HDIM):
        rows = slice(h * 128, (h + 1) * 128)
        ds = jnp.concatenate([m[rows] for m in means] + [all_ds[h][4]], axis=0)
        gq = dot(all_keys[h], ds)
        dq_ref[:, h * HDIM : (h + 1) * HDIM] = (gq.T * SCALE).astype(BF)


def weight_kernel(at_ref, own_ref, other_ref, att_ref, attp_ref, *outs):
    x = at_ref[3]

    def heads(ref, half):
        blocks = []
        for jx in ORDER:
            col = pl.multiple_of(((x ^ jx) * 2 + half) * 128, 128)
            blocks.append(ref[:, pl.ds(col, 128)])
        return jnp.concatenate(blocks, axis=1)

    def term(n, half):
        rows = slice(n * 256, (n + 1) * 256)
        return (dot(own_ref[rows, :], mine[half]) + dot(other_ref[rows, :], theirs[half])).astype(BF)

    mine = [heads(att_ref, half) for half in range(2)]
    theirs = [heads(attp_ref, half) for half in range(2)]
    for n in range(4):
        outs[n][...] = term(n, 0)
        part = term(n, 1)
        for m in range(4):
            outs[4 + m][n * 256 : (n + 1) * 256, :] = part[:, m * 128 : (m + 1) * 128]


def sum_first_kernel(*refs):
    ins, (keep_x, send_x, keep_y, send_y) = refs[:8], refs[8:]
    for n, out in enumerate((keep_x, send_x)):
        cols = slice(n * 256, (n + 1) * 256)
        out[...] = sum(r[:, cols].astype(F32) for r in ins[:4]).astype(out.dtype)
    for n, out in enumerate((keep_y, send_y)):
        rows = slice(n * 512, (n + 1) * 512)
        out[...] = sum(r[rows, :].astype(F32) for r in ins[4:]).astype(out.dtype)


def sum_second_kernel(in_x, got_x, in_y, got_y, keep_x, send_x, keep_y, send_y):
    for n, out in enumerate((keep_x, send_x)):
        cols = slice(n * 128, (n + 1) * 128)
        out[...] = (in_x[:, cols] + got_x[:, cols].astype(F32)).astype(out.dtype)
    for n, out in enumerate((keep_y, send_y)):
        rows = slice(n * 256, (n + 1) * 256)
        out[...] = (in_y[rows, :] + got_y[rows, :].astype(F32)).astype(out.dtype)


def sum_third_kernel(in_x, got_x, in_y, got_y, keep_ref, send_ref):
    for half, (own, got) in enumerate(((in_x, got_x), (in_y, got_y))):
        cols = slice(half * 128, (half + 1) * 128)
        total = own[...] + got[...].astype(F32)
        keep_ref[:, cols] = total[0:128]
        send_ref[:, cols] = total[128:256].astype(BF)


def place_kernel(at_ref, a, b, c, d, out_ref):
    x = at_ref[3]
    for j, ref in enumerate((a, b, c, d)):
        col = pl.multiple_of((x ^ j) * 256, 256)
        out_ref[:, pl.ds(col, 256)] = ref[...].astype(F32)


def finish_kernel(gk_ref, gv_ref, r1, r2, r3, r4, dk_ref, dv_ref, bufs):
    for h in range(gk_ref.shape[1] // HDIM):
        cols = slice(h * HDIM, (h + 1) * HDIM)
        for which, (g0_ref, out_ref) in enumerate(((gk_ref, dk_ref), (gv_ref, dv_ref))):
            g = None
            for ref, rows in ((r4, 16), (r3, 32), (r2, 64), (r1, 128)):
                own = ref[which * rows : (which + 1) * rows, cols].astype(F32)
                g = own if g is None else own + rep2(bufs.at[2 * h + which], 0.5 * g)
            g = g0_ref[:, cols] + rep2(bufs.at[2 * h + which], 0.5 * g)
            out_ref[:, cols] = g.astype(BF)


def shape(rows, cols, dtype=BF):
    return jax.ShapeDtypeStruct((rows, cols), dtype)


SMEM = pl.BlockSpec(memory_space=pltpu.SMEM)


def by_heads(rows, step):
    return pl.BlockSpec((rows, step), lambda i: (0, i))


def whole(rows, cols):
    return pl.BlockSpec((rows, cols), lambda i: (0, 0))


def cost(flops, bytes_accessed):
    return pl.CostEstimate(flops=int(flops), bytes_accessed=int(bytes_accessed), transcendentals=0)


def call(kernel, out, **kw):
    return pl.pallas_call(kernel, out_shape=out, compiler_params=VMEM, **kw)


def per_device(queries, keys, values, d_out, w_out):
    q, k, v, dout = queries[0], keys[0], values[0], d_out[0]
    seq, dp = lax.axis_index("seq"), lax.axis_index("dp")
    place = jnp.stack([seq // 4, seq // 2 % 2, seq % 2, dp % 4]).astype(jnp.int32)
    step = 2 * HDIM
    grid = (WIDTH // step,)
    hs = functools.partial(by_heads, step=step)

    l1, l2, l3, l4 = call(
        coarsen_kernel,
        [shape(2 * rows, WIDTH) for rows in LEVEL_ROWS],
    )(k, v)
    b4 = swap(l4, "seq", Y3)
    c4 = swap(l4, "seq", Y2)
    b3 = swap(l3, "seq", Y1)
    b2 = swap(l2, "seq", ZLO)
    a1 = swap(l1, "seq", CORE)
    qx, n0, m0, l0 = call(
        local_kernel,
        [shape(4 * ROWS, WIDTH)] + [shape(ROWS, WIDTH, F32)] * 3,
        grid=grid,
        in_specs=[hs(ROWS)] * 3 + [hs(256)],
        out_specs=[hs(4 * ROWS)] + [hs(ROWS)] * 3,
        cost_estimate=cost(2.0e9, 10e6),
    )(q, k, v, a1)
    t = jnp.concatenate([b3, c4, b4])
    t, n0 = lax.optimization_barrier((t, n0))
    d = swap(t, "seq", ZLO)
    datt = call(
        project_kernel,
        shape(ROWS, WIDTH),
        grid=grid,
        in_specs=[whole(ROWS, DMODEL), hs(DMODEL)],
        out_specs=hs(ROWS),
        cost_estimate=cost(2.0e9, 10e6),
    )(dout, w_out)
    u = jnp.concatenate([b2, t, d])
    u, datt = lax.optimization_barrier((u, datt))
    e = swap(u, "seq", CORE)
    own_t, other_t = call(
        arrange_kernel,
        [shape(1024, ROWS)] * 2,
        in_specs=[SMEM, pl.BlockSpec(memory_space=pltpu.VMEM)],
    )(place, dout)
    rec_t = swap(other_t, "seq", CORE)
    att, lse = call(
        forward_kernel,
        [shape(ROWS, WIDTH), shape(ROWS, WIDTH, F32)],
        grid=grid,
        in_specs=[hs(4 * ROWS), hs(384), hs(384)] + [hs(ROWS)] * 3,
        out_specs=[hs(ROWS), hs(ROWS)],
        cost_estimate=cost(1.0e9, 8e6),
    )(qx, u, e, n0, m0, l0)

    attp = swap(att, "seq", CORE)
    o = call(
        weight_kernel,
        [shape(256, 512)] * 4 + [shape(1024, 128)] * 4,
        in_specs=[SMEM] + [pl.BlockSpec(memory_space=pltpu.VMEM)] * 4,
        cost_estimate=cost(1.0e9, 4e6),
    )(place, own_t, rec_t, att, attp)
    keep_x, send_x, keep_y, send_y = call(
        sum_first_kernel,
        [shape(256, 256, F32), shape(256, 256), shape(512, 128, F32), shape(512, 128)],
    )(
        o[0], swap(o[1], "seq", Y3), swap(o[2], "seq", Y1), swap(o[3], "seq", Y2),
        o[4], swap(o[5], "dp", X3), swap(o[6], "dp", X1), swap(o[7], "dp", X2),
    )
    send, keep, dq, gk0, gv0 = call(
        back_kernel,
        [shape(640, WIDTH), shape(384, WIDTH, F32), shape(ROWS, WIDTH)]
        + [shape(ROWS, WIDTH, F32)] * 2,
        grid=grid,
        in_specs=[hs(ROWS)] * 3 + [hs(4 * ROWS), hs(256), hs(384), hs(384)] + [hs(ROWS)] * 3,
        out_specs=[hs(640), hs(384)] + [hs(ROWS)] * 3,
        scratch_shapes=[pltpu.VMEM((4 * ROWS, ROWS), BF)],
        cost_estimate=cost(4.0e9, 12e6),
    )(q, k, v, qx, a1, u, e, datt, att, lse)
    send, _ = lax.optimization_barrier((send, send_x))

    rc = swap(send, "seq", CORE)
    s = keep + rc[256:640].astype(F32)
    rz = swap(s[256:384].astype(BF), "seq", ZLO)
    r2 = swap(s[0:128].astype(BF), "seq", ZLO)
    t = s[128:256] + rz.astype(F32)
    ry = swap(t[0:96].astype(BF), "seq", Y1)
    r4 = swap((t[96:128] + ry[64:96].astype(F32)).astype(BF), "seq", Y3)
    dk, dv = call(
        finish_kernel,
        [shape(ROWS, WIDTH)] * 2,
        grid=grid,
        in_specs=[hs(ROWS)] * 2 + [hs(256), hs(128), hs(64), hs(32)],
        out_specs=[hs(ROWS)] * 2,
        scratch_shapes=[pltpu.VMEM((4, ROWS, HDIM), F32)],
    )(gk0, gv0, rc, r2, ry, r4)

    halves = [shape(256, 128, F32), shape(256, 128)] * 2
    keep_x, send_x, keep_y, send_y = call(sum_second_kernel, halves)(
        keep_x, swap(send_x, "dp", X1), keep_y, swap(send_y, "seq", Y1)
    )
    kept, sent = call(sum_third_kernel, [shape(128, 256, F32), shape(128, 256)])(
        keep_x, swap(send_x, "dp", X3), keep_y, swap(send_y, "seq", Y3)
    )
    g = kept + swap(sent, "seq", ZLO).astype(F32)
    for mask in (ZH1, ZH3):
        g = g.astype(BF)
        g = g.astype(F32) + swap(g, "dp", mask).astype(F32)
    g = g.astype(BF)
    dw = call(
        place_kernel,
        shape(128, WIDTH, F32),
        in_specs=[SMEM] + [pl.BlockSpec(memory_space=pltpu.VMEM)] * 4,
    )(place, g, swap(g, "dp", X1), swap(g, "dp", X2), swap(g, "dp", X3))
    return dq[None], dk[None], dv[None], dw


def solution(mesh):
    rows = P("dp", "seq", None)
    return jax.shard_map(
        per_device,
        mesh=mesh,
        in_specs=(rows, rows, rows, rows, P()),
        out_specs=(rows, rows, rows, P("seq", None)),
        check_vma=False,
    )
```

time: 137 us -> 112 us (0.82)
  Pallas kernels: 43.3 us -> 29.5 us
  starting transfers between devices: 48.6 us -> 37 us
  local copies, waits for them, and re-layouts: 6.26 us -> 9.61 us
  waiting for transfers between devices: 35.7 us -> 33.9 us
    pallas_call x6 -> x7, Pallas kernels: 35.5 us -> 22.2 us  [the longest x1 8.49 us: per_device(): call(back_kernel, [shape(640, WIDTH), shape(384, WIDTH, F32), shape(ROWS,...]
    ppermute x32 -> x30, starting transfers between devices: 48.6 us -> 37 us  [swap(): return lax.ppermute(value, axis, pairs)]
    unnamed x26 -> x36, local copies, waits for them, and re-layouts: 6.14 us -> 9.55 us
    ppermute x32 -> x30, waiting for transfers between devices: 35.7 us -> 33.9 us  [swap(): return lax.ppermute(value, axis, pairs)]
  transfers between devices with their start and end apart: 32 -> 30, of which waited for: 12 -> 15; matrix products, arithmetic and copies ran while one was open for 0% -> 1% of each run, Pallas kernels for 29% -> 22%
where the time goes in v2:
time: 112 us
  starting transfers between devices  37 us (33%)
  waiting for transfers between devices  33.9 us (30%)
  Pallas kernels  29.5 us (26%)
  local copies, waits for them, and re-layouts  9.61 us (9%)
    ppermute x30, starting transfers between devices, swap(): return lax.ppermute(value, axis, pairs)  37 us
    ppermute x30, waiting for transfers between devices, swap(): return lax.ppermute(value, axis, pairs)  33.9 us
    unnamed x36, local copies, waits for them, and re-layouts  9.55 us
    pallas_call x1, Pallas kernels, per_device(): call(back_kernel, [shape(640, WIDTH), shape(384, WIDTH, F32), shape(ROWS,...  8.49 us
    pallas_call x1, Pallas kernels, per_device(): call(local_kernel, [shape(4 * ROWS, WIDTH)] + [shape(ROWS, WIDTH, F32)] *...  6.19 us
    pallas_call x1, Pallas kernels, per_device(): call(forward_kernel, [shape(ROWS, WIDTH), shape(ROWS, WIDTH, F32)], grid=...  4.76 us
    pallas_call x1, Pallas kernels, per_device(): call(project_kernel, shape(ROWS, WIDTH), grid=grid, in_specs=[whole(ROWS,...  2.44 us
  transfers between devices with their start and end apart: 30, of which 15 were waited for; matrix products, arithmetic and copies ran while one was open for 1% of the time, Pallas kernels for 22%

profile of v2, /device:TPU:32, one launch (start us, length us, event | category | flops | bytes accessed | tf_op | source)
XLA Modules:
  0.0 111.6 jit_solution(16907666681791393214)
XLA Ops:
  0.6 1.0 copy-done.8
  1.7 1.0 copy-done.10
  2.7 1.1 shard_map.84
  3.8 1.7 %collective-permute-start.2 = (bf16[64,1024]{1,0:T(8,128)(2,1)S(1)}, bf16[64,1024]{1,0:T(8,128)(2,1)S(1)}, u32[]{:S(2)}, u32[]{:S(2)}) collective-permute-start(bf16[64,1024]{1,0:T(8,128)(2,1)S(1)} %get-tuple-element.49), channel_id=1, source_target_pairs={{0,4},{1,5},{2,6},{3,7},{4,0},{5,1},{6,2},{7,3},{8,12},{9,13},{10,... | collective-permute-start | bytes 393224 | tf_op jit(solution)/shard_map/ppermute | solution.py:31
  5.5 2.2 %collective-permute-start.4 = (bf16[32,1024]{1,0:T(8,128)(2,1)S(1)}, bf16[32,1024]{1,0:T(8,128)(2,1)S(1)}, u32[]{:S(2)}, u32[]{:S(2)}) collective-permute-start(bf16[32,1024]{1,0:T(8,128)(2,1)S(1)} %get-tuple-element.50), channel_id=1, source_target_pairs={{0,12},{1,13},{2,14},{3,15},{4,8},{5,9},{6,10},{7,11},{8,4},{9,5},... | collective-permute-start | bytes 196616 | tf_op jit(solution)/shard_map/ppermute | solution.py:31
  7.7 0.7 collective-permute-start.3
  8.4 1.5 %collective-permute-start.1 = (bf16[128,1024]{1,0:T(8,128)(2,1)S(1)}, bf16[128,1024]{1,0:T(8,128)(2,1)S(1)}, u32[]{:S(2)}, u32[]{:S(2)}) collective-permute-start(bf16[128,1024]{1,0:T(8,128)(2,1)S(1)} %get-tuple-element.48), channel_id=1, source_target_pairs={{0,2},{1,3},{2,0},{3,1},{4,6},{5,7},{6,4},{7,5},{8,10},{9,11},{10,... | collective-permute-start | bytes 786440 | tf_op jit(solution)/shard_map/ppermute | solution.py:31
  9.9 1.1 collective-permute-done.4
  11.0 2.6 %collective-permute-done.3 = bf16[32,1024]{1,0:T(8,128)(2,1)S(1)} collective-permute-done((bf16[32,1024]{1,0:T(8,128)(2,1)S(1)}, bf16[32,1024]{1,0:T(8,128)(2,1)S(1)}, u32[]{:S(2)}, u32[]{:S(2)}) %collective-permute-start.3) | collective-permute-done | bytes 65568 | tf_op jit(solution)/shard_map/ppermute | solution.py:31
  13.7 6.2 %shard_map.85 = (bf16[1024,1024]{1,0:T(8,128)(2,1)S(1)}, f32[256,1024]{1,0:T(8,128)S(1)}, f32[256,1024]{1,0:T(8,128)S(1)}, f32[256,1024]{1,0:T(8,128)S(1)}) custom-call(bf16[256,1024]{1,0:T(8,128)(2,1)S(1)} %bitcast.19, bf16[256,1024]{1,0:T(8,128)(2,1)S(1)} %bitcast.14, bf16[256,1024]{1,0:T(8,128)(2,1)S(1)} %bitcast.17, ...), custom_call_target="tpu_custom_call" | custom-call | flops 2000000000 | bytes 10000000 | tf_op jit(solution)/shard_map/pallas_call | solution.py:320
  19.9 1.0 copy-done.2
  20.9 1.0 copy-done.4
  21.9 1.0 copy-done.6
  22.9 0.1 collective-permute-start.5
  23.0 2.4 %shard_map.86.datt_ref = bf16[256,1024]{1,0:T(8,128)(2,1)S(1)} custom-call(bf16[256,2048]{1,0:T(8,128)(2,1)S(1)} %bitcast.11, bf16[2048,1024]{1,0:T(8,128)(2,1)S(1)} %copy-done.12), custom_call_target="tpu_custom_call" | custom-call | flops 2000000000 | bytes 10000000 | tf_op jit(solution)/shard_map/pallas_call | solution.py:331
  25.5 0.8 copy-done.16
  26.3 4.4 %collective-permute-done.5 = bf16[128,1024]{1,0:T(8,128)(2,1)S(1)} collective-permute-done((bf16[128,1024]{1,0:T(8,128)(2,1)S(1)}, bf16[128,1024]{1,0:T(8,128)(2,1)S(1)}, u32[]{:S(2)}, u32[]{:S(2)}) %collective-permute-start.5) | collective-permute-done | bytes 262176 | tf_op jit(solution)/shard_map/ppermute | solution.py:31
  30.7 0.1 collective-permute-start.6
  30.8 0.1 pad_add_fusion.at_ref
  30.9 1.2 %copy-done.1 = bf16[1,256,2048]{2,1,0:T(8,128)(2,1)S(1)} copy-done((bf16[1,256,2048]{2,1,0:T(8,128)(2,1)S(1)}, bf16[1,256,2048]{2,1,0:T(8,128)(2,1)}, u32[]{:S(2)}) %copy-start.1) | copy-done | bytes 1048600
  32.1 0.9 shard_map.89
  33.0 0.5 collective-permute-start.7
  33.5 1.2 %copy-done.5 = f32[256,1024]{1,0:T(8,128)S(1)} copy-done((f32[256,1024]{1,0:T(8,128)S(1)}, f32[256,1024]{1,0:T(8,128)}, u32[]{:S(2)}) %copy-start.5) | copy-done | bytes 1048600
  34.8 1.2 %copy-done.7 = f32[256,1024]{1,0:T(8,128)S(1)} copy-done((f32[256,1024]{1,0:T(8,128)S(1)}, f32[256,1024]{1,0:T(8,128)}, u32[]{:S(2)}) %copy-start.7) | copy-done | bytes 1048600
  36.0 4.8 %shard_map.87 = (bf16[256,1024]{1,0:T(8,128)(2,1)S(1)}, f32[256,1024]{1,0:T(8,128)S(1)}) custom-call(bf16[1024,1024]{1,0:T(8,128)(2,1)S(1)} %get-tuple-element.47.qx_ref, bf16[384,1024]{1,0:T(8,128)(2,1)S(1)} %pad_maximum_fusion.u_ref, bf16[384,1024]{1,0:T(8,128)(2,1)} %collective-permute-done.6.e_ref, f32[256,1024]{1,0:T(8,128)S(1)} %copy-done.3, ...), custom_call_target="tpu_custom_call" | custom-call | flops 1000000000 | bytes 8000000 | tf_op jit(solution)/shard_map/pallas_call | solution.py:348
  40.8 0.3 collective-permute-start.8
  41.1 1.7 %collective-permute-done.8.attp_ref = bf16[256,1024]{1,0:T(8,128)(2,1)S(1)} collective-permute-done((bf16[256,1024]{1,0:T(8,128)(2,1)S(1)}, bf16[256,1024]{1,0:T(8,128)(2,1)S(1)}, u32[]{:S(2)}, u32[]{:S(2)}) %collective-permute-start.8) | collective-permute-done | bytes 524320 | tf_op jit(solution)/shard_map/ppermute | solution.py:31
  42.8 1.9 %shard_map.90 = (bf16[256,512]{1,0:T(8,128)(2,1)S(1)}, bf16[256,512]{1,0:T(8,128)(2,1)S(1)}, bf16[256,512]{1,0:T(8,128)(2,1)S(1)}, bf16[256,512]{1,0:T(8,128)(2,...) custom-call(s32[4]{0:T(128)S(1)} %pad_add_fusion.at_ref, ...), custom_call_target="tpu_custom_call" | custom-call | flops 1000000000 | bytes 4000000 | tf_op jit(solution)/shard_map/pallas_call | solution.py:358
  44.7 0.6 collective-permute-start.9
  45.3 0.1 collective-permute-start.10
  45.4 4.1 %collective-permute-start.11 = (bf16[256,512]{1,0:T(8,128)(2,1)S(1)}, bf16[256,512]{1,0:T(8,128)(2,1)S(1)}, u32[]{:S(2)}, u32[]{:S(2)}) collective-permute-start(bf16[256,512]{1,0:T(8,128)(2,1)S(1)} %get-tuple-element.69), channel_id=1, source_target_pairs={{0,8},{1,9},{2,10},{3,11},{4,12},{5,13},{6,14},{7,15},{8,0},{9,1},... | collective-permute-start | bytes 786440 | tf_op jit(solution)/shard_map/ppermute | solution.py:31
  49.5 2.8 %collective-permute-start.12 = (bf16[1024,128]{1,0:T(8,128)(2,1)S(1)}, bf16[1024,128]{1,0:T(8,128)(2,1)S(1)}, u32[]{:S(2)}, u32[]{:S(2)}) collective-permute-start(bf16[1024,128]{1,0:T(8,128)(2,1)S(1)} %get-tuple-element.71), channel_id=1, source_target_pairs={{0,48},{16,32},{32,16},{48,0},{64,112},{80,96},{96,80},{112,64},{1... | collective-permute-start | bytes 786440 | tf_op jit(solution)/shard_map/ppermute | solution.py:31
  52.3 0.2 collective-permute-start.13
  52.5 2.0 %collective-permute-done.9.refs_1_ = bf16[256,512]{1,0:T(8,128)(2,1)S(1)} collective-permute-done((bf16[256,512]{1,0:T(8,128)(2,1)S(1)}, bf16[256,512]{1,0:T(8,128)(2,1)S(1)}, u32[]{:S(2)}, u32[]{:S(2)}) %collective-permute-start.9) | collective-permute-done | bytes 262176 | tf_op jit(solution)/shard_map/ppermute | solution.py:31
  54.5 3.0 %collective-permute-start.14 = (bf16[1024,128]{1,0:T(8,128)(2,1)S(1)}, bf16[1024,128]{1,0:T(8,128)(2,1)S(1)}, u32[]{:S(2)}, u32[]{:S(2)}) collective-permute-start(bf16[1024,128]{1,0:T(8,128)(2,1)S(1)} %get-tuple-element.73), channel_id=1, source_target_pairs={{0,32},{16,48},{32,0},{48,16},{64,96},{80,112},{96,64},{112,80},{1... | collective-permute-start | bytes 786440 | tf_op jit(solution)/shard_map/ppermute | solution.py:31
  57.5 8.5 %shard_map.88 = (bf16[640,1024]{1,0:T(8,128)(2,1)S(1)}, f32[384,1024]{1,0:T(8,128)S(1)}, bf16[256,1024]{1,0:T(8,128)(2,1)}, f32[256,1024]{1,0:T(8,128)S(1)}, f32[256,1024]{1,0:T(8,128)S(1)}) custom-call(bf16[256,1024]{1,0:T(8,128)(2,1)S(1)} %bitcast.20, bf16[256,1024]{1,0:T(8,128)(2,1)S(1)} %bitcast.15, bf16[256,1024]{1,0:T(8,128)(2,1)S(1)} %bitcast.18, ...), custom_call_target="tpu_custom_call" | custom-call | flops 4000000000 | bytes 12000000 | tf_op jit(solution)/shard_map/pallas_call | solution.py:371
  66.0 0.3 shard_map.91
  66.3 0.1 collective-permute-start.15
  66.4 0.7 collective-permute-start.20
  67.1 5.2 %collective-permute-done.20.got_x = bf16[256,256]{1,0:T(8,128)(2,1)S(1)} collective-permute-done((bf16[256,256]{1,0:T(8,128)(2,1)S(1)}, bf16[256,256]{1,0:T(8,128)(2,1)S(1)}, u32[]{:S(2)}, u32[]{:S(2)}) %collective-permute-start.20) | collective-permute-done | bytes 131104 | tf_op jit(solution)/shard_map/ppermute | solution.py:31
  72.3 0.3 collective-permute-done.21.got_y
  72.7 1.6 %collective-permute-start.22 = (bf16[256,128]{1,0:T(8,128)(2,1)S(1)}, bf16[256,128]{1,0:T(8,128)(2,1)S(1)}, u32[]{:S(2)}, u32[]{:S(2)}) collective-permute-start(bf16[256,128]{1,0:T(8,128)(2,1)S(1)} %get-tuple-element.83), channel_id=1, source_target_pairs={{0,48},{16,32},{32,16},{48,0},{64,112},{80,96},{96,80},{112,64},{1... | collective-permute-start | bytes 196616 | tf_op jit(solution)/shard_map/ppermute | solution.py:31
  74.3 0.4 collective-permute-start.23
  74.7 3.6 %collective-permute-done.22.got_x = bf16[256,128]{1,0:T(8,128)(2,1)S(1)} collective-permute-done((bf16[256,128]{1,0:T(8,128)(2,1)S(1)}, bf16[256,128]{1,0:T(8,128)(2,1)S(1)}, u32[]{:S(2)}, u32[]{:S(2)}) %collective-permute-start.22) | collective-permute-done | bytes 65568 | tf_op jit(solution)/shard_map/ppermute | solution.py:31
  78.3 1.5 %collective-permute-done.23.got_y = bf16[256,128]{1,0:T(8,128)(2,1)S(1)} collective-permute-done((bf16[256,128]{1,0:T(8,128)(2,1)S(1)}, bf16[256,128]{1,0:T(8,128)(2,1)S(1)}, u32[]{:S(2)}, u32[]{:S(2)}) %collective-permute-start.23) | collective-permute-done | bytes 65568 | tf_op jit(solution)/shard_map/ppermute | solution.py:31
  79.8 0.4 collective-permute-start.24
  80.2 4.0 %collective-permute-done.24 = bf16[128,256]{1,0:T(8,128)(2,1)S(1)} collective-permute-done((bf16[128,256]{1,0:T(8,128)(2,1)S(1)}, bf16[128,256]{1,0:T(8,128)(2,1)S(1)}, u32[]{:S(2)}, u32[]{:S(2)}) %collective-permute-start.24) | collective-permute-done | bytes 65568 | tf_op jit(solution)/shard_map/ppermute | solution.py:31
  84.2 3.4 %collective-permute-start.25 = (bf16[128,256]{1,0:T(8,128)(2,1)S(1)}, bf16[128,256]{1,0:T(8,128)(2,1)S(1)}, u32[]{:S(2)}, u32[]{:S(2)}) collective-permute-start(bf16[128,256]{1,0:T(8,128)(2,1)S(1)} %add_convert_fusion.2), channel_id=1, source_target_pairs={{0,64},{16,80},{32,96},{48,112},{64,0},{80,16},{96,32},{112,48},{1... | collective-permute-start | bytes 196616 | tf_op jit(solution)/shard_map/ppermute | solution.py:31
  87.6 0.3 fusion.1
  87.9 0.4 collective-permute-start.17
  88.3 1.7 %collective-permute-done.25 = bf16[128,256]{1,0:T(8,128)(2,1)S(1)} collective-permute-done((bf16[128,256]{1,0:T(8,128)(2,1)S(1)}, bf16[128,256]{1,0:T(8,128)(2,1)S(1)}, u32[]{:S(2)}, u32[]{:S(2)}) %collective-permute-start.25) | collective-permute-done | bytes 65568 | tf_op jit(solution)/shard_map/ppermute | solution.py:31
  90.0 5.1 %collective-permute-start.26 = (bf16[128,256]{1,0:T(8,128)(2,1)S(1)}, bf16[128,256]{1,0:T(8,128)(2,1)S(1)}, u32[]{:S(2)}, u32[]{:S(2)}) collective-permute-start(bf16[128,256]{1,0:T(8,128)(2,1)S(1)} %add_convert_fusion.1), channel_id=1, source_target_pairs={{0,192},{16,208},{32,224},{48,240},{64,128},{80,144},{96,160},{112... | collective-permute-start | bytes 196616 | tf_op jit(solution)/shard_map/ppermute | solution.py:31
  95.2 0.1 collective-permute-start.18
  95.3 2.0 %collective-permute-done.26 = bf16[128,256]{1,0:T(8,128)(2,1)S(1)} collective-permute-done((bf16[128,256]{1,0:T(8,128)(2,1)S(1)}, bf16[128,256]{1,0:T(8,128)(2,1)S(1)}, u32[]{:S(2)}, u32[]{:S(2)}) %collective-permute-start.26) | collective-permute-done | bytes 65568 | tf_op jit(solution)/shard_map/ppermute | solution.py:31
  97.4 1.1 %collective-permute-start.27 = (bf16[128,256]{1,0:T(8,128)(2,1)S(1)}, bf16[128,256]{1,0:T(8,128)(2,1)S(1)}, u32[]{:S(2)}, u32[]{:S(2)}) collective-permute-start(bf16[128,256]{1,0:T(8,128)(2,1)S(1)} %add_convert_fusion.a), channel_id=1, source_target_pairs={{0,16},{16,0},{32,48},{48,32},{64,80},{80,64},{96,112},{112,96},{1... | collective-permute-start | bytes 196616 | tf_op jit(solution)/shard_map/ppermute | solution.py:31
  98.5 3.4 %collective-permute-start.28 = (bf16[128,256]{1,0:T(8,128)(2,1)S(1)}, bf16[128,256]{1,0:T(8,128)(2,1)S(1)}, u32[]{:S(2)}, u32[]{:S(2)}) collective-permute-start(bf16[128,256]{1,0:T(8,128)(2,1)S(1)} %add_convert_fusion.a), channel_id=1, source_target_pairs={{0,32},{16,48},{32,0},{48,16},{64,96},{80,112},{96,64},{112,80},{1... | collective-permute-start | bytes 196616 | tf_op jit(solution)/shard_map/ppermute | solution.py:31
  102.0 0.2 collective-permute-start.29
  102.2 1.7 %collective-permute-start.16 = (bf16[128,1024]{1,0:T(8,128)(2,1)S(1)}, bf16[128,1024]{1,0:T(8,128)(2,1)S(1)}, u32[]{:S(2)}, u32[]{:S(2)}) collective-permute-start(bf16[128,1024]{1,0:T(8,128)(2,1)S(1)} %get-tuple-element.91), channel_id=1, source_target_pairs={{0,2},{1,3},{2,0},{3,1},{4,6},{5,7},{6,4},{7,5},{8,10},{9,11},{10,... | collective-permute-start | bytes 786440 | tf_op jit(solution)/shard_map/ppermute | solution.py:31
  104.0 0.4 collective-permute-start.19
  104.4 0.5 collective-permute-done.28.c
  104.9 2.5 %collective-permute-done.29.d = bf16[128,256]{1,0:T(8,128)(2,1)S(1)} collective-permute-done((bf16[128,256]{1,0:T(8,128)(2,1)S(1)}, bf16[128,256]{1,0:T(8,128)(2,1)S(1)}, u32[]{:S(2)}, u32[]{:S(2)}) %collective-permute-start.29) | collective-permute-done | bytes 65568 | tf_op jit(solution)/shard_map/ppermute | solution.py:31
  107.4 1.4 %shard_map.95 = f32[128,1024]{1,0:T(8,128)} custom-call(s32[4]{0:T(128)S(1)} %pad_add_fusion.at_ref, bf16[128,256]{1,0:T(8,128)(2,1)S(1)} %add_convert_fusion.a, bf16[128,256]{1,0:T(8,128)(2,1)S(1)} %collective-permute-done.27.b, bf16[128,256]{1,0:T(8,128)(2,1)S(1)} %collective-permute-done.28.c, bf16[128,256]{1,0:T(8,128)(2,1)S(1)} %collective-permute-done.29.d), custom_call_target="tpu_custom_call" | custom-call | tf_op jit(solution)/shard_map/pallas_call | solution.py:411
  108.8 0.7 collective-permute-done.19.r4
  109.5 2.1 %shard_map.92 = (bf16[256,1024]{1,0:T(8,128)(2,1)}, bf16[256,1024]{1,0:T(8,128)(2,1)}) custom-call(f32[256,1024]{1,0:T(8,128)S(1)} %get-tuple-element.61.gk_ref, f32[256,1024]{1,0:T(8,128)S(1)} %get-tuple-element.62.gv_ref, bf16[640,1024]{1,0:T(8,128)(2,1)S(1)} %collective-permute-done.15.r1, bf16[128,1024]{1,0:T(8,128)(2,1)S(1)} %collective-permute-done.16.r2, ...), custom_call_target="tpu_custom_call" | custom-call | tf_op jit(solution)/shard_map/pallas_call | solution.py:390
  (55 shorter events, 0.4 us)
Async XLA Ops:
  0.6 1.0 copy-start.8
  1.7 1.0 copy-start.10
  2.7 11.0 %copy-start.13 = (bf16[1,256,1024]{2,1,0:T(8,128)(2,1)S(1)}, bf16[1,256,1024]{2,1,0:T(8,128)(2,1)}, u32[]{:S(2)}) copy-start(bf16[1,256,1024]{2,1,0:T(8,128)(2,1)} %param.5) | copy-start | bytes 1572868
  3.8 9.8 %collective-permute-start = (bf16[256,1024]{1,0:T(8,128)(2,1)S(1)}, bf16[256,1024]{1,0:T(8,128)(2,1)S(1)}, u32[]{:S(2)}, u32[]{:S(2)}) collective-permute-start(bf16[256,1024]{1,0:T(8,128)(2,1)S(1)} %get-tuple-element.46), channel_id=1, source_target_pairs={{0,1},{1,0},{2,3},{3,2},{4,5},{5,4},{6,7},{7,6},{8,9},{9,8},{10,11... | collective-permute-start | bytes 1572872 | tf_op jit(solution)/shard_map/ppermute | solution.py:31
  3.8 9.8 %collective-permute-start.2 = (bf16[64,1024]{1,0:T(8,128)(2,1)S(1)}, bf16[64,1024]{1,0:T(8,128)(2,1)S(1)}, u32[]{:S(2)}, u32[]{:S(2)}) collective-permute-start(bf16[64,1024]{1,0:T(8,128)(2,1)S(1)} %get-tuple-element.49), channel_id=1, source_target_pairs={{0,4},{1,5},{2,6},{3,7},{4,0},{5,1},{6,2},{7,3},{8,12},{9,13},{10,... | collective-permute-start | bytes 393224 | tf_op jit(solution)/shard_map/ppermute | solution.py:31
  5.5 5.5 %collective-permute-start.4 = (bf16[32,1024]{1,0:T(8,128)(2,1)S(1)}, bf16[32,1024]{1,0:T(8,128)(2,1)S(1)}, u32[]{:S(2)}, u32[]{:S(2)}) collective-permute-start(bf16[32,1024]{1,0:T(8,128)(2,1)S(1)} %get-tuple-element.50), channel_id=1, source_target_pairs={{0,12},{1,13},{2,14},{3,15},{4,8},{5,9},{6,10},{7,11},{8,4},{9,5},... | collective-permute-start | bytes 196616 | tf_op jit(solution)/shard_map/ppermute | solution.py:31
  7.7 5.9 %collective-permute-start.3 = (bf16[32,1024]{1,0:T(8,128)(2,1)S(1)}, bf16[32,1024]{1,0:T(8,128)(2,1)S(1)}, u32[]{:S(2)}, u32[]{:S(2)}) collective-permute-start(bf16[32,1024]{1,0:T(8,128)(2,1)S(1)} %get-tuple-element.50), channel_id=1, source_target_pairs={{0,8},{1,9},{2,10},{3,11},{4,12},{5,13},{6,14},{7,15},{8,0},{9,1},... | collective-permute-start | bytes 196616 | tf_op jit(solution)/shard_map/ppermute | solution.py:31
  8.4 17.9 %collective-permute-start.1 = (bf16[128,1024]{1,0:T(8,128)(2,1)S(1)}, bf16[128,1024]{1,0:T(8,128)(2,1)S(1)}, u32[]{:S(2)}, u32[]{:S(2)}) collective-permute-start(bf16[128,1024]{1,0:T(8,128)(2,1)S(1)} %get-tuple-element.48), channel_id=1, source_target_pairs={{0,2},{1,3},{2,0},{3,1},{4,6},{5,7},{6,4},{7,5},{8,10},{9,11},{10,... | collective-permute-start | bytes 786440 | tf_op jit(solution)/shard_map/ppermute | solution.py:31
  13.7 6.2 %copy-start.14 = (bf16[256,1024]{1,0:T(8,128)(2,1)}, bf16[256,1024]{1,0:T(8,128)(2,1)S(1)}, u32[]{:S(2)}) copy-start(bf16[256,1024]{1,0:T(8,128)(2,1)S(1)} %collective-permute-done.a_ref) | copy-start | bytes 1572868
  13.7 9.3 %copy-start = (bf16[1,256,2048]{2,1,0:T(8,128)(2,1)S(1)}, bf16[1,256,2048]{2,1,0:T(8,128)(2,1)}, u32[]{:S(2)}) copy-start(bf16[1,256,2048]{2,1,0:T(8,128)(2,1)} %param.8) | copy-start | bytes 3145732
  13.7 9.3 %copy-start.12 = (bf16[2048,1024]{1,0:T(8,128)(2,1)S(1)}, bf16[2048,1024]{1,0:T(8,128)(2,1)}, u32[]{:S(2)}) copy-start(bf16[2048,1024]{1,0:T(8,128)(2,1)} %w_ref.1) | copy-start | bytes 12582916
  19.9 1.0 copy-start.2
  20.9 1.0 copy-start.4
  21.9 1.0 copy-start.6
  22.9 7.7 %collective-permute-start.5 = (bf16[128,1024]{1,0:T(8,128)(2,1)S(1)}, bf16[128,1024]{1,0:T(8,128)(2,1)S(1)}, u32[]{:S(2)}, u32[]{:S(2)}) collective-permute-start(bf16[128,1024]{1,0:T(8,128)(2,1)S(1)} %pad_maximum_fusion.1), channel_id=1, source_target_pairs={{0,2},{1,3},{2,0},{3,1},{4,6},{5,7},{6,4},{7,5},{8,10},{9,11},{10,... | collective-permute-start | bytes 786440 | tf_op jit(solution)/shard_map/ppermute | solution.py:31
  25.5 0.8 copy-start.16
  30.7 2.9 %collective-permute-start.6 = (bf16[384,1024]{1,0:T(8,128)(2,1)S(1)}, bf16[384,1024]{1,0:T(8,128)(2,1)}, u32[]{:S(2)}, u32[]{:S(2)}) collective-permute-start(bf16[384,1024]{1,0:T(8,128)(2,1)S(1)} %pad_maximum_fusion.u_ref), channel_id=1, source_target_pairs={{0,1},{1,0},{2,3},{3,2},{4,5},{5,4},{6,7},{7,6},{8,9},{9,8},{10,11... | collective-permute-start | bytes 2359304 | tf_op jit(solution)/shard_map/ppermute | solution.py:31
  30.9 1.2 %copy-start.1 = (bf16[1,256,2048]{2,1,0:T(8,128)(2,1)S(1)}, bf16[1,256,2048]{2,1,0:T(8,128)(2,1)}, u32[]{:S(2)}) copy-start(bf16[1,256,2048]{2,1,0:T(8,128)(2,1)} %param.8) | copy-start | bytes 3145732
  32.1 1.4 %copy-start.3 = (f32[256,1024]{1,0:T(8,128)S(1)}, f32[256,1024]{1,0:T(8,128)}, u32[]{:S(2)}) copy-start(f32[256,1024]{1,0:T(8,128)} %copy-done.2) | copy-start | bytes 3145732
  33.0 8.1 %collective-permute-start.7 = (bf16[1024,256]{1,0:T(8,128)(2,1)S(1)}, bf16[1024,256]{1,0:T(8,128)(2,1)S(1)}, u32[]{:S(2)}, u32[]{:S(2)}) collective-permute-start(bf16[1024,256]{1,0:T(8,128)(2,1)S(1)} %get-tuple-element.65), channel_id=1, source_target_pairs={{0,1},{1,0},{2,3},{3,2},{4,5},{5,4},{6,7},{7,6},{8,9},{9,8},{10,11... | collective-permute-start | bytes 1572872 | tf_op jit(solution)/shard_map/ppermute | solution.py:31
  33.5 1.2 %copy-start.5 = (f32[256,1024]{1,0:T(8,128)S(1)}, f32[256,1024]{1,0:T(8,128)}, u32[]{:S(2)}) copy-start(f32[256,1024]{1,0:T(8,128)} %copy-done.4) | copy-start | bytes 3145732
  34.8 1.2 %copy-start.7 = (f32[256,1024]{1,0:T(8,128)S(1)}, f32[256,1024]{1,0:T(8,128)}, u32[]{:S(2)}) copy-start(f32[256,1024]{1,0:T(8,128)} %copy-done.6) | copy-start | bytes 3145732
  40.8 2.0 %collective-permute-start.8 = (bf16[256,1024]{1,0:T(8,128)(2,1)S(1)}, bf16[256,1024]{1,0:T(8,128)(2,1)S(1)}, u32[]{:S(2)}, u32[]{:S(2)}) collective-permute-start(bf16[256,1024]{1,0:T(8,128)(2,1)S(1)} %get-tuple-element.58.att_ref), channel_id=1, source_target_pairs={{0,1},{1,0},{2,3},{3,2},{4,5},{5,4},{6,7},{7,6},{8,9},{9,8},{10,11... | collective-permute-start | bytes 1572872 | tf_op jit(solution)/shard_map/ppermute | solution.py:31
  42.8 14.7 %copy-start.9 = (bf16[1,256,1024]{2,1,0:T(8,128)(2,1)S(1)}, bf16[1,256,1024]{2,1,0:T(8,128)(2,1)}, u32[]{:S(2)}) copy-start(bf16[1,256,1024]{2,1,0:T(8,128)(2,1)} %param.6) | copy-start | bytes 1572868
  42.8 14.7 %copy-start.11 = (bf16[1,256,1024]{2,1,0:T(8,128)(2,1)S(1)}, bf16[1,256,1024]{2,1,0:T(8,128)(2,1)}, u32[]{:S(2)}) copy-start(bf16[1,256,1024]{2,1,0:T(8,128)(2,1)} %param.7) | copy-start | bytes 1572868
  42.8 14.7 %copy-start.15 = (bf16[256,1024]{1,0:T(8,128)(2,1)S(1)}, bf16[256,1024]{1,0:T(8,128)(2,1)}, u32[]{:S(2)}) copy-start(bf16[256,1024]{1,0:T(8,128)(2,1)} %copy-done.14) | copy-start | bytes 1572868
  42.8 14.7 %copy-start.17 = (bf16[256,1024]{1,0:T(8,128)(2,1)S(1)}, bf16[256,1024]{1,0:T(8,128)(2,1)}, u32[]{:S(2)}) copy-start(bf16[256,1024]{1,0:T(8,128)(2,1)} %copy-done.16) | copy-start | bytes 1572868
  44.7 9.8 %collective-permute-start.9 = (bf16[256,512]{1,0:T(8,128)(2,1)S(1)}, bf16[256,512]{1,0:T(8,128)(2,1)S(1)}, u32[]{:S(2)}, u32[]{:S(2)}) collective-permute-start(bf16[256,512]{1,0:T(8,128)(2,1)S(1)} %get-tuple-element.67), channel_id=1, source_target_pairs={{0,12},{1,13},{2,14},{3,15},{4,8},{5,9},{6,10},{7,11},{8,4},{9,5},... | collective-permute-start | bytes 786440 | tf_op jit(solution)/shard_map/ppermute | solution.py:31
  45.3 20.7 %collective-permute-start.10 = (bf16[256,512]{1,0:T(8,128)(2,1)S(1)}, bf16[256,512]{1,0:T(8,128)(2,1)S(1)}, u32[]{:S(2)}, u32[]{:S(2)}) collective-permute-start(bf16[256,512]{1,0:T(8,128)(2,1)S(1)} %get-tuple-element.68), channel_id=1, source_target_pairs={{0,4},{1,5},{2,6},{3,7},{4,0},{5,1},{6,2},{7,3},{8,12},{9,13},{10,... | collective-permute-start | bytes 786440 | tf_op jit(solution)/shard_map/ppermute | solution.py:31
  45.4 20.6 %collective-permute-start.11 = (bf16[256,512]{1,0:T(8,128)(2,1)S(1)}, bf16[256,512]{1,0:T(8,128)(2,1)S(1)}, u32[]{:S(2)}, u32[]{:S(2)}) collective-permute-start(bf16[256,512]{1,0:T(8,128)(2,1)S(1)} %get-tuple-element.69), channel_id=1, source_target_pairs={{0,8},{1,9},{2,10},{3,11},{4,12},{5,13},{6,14},{7,15},{8,0},{9,1},... | collective-permute-start | bytes 786440 | tf_op jit(solution)/shard_map/ppermute | solution.py:31
  49.5 16.5 %collective-permute-start.12 = (bf16[1024,128]{1,0:T(8,128)(2,1)S(1)}, bf16[1024,128]{1,0:T(8,128)(2,1)S(1)}, u32[]{:S(2)}, u32[]{:S(2)}) collective-permute-start(bf16[1024,128]{1,0:T(8,128)(2,1)S(1)} %get-tuple-element.71), channel_id=1, source_target_pairs={{0,48},{16,32},{32,16},{48,0},{64,112},{80,96},{96,80},{112,64},{1... | collective-permute-start | bytes 786440 | tf_op jit(solution)/shard_map/ppermute | solution.py:31
  52.3 13.8 %collective-permute-start.13 = (bf16[1024,128]{1,0:T(8,128)(2,1)S(1)}, bf16[1024,128]{1,0:T(8,128)(2,1)S(1)}, u32[]{:S(2)}, u32[]{:S(2)}) collective-permute-start(bf16[1024,128]{1,0:T(8,128)(2,1)S(1)} %get-tuple-element.72), channel_id=1, source_target_pairs={{0,16},{16,0},{32,48},{48,32},{64,80},{80,64},{96,112},{112,96},{1... | collective-permute-start | bytes 786440 | tf_op jit(solution)/shard_map/ppermute | solution.py:31
  54.5 11.6 %collective-permute-start.14 = (bf16[1024,128]{1,0:T(8,128)(2,1)S(1)}, bf16[1024,128]{1,0:T(8,128)(2,1)S(1)}, u32[]{:S(2)}, u32[]{:S(2)}) collective-permute-start(bf16[1024,128]{1,0:T(8,128)(2,1)S(1)} %get-tuple-element.73), channel_id=1, source_target_pairs={{0,32},{16,48},{32,0},{48,16},{64,96},{80,112},{96,64},{112,80},{1... | collective-permute-start | bytes 786440 | tf_op jit(solution)/shard_map/ppermute | solution.py:31
  66.3 21.3 %collective-permute-start.15 = (bf16[640,1024]{1,0:T(8,128)(2,1)S(1)}, bf16[640,1024]{1,0:T(8,128)(2,1)S(1)}, u32[]{:S(2)}, u32[]{:S(2)}) collective-permute-start(bf16[640,1024]{1,0:T(8,128)(2,1)S(1)} %get-tuple-element.75), channel_id=1, source_target_pairs={{0,1},{1,0},{2,3},{3,2},{4,5},{5,4},{6,7},{7,6},{8,9},{9,8},{10,11... | collective-permute-start | bytes 3932168 | tf_op jit(solution)/shard_map/ppermute | solution.py:31
  66.4 5.9 %collective-permute-start.20 = (bf16[256,256]{1,0:T(8,128)(2,1)S(1)}, bf16[256,256]{1,0:T(8,128)(2,1)S(1)}, u32[]{:S(2)}, u32[]{:S(2)}) collective-permute-start(bf16[256,256]{1,0:T(8,128)(2,1)S(1)} %get-tuple-element.74), channel_id=1, source_target_pairs={{0,16},{16,0},{32,48},{48,32},{64,80},{80,64},{96,112},{112,96},{1... | collective-permute-start | bytes 393224 | tf_op jit(solution)/shard_map/ppermute | solution.py:31
  67.1 5.6 %collective-permute-start.21 = (bf16[512,128]{1,0:T(8,128)(2,1)S(1)}, bf16[512,128]{1,0:T(8,128)(2,1)S(1)}, u32[]{:S(2)}, u32[]{:S(2)}) collective-permute-start(bf16[512,128]{1,0:T(8,128)(2,1)S(1)} %get-tuple-element.81), channel_id=1, source_target_pairs={{0,4},{1,5},{2,6},{3,7},{4,0},{5,1},{6,2},{7,3},{8,12},{9,13},{10,... | collective-permute-start | bytes 393224 | tf_op jit(solution)/shard_map/ppermute | solution.py:31
  72.7 5.6 %collective-permute-start.22 = (bf16[256,128]{1,0:T(8,128)(2,1)S(1)}, bf16[256,128]{1,0:T(8,128)(2,1)S(1)}, u32[]{:S(2)}, u32[]{:S(2)}) collective-permute-start(bf16[256,128]{1,0:T(8,128)(2,1)S(1)} %get-tuple-element.83), channel_id=1, source_target_pairs={{0,48},{16,32},{32,16},{48,0},{64,112},{80,96},{96,80},{112,64},{1... | collective-permute-start | bytes 196616 | tf_op jit(solution)/shard_map/ppermute | solution.py:31
  74.3 5.5 %collective-permute-start.23 = (bf16[256,128]{1,0:T(8,128)(2,1)S(1)}, bf16[256,128]{1,0:T(8,128)(2,1)S(1)}, u32[]{:S(2)}, u32[]{:S(2)}) collective-permute-start(bf16[256,128]{1,0:T(8,128)(2,1)S(1)} %get-tuple-element.85), channel_id=1, source_target_pairs={{0,12},{1,13},{2,14},{3,15},{4,8},{5,9},{6,10},{7,11},{8,4},{9,5},... | collective-permute-start | bytes 196616 | tf_op jit(solution)/shard_map/ppermute | solution.py:31
  79.8 4.4 %collective-permute-start.24 = (bf16[128,256]{1,0:T(8,128)(2,1)S(1)}, bf16[128,256]{1,0:T(8,128)(2,1)S(1)}, u32[]{:S(2)}, u32[]{:S(2)}) collective-permute-start(bf16[128,256]{1,0:T(8,128)(2,1)S(1)} %get-tuple-element.87), channel_id=1, source_target_pairs={{0,2},{1,3},{2,0},{3,1},{4,6},{5,7},{6,4},{7,5},{8,10},{9,11},{10,... | collective-permute-start | bytes 196616 | tf_op jit(solution)/shard_map/ppermute | solution.py:31
  84.2 5.8 %collective-permute-start.25 = (bf16[128,256]{1,0:T(8,128)(2,1)S(1)}, bf16[128,256]{1,0:T(8,128)(2,1)S(1)}, u32[]{:S(2)}, u32[]{:S(2)}) collective-permute-start(bf16[128,256]{1,0:T(8,128)(2,1)S(1)} %add_convert_fusion.2), channel_id=1, source_target_pairs={{0,64},{16,80},{32,96},{48,112},{64,0},{80,16},{96,32},{112,48},{1... | collective-permute-start | bytes 196616 | tf_op jit(solution)/shard_map/ppermute | solution.py:31
  87.9 7.2 %collective-permute-start.17 = (bf16[128,1024]{1,0:T(8,128)(2,1)S(1)}, bf16[128,1024]{1,0:T(8,128)(2,1)S(1)}, u32[]{:S(2)}, u32[]{:S(2)}) collective-permute-start(bf16[128,1024]{1,0:T(8,128)(2,1)S(1)} %get-tuple-element.90), channel_id=1, source_target_pairs={{0,2},{1,3},{2,0},{3,1},{4,6},{5,7},{6,4},{7,5},{8,10},{9,11},{10,... | collective-permute-start | bytes 786440 | tf_op jit(solution)/shard_map/ppermute | solution.py:31
  90.0 7.4 %collective-permute-start.26 = (bf16[128,256]{1,0:T(8,128)(2,1)S(1)}, bf16[128,256]{1,0:T(8,128)(2,1)S(1)}, u32[]{:S(2)}, u32[]{:S(2)}) collective-permute-start(bf16[128,256]{1,0:T(8,128)(2,1)S(1)} %add_convert_fusion.1), channel_id=1, source_target_pairs={{0,192},{16,208},{32,224},{48,240},{64,128},{80,144},{96,160},{112... | collective-permute-start | bytes 196616 | tf_op jit(solution)/shard_map/ppermute | solution.py:31
  95.2 8.7 %collective-permute-start.18 = (bf16[96,1024]{1,0:T(8,128)(2,1)S(1)}, bf16[96,1024]{1,0:T(8,128)(2,1)S(1)}, u32[]{:S(2)}, u32[]{:S(2)}) collective-permute-start(bf16[96,1024]{1,0:T(8,128)(2,1)S(1)} %slice.45), channel_id=1, source_target_pairs={{0,4},{1,5},{2,6},{3,7},{4,0},{5,1},{6,2},{7,3},{8,12},{9,13},{10,... | collective-permute-start | bytes 589832 | tf_op jit(solution)/shard_map/ppermute | solution.py:31
  97.4 7.0 %collective-permute-start.27 = (bf16[128,256]{1,0:T(8,128)(2,1)S(1)}, bf16[128,256]{1,0:T(8,128)(2,1)S(1)}, u32[]{:S(2)}, u32[]{:S(2)}) collective-permute-start(bf16[128,256]{1,0:T(8,128)(2,1)S(1)} %add_convert_fusion.a), channel_id=1, source_target_pairs={{0,16},{16,0},{32,48},{48,32},{64,80},{80,64},{96,112},{112,96},{1... | collective-permute-start | bytes 196616 | tf_op jit(solution)/shard_map/ppermute | solution.py:31
  98.5 6.4 %collective-permute-start.28 = (bf16[128,256]{1,0:T(8,128)(2,1)S(1)}, bf16[128,256]{1,0:T(8,128)(2,1)S(1)}, u32[]{:S(2)}, u32[]{:S(2)}) collective-permute-start(bf16[128,256]{1,0:T(8,128)(2,1)S(1)} %add_convert_fusion.a), channel_id=1, source_target_pairs={{0,32},{16,48},{32,0},{48,16},{64,96},{80,112},{96,64},{112,80},{1... | collective-permute-start | bytes 196616 | tf_op jit(solution)/shard_map/ppermute | solution.py:31
  102.0 5.5 %collective-permute-start.29 = (bf16[128,256]{1,0:T(8,128)(2,1)S(1)}, bf16[128,256]{1,0:T(8,128)(2,1)S(1)}, u32[]{:S(2)}, u32[]{:S(2)}) collective-permute-start(bf16[128,256]{1,0:T(8,128)(2,1)S(1)} %add_convert_fusion.a), channel_id=1, source_target_pairs={{0,48},{16,32},{32,16},{48,0},{64,112},{80,96},{96,80},{112,64},{1... | collective-permute-start | bytes 196616 | tf_op jit(solution)/shard_map/ppermute | solution.py:31
  102.2 6.6 %collective-permute-start.16 = (bf16[128,1024]{1,0:T(8,128)(2,1)S(1)}, bf16[128,1024]{1,0:T(8,128)(2,1)S(1)}, u32[]{:S(2)}, u32[]{:S(2)}) collective-permute-start(bf16[128,1024]{1,0:T(8,128)(2,1)S(1)} %get-tuple-element.91), channel_id=1, source_target_pairs={{0,2},{1,3},{2,0},{3,1},{4,6},{5,7},{6,4},{7,5},{8,10},{9,11},{10,... | collective-permute-start | bytes 786440 | tf_op jit(solution)/shard_map/ppermute | solution.py:31
  104.0 5.6 %collective-permute-start.19 = (bf16[32,1024]{1,0:T(8,128)(2,1)S(1)}, bf16[32,1024]{1,0:T(8,128)(2,1)S(1)}, u32[]{:S(2)}, u32[]{:S(2)}) collective-permute-start(bf16[32,1024]{1,0:T(8,128)(2,1)S(1)} %fusion), channel_id=1, source_target_pairs={{0,12},{1,13},{2,14},{3,15},{4,8},{5,9},{6,10},{7,11},{8,4},{9,5},... | collective-permute-start | bytes 196616 | tf_op jit(solution)/shard_map/ppermute | solution.py:31

commit v3 on v2

--- a/solution.py
+++ b/solution.py
@@ -88,8 +88,9 @@
         out[rows : 2 * rows, :] = v
 
 
-def arrange_kernel(at_ref, dout_ref, own_ref, other_ref):
-    y, zl, c = at_ref[0], at_ref[1], at_ref[2]
+def arrange_kernel(dout_ref, own_ref, other_ref):
+    seq = lax.axis_index("seq")
+    y, zl, c = seq >> 2, (seq >> 1) & 1, seq & 1
     for n in range(8):
         jy, iz = ORDER[n // 2], n % 2
         base = (y ^ jy) * 4 + (zl ^ iz) * 2
@@ -151,9 +152,14 @@
         lse_ref[:, cols] = top + jnp.log2(total)
 
 
+def row_form(datt_ref, att_ref, lse_ref, cols):
+    datt = datt_ref[:, cols].astype(F32)
+    delta = jnp.sum(datt * att_ref[:, cols].astype(F32), axis=1, keepdims=True)
+    return wide(delta).T[0:1, :], lse_ref[:, cols].T[0:1, :]
+
+
 def back_kernel(
-    q_ref, k_ref, v_ref, qx_ref, a_ref, u_ref, e_ref, datt_ref, att_ref, lse_ref,
-    send_ref, keep_ref, dq_ref, gk_ref, gv_ref, avg_ref,
+    qx_ref, a_ref, u_ref, e_ref, datt_ref, att_ref, lse_ref, send_ref, keep_ref, dq_ref, avg_ref
 ):
     @pl.when(pl.program_id(0) == 0)
     def _():
@@ -161,24 +167,19 @@
             avg_ref[(level - 1) * ROWS : level * ROWS, :] = average_matrix(level)
 
     all_keys, all_ds = [], []
-    for h in range(q_ref.shape[1] // HDIM):
+    for h in range(qx_ref.shape[1] // HDIM):
         cols = slice(h * HDIM, (h + 1) * HDIM)
         datt = datt_ref[:, cols]
-        delta = jnp.sum(datt.astype(F32) * att_ref[:, cols].astype(F32), axis=1, keepdims=True)
-        delta = wide(delta).T[0:1, :]
-        lse = lse_ref[:, cols].T[0:1, :]
+        delta, lse = row_form(datt_ref, att_ref, lse_ref, cols)
         sides = [sibling(level, a_ref, u_ref, e_ref, cols) for level in range(1, 5)]
-        queries = [qx_ref[n * ROWS : (n + 1) * ROWS, cols] for n in range(4)] + [q_ref[:, cols]]
-        keys = [k for k, _ in sides] + [k_ref[:, cols]]
-        vals = jnp.concatenate([v for _, v in sides] + [v_ref[:, cols]], axis=0)
-        scores = [
-            dot_nt(k, q) * SCALE2 + bias
-            for k, q, bias in zip(keys, queries, (1.0, 2.0, 3.0, 4.0, 0.0))
-        ]
+        queries = [qx_ref[n * ROWS : (n + 1) * ROWS, cols] for n in range(4)]
+        keys = [k for k, _ in sides]
+        vals = jnp.concatenate([v for _, v in sides], axis=0)
+        scores = [dot_nt(keys[n], queries[n]) * SCALE2 + float(n + 1) for n in range(4)]
         p = jnp.exp2(jnp.concatenate(scores, axis=0) - lse)
         ds = (p * (dot_nt(vals, datt) - delta)).astype(BF)
         gv = dot(p.astype(BF), datt)
-        ds = [ds[n * 128 : (n + 1) * 128] for n in range(4)] + [ds[512:768]]
+        ds = [ds[n * 128 : (n + 1) * 128] for n in range(4)]
         all_keys.append(jnp.concatenate(keys, axis=0).T)
         all_ds.append(ds)
         for level in range(1, 5):
@@ -195,21 +196,33 @@
                         ref[to : to + n, cols] = gk_l[row : row + n].astype(ref.dtype)
                         ref[to + n : to + 2 * n, cols] = gv_l[row : row + n].astype(ref.dtype)
                         row += n
-        gk_ref[:, cols] = dot(ds[4], queries[4]) * SCALE
-        gv_ref[:, cols] = gv[512:768]
     means = []
     for n in range(4):
         stacked = jnp.concatenate([ds[n] for ds in all_ds], axis=0)
         means.append(dot(stacked, avg_ref[n * ROWS : (n + 1) * ROWS, :]).astype(BF))
+    for h in range(qx_ref.shape[1] // HDIM):
+        rows = slice(h * 128, (h + 1) * 128)
+        gq = dot(all_keys[h], jnp.concatenate([m[rows] for m in means], axis=0))
+        dq_ref[:, h * HDIM : (h + 1) * HDIM] = gq.T * SCALE
+
+
+def local_back_kernel(
+    q_ref, k_ref, v_ref, datt_ref, att_ref, lse_ref, gq_ref, dq_ref, gk_ref, gv_ref
+):
     for h in range(q_ref.shape[1] // HDIM):
-        rows = slice(h * 128, (h + 1) * 128)
-        ds = jnp.concatenate([m[rows] for m in means] + [all_ds[h][4]], axis=0)
-        gq = dot(all_keys[h], ds)
-        dq_ref[:, h * HDIM : (h + 1) * HDIM] = (gq.T * SCALE).astype(BF)
-
-
-def weight_kernel(at_ref, own_ref, other_ref, att_ref, attp_ref, *outs):
-    x = at_ref[3]
+        cols = slice(h * HDIM, (h + 1) * HDIM)
+        q, k, v, datt = q_ref[:, cols], k_ref[:, cols], v_ref[:, cols], datt_ref[:, cols]
+        delta, lse = row_form(datt_ref, att_ref, lse_ref, cols)
+        p = jnp.exp2(dot_nt(k, q) * SCALE2 - lse)
+        ds = (p * (dot_nt(v, datt) - delta)).astype(BF)
+        gk_ref[:, cols] = dot(ds, q) * SCALE
+        gv_ref[:, cols] = dot(p.astype(BF), datt)
+        gq = dot(k.T, ds)
+        dq_ref[:, cols] = (gq_ref[:, cols] + gq.T * SCALE).astype(BF)
+
+
+def weight_kernel(own_ref, other_ref, att_ref, attp_ref, *outs):
+    x = lax.axis_index("dp") & 3
 
     def heads(ref, half):
         blocks = []
@@ -258,11 +271,27 @@
         send_ref[:, cols] = total[128:256].astype(BF)
 
 
-def place_kernel(at_ref, a, b, c, d, out_ref):
-    x = at_ref[3]
+def place_kernel(a, b, c, d, out_ref):
+    x = lax.axis_index("dp") & 3
     for j, ref in enumerate((a, b, c, d)):
         col = pl.multiple_of((x ^ j) * 256, 256)
         out_ref[:, pl.ds(col, 256)] = ref[...].astype(F32)
+
+
+def add_first_kernel(keep_ref, got_ref, out_ref, rest_ref):
+    out_ref[0:128, :] = (keep_ref[256:384, :] + got_ref[512:640, :].astype(F32)).astype(BF)
+    out_ref[128:256, :] = (keep_ref[0:128, :] + got_ref[256:384, :].astype(F32)).astype(BF)
+    rest_ref[...] = keep_ref[128:256, :] + got_ref[384:512, :].astype(F32)
+
+
+def add_second_kernel(rest_ref, got_ref, send_ref, last_ref):
+    total = rest_ref[...] + got_ref[0:128, :].astype(F32)
+    send_ref[...] = total[0:96].astype(BF)
+    last_ref[...] = total[96:128]
+
+
+def add_third_kernel(last_ref, got_ref, out_ref):
+    out_ref[...] = (last_ref[...] + got_ref[64:96, :].astype(F32)).astype(BF)
 
 
 def finish_kernel(gk_ref, gv_ref, r1, r2, r3, r4, dk_ref, dv_ref, bufs):
@@ -281,9 +310,6 @@
     return jax.ShapeDtypeStruct((rows, cols), dtype)
 
 
-SMEM = pl.BlockSpec(memory_space=pltpu.SMEM)
-
-
 def by_heads(rows, step):
     return pl.BlockSpec((rows, step), lambda i: (0, i))
 
@@ -292,18 +318,13 @@
     return pl.BlockSpec((rows, cols), lambda i: (0, 0))
 
 
-def cost(flops, bytes_accessed):
-    return pl.CostEstimate(flops=int(flops), bytes_accessed=int(bytes_accessed), transcendentals=0)
-
-
-def call(kernel, out, **kw):
-    return pl.pallas_call(kernel, out_shape=out, compiler_params=VMEM, **kw)
+def call(kernel, out, flops=1, moved=1, **kw):
+    cost = pl.CostEstimate(flops=int(flops), bytes_accessed=int(moved), transcendentals=0)
+    return pl.pallas_call(kernel, out_shape=out, compiler_params=VMEM, cost_estimate=cost, **kw)
 
 
 def per_device(queries, keys, values, d_out, w_out):
     q, k, v, dout = queries[0], keys[0], values[0], d_out[0]
-    seq, dp = lax.axis_index("seq"), lax.axis_index("dp")
-    place = jnp.stack([seq // 4, seq // 2 % 2, seq % 2, dp % 4]).astype(jnp.int32)
     step = 2 * HDIM
     grid = (WIDTH // step,)
     hs = functools.partial(by_heads, step=step)
@@ -317,33 +338,33 @@
     b3 = swap(l3, "seq", Y1)
     b2 = swap(l2, "seq", ZLO)
     a1 = swap(l1, "seq", CORE)
-    qx, n0, m0, l0 = call(
-        local_kernel,
-        [shape(4 * ROWS, WIDTH)] + [shape(ROWS, WIDTH, F32)] * 3,
-        grid=grid,
-        in_specs=[hs(ROWS)] * 3 + [hs(256)],
-        out_specs=[hs(4 * ROWS)] + [hs(ROWS)] * 3,
-        cost_estimate=cost(2.0e9, 10e6),
-    )(q, k, v, a1)
     t = jnp.concatenate([b3, c4, b4])
-    t, n0 = lax.optimization_barrier((t, n0))
-    d = swap(t, "seq", ZLO)
     datt = call(
         project_kernel,
         shape(ROWS, WIDTH),
         grid=grid,
         in_specs=[whole(ROWS, DMODEL), hs(DMODEL)],
         out_specs=hs(ROWS),
-        cost_estimate=cost(2.0e9, 10e6),
     )(dout, w_out)
+    t, datt = lax.optimization_barrier((t, datt))
+    d = swap(t, "seq", ZLO)
+    qx, n0, m0, l0 = call(
+        local_kernel,
+        flops=8e9,
+        moved=20e6,
+        out=[shape(4 * ROWS, WIDTH)] + [shape(ROWS, WIDTH, F32)] * 3,
+        grid=grid,
+        in_specs=[hs(ROWS)] * 3 + [hs(256)],
+        out_specs=[hs(4 * ROWS)] + [hs(ROWS)] * 3,
+    )(q, k, v, a1)
+    b2, n0 = lax.optimization_barrier((b2, n0))
     u = jnp.concatenate([b2, t, d])
-    u, datt = lax.optimization_barrier((u, datt))
     e = swap(u, "seq", CORE)
     own_t, other_t = call(
         arrange_kernel,
         [shape(1024, ROWS)] * 2,
-        in_specs=[SMEM, pl.BlockSpec(memory_space=pltpu.VMEM)],
-    )(place, dout)
+        in_specs=[pl.BlockSpec(memory_space=pltpu.VMEM)],
+    )(dout)
     rec_t = swap(other_t, "seq", CORE)
     att, lse = call(
         forward_kernel,
@@ -351,16 +372,14 @@
         grid=grid,
         in_specs=[hs(4 * ROWS), hs(384), hs(384)] + [hs(ROWS)] * 3,
         out_specs=[hs(ROWS), hs(ROWS)],
-        cost_estimate=cost(1.0e9, 8e6),
     )(qx, u, e, n0, m0, l0)
 
     attp = swap(att, "seq", CORE)
     o = call(
         weight_kernel,
         [shape(256, 512)] * 4 + [shape(1024, 128)] * 4,
-        in_specs=[SMEM] + [pl.BlockSpec(memory_space=pltpu.VMEM)] * 4,
-        cost_estimate=cost(1.0e9, 4e6),
-    )(place, own_t, rec_t, att, attp)
+        in_specs=[pl.BlockSpec(memory_space=pltpu.VMEM)] * 4,
+    )(own_t, rec_t, att, attp)
     keep_x, send_x, keep_y, send_y = call(
         sum_first_kernel,
         [shape(256, 256, F32), shape(256, 256), shape(512, 128, F32), shape(512, 128)],
@@ -368,51 +387,64 @@
         o[0], swap(o[1], "seq", Y3), swap(o[2], "seq", Y1), swap(o[3], "seq", Y2),
         o[4], swap(o[5], "dp", X3), swap(o[6], "dp", X1), swap(o[7], "dp", X2),
     )
-    send, keep, dq, gk0, gv0 = call(
+    send, keep, gq = call(
         back_kernel,
-        [shape(640, WIDTH), shape(384, WIDTH, F32), shape(ROWS, WIDTH)]
-        + [shape(ROWS, WIDTH, F32)] * 2,
-        grid=grid,
-        in_specs=[hs(ROWS)] * 3 + [hs(4 * ROWS), hs(256), hs(384), hs(384)] + [hs(ROWS)] * 3,
-        out_specs=[hs(640), hs(384)] + [hs(ROWS)] * 3,
+        [shape(640, WIDTH), shape(384, WIDTH, F32), shape(ROWS, WIDTH, F32)],
+        grid=grid,
+        in_specs=[hs(4 * ROWS), hs(256), hs(384), hs(384)] + [hs(ROWS)] * 3,
+        out_specs=[hs(640), hs(384), hs(ROWS)],
         scratch_shapes=[pltpu.VMEM((4 * ROWS, ROWS), BF)],
-        cost_estimate=cost(4.0e9, 12e6),
-    )(q, k, v, qx, a1, u, e, datt, att, lse)
+    )(qx, a1, u, e, datt, att, lse)
     send, _ = lax.optimization_barrier((send, send_x))
 
+    halves = [shape(256, 128, F32), shape(256, 128)] * 2
+    keep_x, next_x, keep_y, next_y = call(sum_second_kernel, halves)(
+        keep_x, swap(send_x, "dp", X1), keep_y, swap(send_y, "seq", Y1)
+    )
+    dq, gk0, gv0 = call(
+        local_back_kernel,
+        flops=5e9,
+        moved=15e6,
+        out=[shape(ROWS, WIDTH)] + [shape(ROWS, WIDTH, F32)] * 2,
+        grid=grid,
+        in_specs=[hs(ROWS)] * 7,
+        out_specs=[hs(ROWS)] * 3,
+    )(q, k, v, datt, att, lse, gq)
+    next_x, gk0 = lax.optimization_barrier((next_x, gk0))
+
     rc = swap(send, "seq", CORE)
-    s = keep + rc[256:640].astype(F32)
-    rz = swap(s[256:384].astype(BF), "seq", ZLO)
-    r2 = swap(s[0:128].astype(BF), "seq", ZLO)
-    t = s[128:256] + rz.astype(F32)
-    ry = swap(t[0:96].astype(BF), "seq", Y1)
-    r4 = swap((t[96:128] + ry[64:96].astype(F32)).astype(BF), "seq", Y3)
+    keep, _ = lax.optimization_barrier((keep, next_x))
+    out, rest = call(add_first_kernel, [shape(256, WIDTH), shape(128, WIDTH, F32)])(keep, rc)
+    rz = swap(out, "seq", ZLO)
+    ty, t4 = call(add_second_kernel, [shape(96, WIDTH), shape(32, WIDTH, F32)])(rest, rz)
+    ry = swap(ty, "seq", Y1)
+    r4 = call(add_third_kernel, shape(32, WIDTH))(t4, ry)
+
+    kept, sent = call(sum_third_kernel, [shape(128, 256, F32), shape(128, 256)])(
+        keep_x, swap(next_x, "dp", X3), keep_y, swap(next_y, "seq", Y3)
+    )
+    g = (kept + swap(sent, "seq", ZLO).astype(F32)).astype(BF)
+    g = g.astype(F32) + swap(g, "dp", ZH1).astype(F32)
+    g, r4 = lax.optimization_barrier((g.astype(BF), r4))
+    r4 = swap(r4, "seq", Y3)
+    g = (g.astype(F32) + swap(g, "dp", ZH3).astype(F32)).astype(BF)
+    g, r4 = lax.optimization_barrier((g, r4))
+    lower = pl.BlockSpec((128, step), lambda i: (1, i))
     dk, dv = call(
         finish_kernel,
-        [shape(ROWS, WIDTH)] * 2,
-        grid=grid,
-        in_specs=[hs(ROWS)] * 2 + [hs(256), hs(128), hs(64), hs(32)],
+        flops=3e9,
+        moved=8e6,
+        out=[shape(ROWS, WIDTH)] * 2,
+        grid=grid,
+        in_specs=[hs(ROWS)] * 2 + [hs(256), lower, hs(64), hs(32)],
         out_specs=[hs(ROWS)] * 2,
         scratch_shapes=[pltpu.VMEM((4, ROWS, HDIM), F32)],
-    )(gk0, gv0, rc, r2, ry, r4)
-
-    halves = [shape(256, 128, F32), shape(256, 128)] * 2
-    keep_x, send_x, keep_y, send_y = call(sum_second_kernel, halves)(
-        keep_x, swap(send_x, "dp", X1), keep_y, swap(send_y, "seq", Y1)
-    )
-    kept, sent = call(sum_third_kernel, [shape(128, 256, F32), shape(128, 256)])(
-        keep_x, swap(send_x, "dp", X3), keep_y, swap(send_y, "seq", Y3)
-    )
-    g = kept + swap(sent, "seq", ZLO).astype(F32)
-    for mask in (ZH1, ZH3):
-        g = g.astype(BF)
-        g = g.astype(F32) + swap(g, "dp", mask).astype(F32)
-    g = g.astype(BF)
+    )(gk0, gv0, rc, rz, ry, r4)
     dw = call(
         place_kernel,
         shape(128, WIDTH, F32),
-        in_specs=[SMEM] + [pl.BlockSpec(memory_space=pltpu.VMEM)] * 4,
-    )(place, g, swap(g, "dp", X1), swap(g, "dp", X2), swap(g, "dp", X3))
+        in_specs=[pl.BlockSpec(memory_space=pltpu.VMEM)] * 4,
+    )(g, swap(g, "dp", X1), swap(g, "dp", X2), swap(g, "dp", X3))
     return dq[None], dk[None], dv[None], dw
 
 

time: 112 us -> 103 us (0.920)
  waiting for transfers between devices: 33.9 us -> 27.2 us
  local copies, waits for them, and re-layouts: 9.61 us -> 4.43 us
  starting transfers between devices: 37 us -> 41 us
    ppermute x30 -> x29, waiting for transfers between devices: 33.9 us -> 27.2 us  [swap(): return lax.ppermute(value, axis, pairs)]
    unnamed x36 -> x16, local copies, waits for them, and re-layouts: 9.55 us -> 4.41 us
    ppermute x30 -> x29, starting transfers between devices: 37 us -> 41 us  [swap(): return lax.ppermute(value, axis, pairs)]
    pallas_call x4 -> x8, Pallas kernels: 10.5 us -> 13.9 us  [the longest x1 6.17 us: per_device(): call(local_kernel, flops=8000000000.0, moved=20000000.0, out=[shape(4 * R...]
    pallas_call x1, Pallas kernels: 8.49 us -> 5.88 us  [per_device(): call(back_kernel, [shape(640, WIDTH), shape(384, WIDTH, F32), shape(ROWS,...]
  transfers between devices with their start and end apart: 30 -> 29, of which waited for: 15 -> 15; matrix products, arithmetic and copies ran while one was open for 1% -> 0% of each run, Pallas kernels for 22% -> 25%
where the time goes in v3:
time: 103 us
  starting transfers between devices  41 us (40%)
  Pallas kernels  29.1 us (28%)
  waiting for transfers between devices  27.2 us (26%)
  local copies, waits for them, and re-layouts  4.43 us (4%)
    ppermute x29, starting transfers between devices, swap(): return lax.ppermute(value, axis, pairs)  41 us
    ppermute x29, waiting for transfers between devices, swap(): return lax.ppermute(value, axis, pairs)  27.2 us
    pallas_call x1, Pallas kernels, per_device(): call(local_kernel, flops=8000000000.0, moved=20000000.0, out=[shape(4 * R...  6.17 us
    pallas_call x1, Pallas kernels, per_device(): call(back_kernel, [shape(640, WIDTH), shape(384, WIDTH, F32), shape(ROWS,...  5.88 us
    unnamed x16, local copies, waits for them, and re-layouts  4.41 us
    pallas_call x1, Pallas kernels, per_device(): call(local_back_kernel, flops=5000000000.0, moved=15000000.0, out=[shape(...  4.28 us
    pallas_call x1, Pallas kernels, per_device(): call(forward_kernel, [shape(ROWS, WIDTH), shape(ROWS, WIDTH, F32)], grid=...  4.14 us
    pallas_call x1, Pallas kernels, per_device(): call(project_kernel, shape(ROWS, WIDTH), grid=grid, in_specs=[whole(ROWS,...  2.42 us
  transfers between devices with their start and end apart: 29, of which 15 were waited for; matrix products, arithmetic and copies ran while one was open for 0% of the time, Pallas kernels for 25%

profile of v3, /device:TPU:32, one launch (start us, length us, event | category | flops | bytes accessed | tf_op | source)
XLA Modules:
  0.0 102.8 jit_solution(16827457000752516311)
XLA Ops:
  0.6 0.0 copy-start.2
  0.7 1.1 %copy-done.2 = bf16[1,256,1024]{2,1,0:T(8,128)(2,1)S(1)} copy-done((bf16[1,256,1024]{2,1,0:T(8,128)(2,1)S(1)}, bf16[1,256,1024]{2,1,0:T(8,128)(2,1)}, u32[]{:S(2)}) %copy-start.2) | copy-done | bytes 524312
  1.8 1.0 %copy-done.4 = bf16[1,256,1024]{2,1,0:T(8,128)(2,1)S(1)} copy-done((bf16[1,256,1024]{2,1,0:T(8,128)(2,1)S(1)}, bf16[1,256,1024]{2,1,0:T(8,128)(2,1)}, u32[]{:S(2)}) %copy-start.4) | copy-done | bytes 524312
  2.8 1.1 %shard_map.84 = (bf16[256,1024]{1,0:T(8,128)(2,1)S(1)}, bf16[128,1024]{1,0:T(8,128)(2,1)S(1)}, bf16[64,1024]{1,0:T(8,128)(2,1)S(1)}, bf16[32,1024]{1,0:T(8,128)(2,1)S(1)}) custom-call(bf16[256,1024]{1,0:T(8,128)(2,1)S(1)} %bitcast.9, bf16[256,1024]{1,0:T(8,128)(2,1)S(1)} %bitcast.12), custom_call_target="tpu_custom_call" | custom-call | flops 1 | bytes 1 | tf_op jit(solution)/shard_map/pallas_call | solution.py:332
  3.9 0.0 collective-permute-start.3
  3.9 1.7 %collective-permute-start = (bf16[64,1024]{1,0:T(8,128)(2,1)S(1)}, bf16[64,1024]{1,0:T(8,128)(2,1)S(1)}, u32[]{:S(2)}, u32[]{:S(2)}) collective-permute-start(bf16[64,1024]{1,0:T(8,128)(2,1)S(1)} %get-tuple-element.58), channel_id=1, source_target_pairs={{0,4},{1,5},{2,6},{3,7},{4,0},{5,1},{6,2},{7,3},{8,12},{9,13},{10,... | collective-permute-start | bytes 393224 | tf_op jit(solution)/shard_map/ppermute | solution.py:31
  5.6 2.2 %collective-permute-start.2 = (bf16[32,1024]{1,0:T(8,128)(2,1)S(1)}, bf16[32,1024]{1,0:T(8,128)(2,1)S(1)}, u32[]{:S(2)}, u32[]{:S(2)}) collective-permute-start(bf16[32,1024]{1,0:T(8,128)(2,1)S(1)} %get-tuple-element.59), channel_id=1, source_target_pairs={{0,12},{1,13},{2,14},{3,15},{4,8},{5,9},{6,10},{7,11},{8,4},{9,5},... | collective-permute-start | bytes 196616 | tf_op jit(solution)/shard_map/ppermute | solution.py:31
  7.8 0.7 collective-permute-start.1
  8.5 1.5 %collective-permute-start.4 = (bf16[128,1024]{1,0:T(8,128)(2,1)S(1)}, bf16[128,1024]{1,0:T(8,128)(2,1)S(1)}, u32[]{:S(2)}, u32[]{:S(2)}) collective-permute-start(bf16[128,1024]{1,0:T(8,128)(2,1)S(1)} %get-tuple-element.63), channel_id=1, source_target_pairs={{0,2},{1,3},{2,0},{3,1},{4,6},{5,7},{6,4},{7,5},{8,10},{9,11},{10,... | collective-permute-start | bytes 786440 | tf_op jit(solution)/shard_map/ppermute | solution.py:31
  10.0 2.2 %copy-done = bf16[2048,1024]{1,0:T(8,128)(2,1)S(1)} copy-done((bf16[2048,1024]{1,0:T(8,128)(2,1)S(1)}, bf16[2048,1024]{1,0:T(8,128)(2,1)}, u32[]{:S(2)}) %copy-start) | copy-done | bytes 4194328
  12.2 2.4 %shard_map.85.datt_ref = bf16[256,1024]{1,0:T(8,128)(2,1)S(1)} custom-call(bf16[256,2048]{1,0:T(8,128)(2,1)S(1)} %bitcast.7, bf16[2048,1024]{1,0:T(8,128)(2,1)S(1)} %copy-done), custom_call_target="tpu_custom_call" | custom-call | flops 1 | bytes 1 | tf_op jit(solution)/shard_map/pallas_call | solution.py:342
  14.6 0.0 collective-permute-done
  14.6 0.7 collective-permute-start.5
  15.3 0.0 collective-permute-done.3.a_ref
  15.3 6.2 %shard_map.86 = (bf16[1024,1024]{1,0:T(8,128)(2,1)S(1)}, f32[256,1024]{1,0:T(8,128)S(1)}, f32[256,1024]{1,0:T(8,128)S(1)}, f32[256,1024]{1,0:T(8,128)S(1)}) custom-call(bf16[256,1024]{1,0:T(8,128)(2,1)S(1)} %bitcast.15, bf16[256,1024]{1,0:T(8,128)(2,1)S(1)} %bitcast.10, bf16[256,1024]{1,0:T(8,128)(2,1)S(1)} %bitcast.13, ...), custom_call_target="tpu_custom_call" | custom-call | flops 8000000000 | bytes 20000000 | tf_op jit(solution)/shard_map/pallas_call | solution.py:351
  21.6 0.7 collective-permute-done.5
  22.3 0.1 collective-permute-start.6
  22.4 0.3 shard_map.90
  22.7 0.6 collective-permute-start.7
  23.3 1.4 %collective-permute-done.6.e_ref = bf16[384,1024]{1,0:T(8,128)(2,1)S(1)} collective-permute-done((bf16[384,1024]{1,0:T(8,128)(2,1)S(1)}, bf16[384,1024]{1,0:T(8,128)(2,1)S(1)}, u32[]{:S(2)}, u32[]{:S(2)}) %collective-permute-start.6) | collective-permute-done | bytes 786464 | tf_op jit(solution)/shard_map/ppermute | solution.py:31
  24.7 4.1 %shard_map.87 = (bf16[256,1024]{1,0:T(8,128)(2,1)S(1)}, f32[256,1024]{1,0:T(8,128)S(1)}) custom-call(bf16[1024,1024]{1,0:T(8,128)(2,1)S(1)} %get-tuple-element.62.qx_ref, bf16[384,1024]{1,0:T(8,128)(2,1)S(1)} %constant_dynamic-update-slice_fusion.u_ref, bf16[384,1024]{1,0:T(8,128)(2,1)S(1)} %collective-permute-done.6.e_ref, ...), custom_call_target="tpu_custom_call" | custom-call | flops 1 | bytes 1 | tf_op jit(solution)/shard_map/pallas_call | solution.py:369
  28.8 0.2 collective-permute-start.8
  29.0 1.8 %collective-permute-done.8.attp_ref = bf16[256,1024]{1,0:T(8,128)(2,1)S(1)} collective-permute-done((bf16[256,1024]{1,0:T(8,128)(2,1)S(1)}, bf16[256,1024]{1,0:T(8,128)(2,1)S(1)}, u32[]{:S(2)}, u32[]{:S(2)}) %collective-permute-start.8) | collective-permute-done | bytes 524320 | tf_op jit(solution)/shard_map/ppermute | solution.py:31
  30.8 1.4 %shard_map.91 = (bf16[256,512]{1,0:T(8,128)(2,1)S(1)}, bf16[256,512]{1,0:T(8,128)(2,1)S(1)}, bf16[256,512]{1,0:T(8,128)(2,1)S(1)}, bf16[256,512]{1,0:T(8,128)(2,...) custom-call(bf16[1024,256]{1,0:T(8,128)(2,1)S(1)} %get-tuple-element, ...), custom_call_target="tpu_custom_call" | custom-call | flops 1 | bytes 1 | tf_op jit(solution)/shard_map/pallas_call | solution.py:378
  32.2 2.4 %collective-permute-start.9 = (bf16[256,512]{1,0:T(8,128)(2,1)S(1)}, bf16[256,512]{1,0:T(8,128)(2,1)S(1)}, u32[]{:S(2)}, u32[]{:S(2)}) collective-permute-start(bf16[256,512]{1,0:T(8,128)(2,1)S(1)} %get-tuple-element.77), channel_id=1, source_target_pairs={{0,12},{1,13},{2,14},{3,15},{4,8},{5,9},{6,10},{7,11},{8,4},{9,5},... | collective-permute-start | bytes 786440 | tf_op jit(solution)/shard_map/ppermute | solution.py:31
  34.6 0.1 collective-permute-start.10
  34.7 2.3 %collective-permute-start.11 = (bf16[256,512]{1,0:T(8,128)(2,1)S(1)}, bf16[256,512]{1,0:T(8,128)(2,1)S(1)}, u32[]{:S(2)}, u32[]{:S(2)}) collective-permute-start(bf16[256,512]{1,0:T(8,128)(2,1)S(1)} %get-tuple-element.79), channel_id=1, source_target_pairs={{0,8},{1,9},{2,10},{3,11},{4,12},{5,13},{6,14},{7,15},{8,0},{9,1},... | collective-permute-start | bytes 786440 | tf_op jit(solution)/shard_map/ppermute | solution.py:31
  37.0 2.7 %collective-permute-start.12 = (bf16[1024,128]{1,0:T(8,128)(2,1)S(1)}, bf16[1024,128]{1,0:T(8,128)(2,1)S(1)}, u32[]{:S(2)}, u32[]{:S(2)}) collective-permute-start(bf16[1024,128]{1,0:T(8,128)(2,1)S(1)} %get-tuple-element.81), channel_id=1, source_target_pairs={{0,48},{16,32},{32,16},{48,0},{64,112},{80,96},{96,80},{112,64},{1... | collective-permute-start | bytes 786440 | tf_op jit(solution)/shard_map/ppermute | solution.py:31
  39.7 0.2 collective-permute-start.13
  39.9 1.9 %collective-permute-done.9.refs_1_ = bf16[256,512]{1,0:T(8,128)(2,1)S(1)} collective-permute-done((bf16[256,512]{1,0:T(8,128)(2,1)S(1)}, bf16[256,512]{1,0:T(8,128)(2,1)S(1)}, u32[]{:S(2)}, u32[]{:S(2)}) %collective-permute-start.9) | collective-permute-done | bytes 262176 | tf_op jit(solution)/shard_map/ppermute | solution.py:31
  41.9 3.0 %collective-permute-start.14 = (bf16[1024,128]{1,0:T(8,128)(2,1)S(1)}, bf16[1024,128]{1,0:T(8,128)(2,1)S(1)}, u32[]{:S(2)}, u32[]{:S(2)}) collective-permute-start(bf16[1024,128]{1,0:T(8,128)(2,1)S(1)} %get-tuple-element.83), channel_id=1, source_target_pairs={{0,32},{16,48},{32,0},{48,16},{64,96},{80,112},{96,64},{112,80},{1... | collective-permute-start | bytes 786440 | tf_op jit(solution)/shard_map/ppermute | solution.py:31
  44.8 5.9 %shard_map.88 = (bf16[640,1024]{1,0:T(8,128)(2,1)S(1)}, f32[384,1024]{1,0:T(8,128)S(1)}, f32[256,1024]{1,0:T(8,128)S(1)}) custom-call(bf16[1024,1024]{1,0:T(8,128)(2,1)S(1)} %get-tuple-element.62.qx_ref, bf16[256,1024]{1,0:T(8,128)(2,1)S(1)} %collective-permute-done.3.a_ref, bf16[384,1024]{1,0:T(8,128)(2,1)S(1)} %constant_dynamic-update-slice_fusion.u_ref, ...), custom_call_target="tpu_custom_call" | custom-call | flops 1 | bytes 1 | tf_op jit(solution)/shard_map/pallas_call | solution.py:390
  50.7 0.0 copy-start.3
  50.7 0.0 copy-start.5
  50.8 0.0 collective-permute-done.11.refs_3_
  50.8 1.7 %collective-permute-done.14.refs_7_ = bf16[1024,128]{1,0:T(8,128)(2,1)S(1)} collective-permute-done((bf16[1024,128]{1,0:T(8,128)(2,1)S(1)}, bf16[1024,128]{1,0:T(8,128)(2,1)S(1)}, u32[]{:S(2)}, u32[]{:S(2)}) %collective-permute-start.14) | collective-permute-done | bytes 262176 | tf_op jit(solution)/shard_map/ppermute | solution.py:31
  52.5 0.2 shard_map.92
  52.8 0.1 collective-permute-start.17
  52.9 0.3 collective-permute-start.15
  53.2 4.3 %shard_map.89 = (bf16[256,1024]{1,0:T(8,128)(2,1)}, f32[256,1024]{1,0:T(8,128)S(1)}, f32[256,1024]{1,0:T(8,128)S(1)}) custom-call(bf16[256,1024]{1,0:T(8,128)(2,1)S(1)} %bitcast.16, bf16[256,1024]{1,0:T(8,128)(2,1)S(1)} %bitcast.11, bf16[256,1024]{1,0:T(8,128)(2,1)S(1)} %bitcast.14, bf16[256,1024]{1,0:T(8,128)(2,1)S(1)} %shard_map.85.datt_ref, ...), custom_call_target="tpu_custom_call" | custom-call | flops 5000000000 | bytes 15000000 | tf_op jit(solution)/shard_map/pallas_call | solution.py:404
  57.5 1.3 %collective-permute-done.15.got_x = bf16[256,256]{1,0:T(8,128)(2,1)S(1)} collective-permute-done((bf16[256,256]{1,0:T(8,128)(2,1)S(1)}, bf16[256,256]{1,0:T(8,128)(2,1)S(1)}, u32[]{:S(2)}, u32[]{:S(2)}) %collective-permute-start.15) | collective-permute-done | bytes 131104 | tf_op jit(solution)/shard_map/ppermute | solution.py:31
  58.9 0.1 shard_map.94
  59.0 1.2 %collective-permute-start.18 = (bf16[256,1024]{1,0:T(8,128)(2,1)S(1)}, bf16[256,1024]{1,0:T(8,128)(2,1)S(1)}, u32[]{:S(2)}, u32[]{:S(2)}) collective-permute-start(bf16[256,1024]{1,0:T(8,128)(2,1)S(1)} %get-tuple-element.97), channel_id=1, source_target_pairs={{0,2},{1,3},{2,0},{3,1},{4,6},{5,7},{6,4},{7,5},{8,10},{9,11},{10,... | collective-permute-start | bytes 1572872 | tf_op jit(solution)/shard_map/ppermute | solution.py:31
  60.2 2.5 %collective-permute-start.20 = (bf16[256,128]{1,0:T(8,128)(2,1)S(1)}, bf16[256,128]{1,0:T(8,128)(2,1)S(1)}, u32[]{:S(2)}, u32[]{:S(2)}) collective-permute-start(bf16[256,128]{1,0:T(8,128)(2,1)S(1)} %get-tuple-element.95), channel_id=1, source_target_pairs={{0,48},{16,32},{32,16},{48,0},{64,112},{80,96},{96,80},{112,64},{1... | collective-permute-start | bytes 196616 | tf_op jit(solution)/shard_map/ppermute | solution.py:31
  62.7 2.3 %collective-permute-start.21 = (bf16[256,128]{1,0:T(8,128)(2,1)S(1)}, bf16[256,128]{1,0:T(8,128)(2,1)S(1)}, u32[]{:S(2)}, u32[]{:S(2)}) collective-permute-start(bf16[256,128]{1,0:T(8,128)(2,1)S(1)} %get-tuple-element.102), channel_id=1, source_target_pairs={{0,12},{1,13},{2,14},{3,15},{4,8},{5,9},{6,10},{7,11},{8,4},{9,5},... | collective-permute-start | bytes 196616 | tf_op jit(solution)/shard_map/ppermute | solution.py:31
  65.0 0.6 collective-permute-done.20.got_x
  65.7 2.5 %collective-permute-done.21.got_y = bf16[256,128]{1,0:T(8,128)(2,1)S(1)} collective-permute-done((bf16[256,128]{1,0:T(8,128)(2,1)S(1)}, bf16[256,128]{1,0:T(8,128)(2,1)S(1)}, u32[]{:S(2)}, u32[]{:S(2)}) %collective-permute-start.21) | collective-permute-done | bytes 65568 | tf_op jit(solution)/shard_map/ppermute | solution.py:31
  68.2 1.2 %collective-permute-start.22 = (bf16[128,256]{1,0:T(8,128)(2,1)S(1)}, bf16[128,256]{1,0:T(8,128)(2,1)S(1)}, u32[]{:S(2)}, u32[]{:S(2)}) collective-permute-start(bf16[128,256]{1,0:T(8,128)(2,1)S(1)} %get-tuple-element.104), channel_id=1, source_target_pairs={{0,2},{1,3},{2,0},{3,1},{4,6},{5,7},{6,4},{7,5},{8,10},{9,11},{10,... | collective-permute-start | bytes 196616 | tf_op jit(solution)/shard_map/ppermute | solution.py:31
  69.4 4.5 %collective-permute-done.22 = bf16[128,256]{1,0:T(8,128)(2,1)S(1)} collective-permute-done((bf16[128,256]{1,0:T(8,128)(2,1)S(1)}, bf16[128,256]{1,0:T(8,128)(2,1)S(1)}, u32[]{:S(2)}, u32[]{:S(2)}) %collective-permute-start.22) | collective-permute-done | bytes 65568 | tf_op jit(solution)/shard_map/ppermute | solution.py:31
  74.0 3.3 %collective-permute-start.23 = (bf16[128,256]{1,0:T(8,128)(2,1)S(1)}, bf16[128,256]{1,0:T(8,128)(2,1)S(1)}, u32[]{:S(2)}, u32[]{:S(2)}) collective-permute-start(bf16[128,256]{1,0:T(8,128)(2,1)S(1)} %add_convert_fusion.2), channel_id=1, source_target_pairs={{0,64},{16,80},{32,96},{48,112},{64,0},{80,16},{96,32},{112,48},{1... | collective-permute-start | bytes 196616 | tf_op jit(solution)/shard_map/ppermute | solution.py:31
  77.3 1.1 %collective-permute-start.19 = (bf16[96,1024]{1,0:T(8,128)(2,1)S(1)}, bf16[96,1024]{1,0:T(8,128)(2,1)S(1)}, u32[]{:S(2)}, u32[]{:S(2)}) collective-permute-start(bf16[96,1024]{1,0:T(8,128)(2,1)S(1)} %get-tuple-element.99), channel_id=1, source_target_pairs={{0,4},{1,5},{2,6},{3,7},{4,0},{5,1},{6,2},{7,3},{8,12},{9,13},{10,... | collective-permute-start | bytes 589832 | tf_op jit(solution)/shard_map/ppermute | solution.py:31
  78.4 1.4 %collective-permute-done.23 = bf16[128,256]{1,0:T(8,128)(2,1)S(1)} collective-permute-done((bf16[128,256]{1,0:T(8,128)(2,1)S(1)}, bf16[128,256]{1,0:T(8,128)(2,1)S(1)}, u32[]{:S(2)}, u32[]{:S(2)}) %collective-permute-start.23) | collective-permute-done | bytes 65568 | tf_op jit(solution)/shard_map/ppermute | solution.py:31
  79.8 3.3 %collective-permute-done.19.got_ref.r3 = bf16[96,1024]{1,0:T(8,128)(2,1)S(1)} collective-permute-done((bf16[96,1024]{1,0:T(8,128)(2,1)S(1)}, bf16[96,1024]{1,0:T(8,128)(2,1)S(1)}, u32[]{:S(2)}, u32[]{:S(2)}) %collective-permute-start.19) | collective-permute-done | bytes 196640 | tf_op jit(solution)/shard_map/ppermute | solution.py:31
  83.1 3.7 %collective-permute-start.24 = (bf16[128,256]{1,0:T(8,128)(2,1)S(1)}, bf16[128,256]{1,0:T(8,128)(2,1)S(1)}, u32[]{:S(2)}, u32[]{:S(2)}) collective-permute-start(bf16[128,256]{1,0:T(8,128)(2,1)S(1)} %add_convert_fusion.1), channel_id=1, source_target_pairs={{0,192},{16,208},{32,224},{48,240},{64,128},{80,144},{96,160},{112... | collective-permute-start | bytes 196616 | tf_op jit(solution)/shard_map/ppermute | solution.py:31
  86.8 2.3 %collective-permute-start.25 = (bf16[32,1024]{1,0:T(8,128)(2,1)S(1)}, bf16[32,1024]{1,0:T(8,128)(2,1)S(1)}, u32[]{:S(2)}, u32[]{:S(2)}) collective-permute-start(bf16[32,1024]{1,0:T(8,128)(2,1)S(1)} %shard_map.97), channel_id=1, source_target_pairs={{0,12},{1,13},{2,14},{3,15},{4,8},{5,9},{6,10},{7,11},{8,4},{9,5},... | collective-permute-start | bytes 196616 | tf_op jit(solution)/shard_map/ppermute | solution.py:31
  89.1 1.1 %collective-permute-done.24 = bf16[128,256]{1,0:T(8,128)(2,1)S(1)} collective-permute-done((bf16[128,256]{1,0:T(8,128)(2,1)S(1)}, bf16[128,256]{1,0:T(8,128)(2,1)S(1)}, u32[]{:S(2)}, u32[]{:S(2)}) %collective-permute-start.24) | collective-permute-done | bytes 65568 | tf_op jit(solution)/shard_map/ppermute | solution.py:31
  90.3 2.0 %collective-permute-done.25.r4 = bf16[32,1024]{1,0:T(8,128)(2,1)S(1)} collective-permute-done((bf16[32,1024]{1,0:T(8,128)(2,1)S(1)}, bf16[32,1024]{1,0:T(8,128)(2,1)S(1)}, u32[]{:S(2)}, u32[]{:S(2)}) %collective-permute-start.25) | collective-permute-done | bytes 65568 | tf_op jit(solution)/shard_map/ppermute | solution.py:31
  92.2 1.4 %collective-permute-start.26 = (bf16[128,256]{1,0:T(8,128)(2,1)S(1)}, bf16[128,256]{1,0:T(8,128)(2,1)S(1)}, u32[]{:S(2)}, u32[]{:S(2)}) collective-permute-start(bf16[128,256]{1,0:T(8,128)(2,1)S(1)} %add_convert_fusion.a), channel_id=1, source_target_pairs={{0,16},{16,0},{32,48},{48,32},{64,80},{80,64},{96,112},{112,96},{1... | collective-permute-start | bytes 196616 | tf_op jit(solution)/shard_map/ppermute | solution.py:31
  93.7 2.8 %collective-permute-start.27 = (bf16[128,256]{1,0:T(8,128)(2,1)S(1)}, bf16[128,256]{1,0:T(8,128)(2,1)S(1)}, u32[]{:S(2)}, u32[]{:S(2)}) collective-permute-start(bf16[128,256]{1,0:T(8,128)(2,1)S(1)} %add_convert_fusion.a), channel_id=1, source_target_pairs={{0,32},{16,48},{32,0},{48,16},{64,96},{80,112},{96,64},{112,80},{1... | collective-permute-start | bytes 196616 | tf_op jit(solution)/shard_map/ppermute | solution.py:31
  96.5 0.5 collective-permute-start.28
  96.9 2.1 %shard_map.98 = (bf16[256,1024]{1,0:T(8,128)(2,1)}, bf16[256,1024]{1,0:T(8,128)(2,1)}) custom-call(f32[256,1024]{1,0:T(8,128)S(1)} %get-tuple-element.90.gk_ref, f32[256,1024]{1,0:T(8,128)S(1)} %get-tuple-element.91.gv_ref, bf16[640,1024]{1,0:T(8,128)(2,1)S(1)} %collective-permute-done.17.got_ref.r1, ...), custom_call_target="tpu_custom_call" | custom-call | flops 3000000000 | bytes 8000000 | tf_op jit(solution)/shard_map/pallas_call | solution.py:433
  99.0 0.4 collective-permute-done.27.c
  99.4 2.5 %collective-permute-done.28.d = bf16[128,256]{1,0:T(8,128)(2,1)S(1)} collective-permute-done((bf16[128,256]{1,0:T(8,128)(2,1)S(1)}, bf16[128,256]{1,0:T(8,128)(2,1)S(1)}, u32[]{:S(2)}, u32[]{:S(2)}) %collective-permute-start.28) | collective-permute-done | bytes 65568 | tf_op jit(solution)/shard_map/ppermute | solution.py:31
  101.9 0.8 shard_map.99
  (31 shorter events, 0.3 us)
Async XLA Ops:
  0.6 9.3 %copy-start.1 = (bf16[1,256,2048]{2,1,0:T(8,128)(2,1)S(1)}, bf16[1,256,2048]{2,1,0:T(8,128)(2,1)}, u32[]{:S(2)}) copy-start(bf16[1,256,2048]{2,1,0:T(8,128)(2,1)} %param.8) | copy-start | bytes 3145732
  0.6 1.1 %copy-start.2 = (bf16[1,256,1024]{2,1,0:T(8,128)(2,1)S(1)}, bf16[1,256,1024]{2,1,0:T(8,128)(2,1)}, u32[]{:S(2)}) copy-start(bf16[1,256,1024]{2,1,0:T(8,128)(2,1)} %param.6) | copy-start | bytes 1572868
  1.8 1.0 %copy-start.4 = (bf16[1,256,1024]{2,1,0:T(8,128)(2,1)S(1)}, bf16[1,256,1024]{2,1,0:T(8,128)(2,1)}, u32[]{:S(2)}) copy-start(bf16[1,256,1024]{2,1,0:T(8,128)(2,1)} %param.7) | copy-start | bytes 1572868
  3.9 11.4 %collective-permute-start.3 = (bf16[256,1024]{1,0:T(8,128)(2,1)S(1)}, bf16[256,1024]{1,0:T(8,128)(2,1)S(1)}, u32[]{:S(2)}, u32[]{:S(2)}) collective-permute-start(bf16[256,1024]{1,0:T(8,128)(2,1)S(1)} %get-tuple-element.61), channel_id=1, source_target_pairs={{0,1},{1,0},{2,3},{3,2},{4,5},{5,4},{6,7},{7,6},{8,9},{9,8},{10,11... | collective-permute-start | bytes 1572872 | tf_op jit(solution)/shard_map/ppermute | solution.py:31
  3.9 10.7 %collective-permute-start = (bf16[64,1024]{1,0:T(8,128)(2,1)S(1)}, bf16[64,1024]{1,0:T(8,128)(2,1)S(1)}, u32[]{:S(2)}, u32[]{:S(2)}) collective-permute-start(bf16[64,1024]{1,0:T(8,128)(2,1)S(1)} %get-tuple-element.58), channel_id=1, source_target_pairs={{0,4},{1,5},{2,6},{3,7},{4,0},{5,1},{6,2},{7,3},{8,12},{9,13},{10,... | collective-permute-start | bytes 393224 | tf_op jit(solution)/shard_map/ppermute | solution.py:31
  5.6 9.0 %collective-permute-start.2 = (bf16[32,1024]{1,0:T(8,128)(2,1)S(1)}, bf16[32,1024]{1,0:T(8,128)(2,1)S(1)}, u32[]{:S(2)}, u32[]{:S(2)}) collective-permute-start(bf16[32,1024]{1,0:T(8,128)(2,1)S(1)} %get-tuple-element.59), channel_id=1, source_target_pairs={{0,12},{1,13},{2,14},{3,15},{4,8},{5,9},{6,10},{7,11},{8,4},{9,5},... | collective-permute-start | bytes 196616 | tf_op jit(solution)/shard_map/ppermute | solution.py:31
  7.8 6.8 %collective-permute-start.1 = (bf16[32,1024]{1,0:T(8,128)(2,1)S(1)}, bf16[32,1024]{1,0:T(8,128)(2,1)S(1)}, u32[]{:S(2)}, u32[]{:S(2)}) collective-permute-start(bf16[32,1024]{1,0:T(8,128)(2,1)S(1)} %get-tuple-element.59), channel_id=1, source_target_pairs={{0,8},{1,9},{2,10},{3,11},{4,12},{5,13},{6,14},{7,15},{8,0},{9,1},... | collective-permute-start | bytes 196616 | tf_op jit(solution)/shard_map/ppermute | solution.py:31
  8.5 13.0 %collective-permute-start.4 = (bf16[128,1024]{1,0:T(8,128)(2,1)S(1)}, bf16[128,1024]{1,0:T(8,128)(2,1)S(1)}, u32[]{:S(2)}, u32[]{:S(2)}) collective-permute-start(bf16[128,1024]{1,0:T(8,128)(2,1)S(1)} %get-tuple-element.63), channel_id=1, source_target_pairs={{0,2},{1,3},{2,0},{3,1},{4,6},{5,7},{6,4},{7,5},{8,10},{9,11},{10,... | collective-permute-start | bytes 786440 | tf_op jit(solution)/shard_map/ppermute | solution.py:31
  10.0 2.2 %copy-start = (bf16[2048,1024]{1,0:T(8,128)(2,1)S(1)}, bf16[2048,1024]{1,0:T(8,128)(2,1)}, u32[]{:S(2)}) copy-start(bf16[2048,1024]{1,0:T(8,128)(2,1)} %w_ref.1) | copy-start | bytes 12582916
  12.2 3.2 %copy-start.6 = (bf16[1,256,1024]{2,1,0:T(8,128)(2,1)S(1)}, bf16[1,256,1024]{2,1,0:T(8,128)(2,1)}, u32[]{:S(2)}) copy-start(bf16[1,256,1024]{2,1,0:T(8,128)(2,1)} %param.5) | copy-start | bytes 1572868
  14.6 7.6 %collective-permute-start.5 = (bf16[128,1024]{1,0:T(8,128)(2,1)S(1)}, bf16[128,1024]{1,0:T(8,128)(2,1)S(1)}, u32[]{:S(2)}, u32[]{:S(2)}) collective-permute-start(bf16[128,1024]{1,0:T(8,128)(2,1)S(1)} %pad_maximum_fusion), channel_id=1, source_target_pairs={{0,2},{1,3},{2,0},{3,1},{4,6},{5,7},{6,4},{7,5},{8,10},{9,11},{10,... | collective-permute-start | bytes 786440 | tf_op jit(solution)/shard_map/ppermute | solution.py:31
  22.3 2.4 %collective-permute-start.6 = (bf16[384,1024]{1,0:T(8,128)(2,1)S(1)}, bf16[384,1024]{1,0:T(8,128)(2,1)S(1)}, u32[]{:S(2)}, u32[]{:S(2)}) collective-permute-start(bf16[384,1024]{1,0:T(8,128)(2,1)S(1)} %constant_dynamic-update-slice_fusion.u_ref), channel_id=1, source_target_pairs={{0,1},{1,0},{2,3},{3,2},{4,5},{5,4},{6,7},{7,6},{8,9},{9,8},{10,11... | collective-permute-start | bytes 2359304 | tf_op jit(solution)/shard_map/ppermute | solution.py:31
  22.7 6.3 %collective-permute-start.7 = (bf16[1024,256]{1,0:T(8,128)(2,1)S(1)}, bf16[1024,256]{1,0:T(8,128)(2,1)S(1)}, u32[]{:S(2)}, u32[]{:S(2)}) collective-permute-start(bf16[1024,256]{1,0:T(8,128)(2,1)S(1)} %get-tuple-element.75), channel_id=1, source_target_pairs={{0,1},{1,0},{2,3},{3,2},{4,5},{5,4},{6,7},{7,6},{8,9},{9,8},{10,11... | collective-permute-start | bytes 1572872 | tf_op jit(solution)/shard_map/ppermute | solution.py:31
  28.8 2.0 %collective-permute-start.8 = (bf16[256,1024]{1,0:T(8,128)(2,1)S(1)}, bf16[256,1024]{1,0:T(8,128)(2,1)S(1)}, u32[]{:S(2)}, u32[]{:S(2)}) collective-permute-start(bf16[256,1024]{1,0:T(8,128)(2,1)S(1)} %get-tuple-element.70.att_ref), channel_id=1, source_target_pairs={{0,1},{1,0},{2,3},{3,2},{4,5},{5,4},{6,7},{7,6},{8,9},{9,8},{10,11... | collective-permute-start | bytes 1572872 | tf_op jit(solution)/shard_map/ppermute | solution.py:31
  32.2 9.6 %collective-permute-start.9 = (bf16[256,512]{1,0:T(8,128)(2,1)S(1)}, bf16[256,512]{1,0:T(8,128)(2,1)S(1)}, u32[]{:S(2)}, u32[]{:S(2)}) collective-permute-start(bf16[256,512]{1,0:T(8,128)(2,1)S(1)} %get-tuple-element.77), channel_id=1, source_target_pairs={{0,12},{1,13},{2,14},{3,15},{4,8},{5,9},{6,10},{7,11},{8,4},{9,5},... | collective-permute-start | bytes 786440 | tf_op jit(solution)/shard_map/ppermute | solution.py:31
  34.6 16.2 %collective-permute-start.10 = (bf16[256,512]{1,0:T(8,128)(2,1)S(1)}, bf16[256,512]{1,0:T(8,128)(2,1)S(1)}, u32[]{:S(2)}, u32[]{:S(2)}) collective-permute-start(bf16[256,512]{1,0:T(8,128)(2,1)S(1)} %get-tuple-element.78), channel_id=1, source_target_pairs={{0,4},{1,5},{2,6},{3,7},{4,0},{5,1},{6,2},{7,3},{8,12},{9,13},{10,... | collective-permute-start | bytes 786440 | tf_op jit(solution)/shard_map/ppermute | solution.py:31
  34.7 16.0 %collective-permute-start.11 = (bf16[256,512]{1,0:T(8,128)(2,1)S(1)}, bf16[256,512]{1,0:T(8,128)(2,1)S(1)}, u32[]{:S(2)}, u32[]{:S(2)}) collective-permute-start(bf16[256,512]{1,0:T(8,128)(2,1)S(1)} %get-tuple-element.79), channel_id=1, source_target_pairs={{0,8},{1,9},{2,10},{3,11},{4,12},{5,13},{6,14},{7,15},{8,0},{9,1},... | collective-permute-start | bytes 786440 | tf_op jit(solution)/shard_map/ppermute | solution.py:31
  37.0 13.8 %collective-permute-start.12 = (bf16[1024,128]{1,0:T(8,128)(2,1)S(1)}, bf16[1024,128]{1,0:T(8,128)(2,1)S(1)}, u32[]{:S(2)}, u32[]{:S(2)}) collective-permute-start(bf16[1024,128]{1,0:T(8,128)(2,1)S(1)} %get-tuple-element.81), channel_id=1, source_target_pairs={{0,48},{16,32},{32,16},{48,0},{64,112},{80,96},{96,80},{112,64},{1... | collective-permute-start | bytes 786440 | tf_op jit(solution)/shard_map/ppermute | solution.py:31
  39.7 11.1 %collective-permute-start.13 = (bf16[1024,128]{1,0:T(8,128)(2,1)S(1)}, bf16[1024,128]{1,0:T(8,128)(2,1)S(1)}, u32[]{:S(2)}, u32[]{:S(2)}) collective-permute-start(bf16[1024,128]{1,0:T(8,128)(2,1)S(1)} %get-tuple-element.82), channel_id=1, source_target_pairs={{0,16},{16,0},{32,48},{48,32},{64,80},{80,64},{96,112},{112,96},{1... | collective-permute-start | bytes 786440 | tf_op jit(solution)/shard_map/ppermute | solution.py:31
  41.9 10.7 %collective-permute-start.14 = (bf16[1024,128]{1,0:T(8,128)(2,1)S(1)}, bf16[1024,128]{1,0:T(8,128)(2,1)S(1)}, u32[]{:S(2)}, u32[]{:S(2)}) collective-permute-start(bf16[1024,128]{1,0:T(8,128)(2,1)S(1)} %get-tuple-element.83), channel_id=1, source_target_pairs={{0,32},{16,48},{32,0},{48,16},{64,96},{80,112},{96,64},{112,80},{1... | collective-permute-start | bytes 786440 | tf_op jit(solution)/shard_map/ppermute | solution.py:31
  50.7 2.5 %copy-start.3 = (bf16[1,256,1024]{2,1,0:T(8,128)(2,1)S(1)}, bf16[1,256,1024]{2,1,0:T(8,128)(2,1)}, u32[]{:S(2)}) copy-start(bf16[1,256,1024]{2,1,0:T(8,128)(2,1)} %param.6) | copy-start | bytes 1572868
  50.7 2.5 %copy-start.5 = (bf16[1,256,1024]{2,1,0:T(8,128)(2,1)S(1)}, bf16[1,256,1024]{2,1,0:T(8,128)(2,1)}, u32[]{:S(2)}) copy-start(bf16[1,256,1024]{2,1,0:T(8,128)(2,1)} %param.7) | copy-start | bytes 1572868
  52.8 6.1 %collective-permute-start.17 = (bf16[640,1024]{1,0:T(8,128)(2,1)S(1)}, bf16[640,1024]{1,0:T(8,128)(2,1)S(1)}, u32[]{:S(2)}, u32[]{:S(2)}) collective-permute-start(bf16[640,1024]{1,0:T(8,128)(2,1)S(1)} %get-tuple-element.93), channel_id=1, source_target_pairs={{0,1},{1,0},{2,3},{3,2},{4,5},{5,4},{6,7},{7,6},{8,9},{9,8},{10,11... | collective-permute-start | bytes 3932168 | tf_op jit(solution)/shard_map/ppermute | solution.py:31
  52.9 5.9 %collective-permute-start.15 = (bf16[256,256]{1,0:T(8,128)(2,1)S(1)}, bf16[256,256]{1,0:T(8,128)(2,1)S(1)}, u32[]{:S(2)}, u32[]{:S(2)}) collective-permute-start(bf16[256,256]{1,0:T(8,128)(2,1)S(1)} %get-tuple-element.85), channel_id=1, source_target_pairs={{0,16},{16,0},{32,48},{48,32},{64,80},{80,64},{96,112},{112,96},{1... | collective-permute-start | bytes 393224 | tf_op jit(solution)/shard_map/ppermute | solution.py:31
  53.2 5.6 %collective-permute-start.16 = (bf16[512,128]{1,0:T(8,128)(2,1)S(1)}, bf16[512,128]{1,0:T(8,128)(2,1)S(1)}, u32[]{:S(2)}, u32[]{:S(2)}) collective-permute-start(bf16[512,128]{1,0:T(8,128)(2,1)S(1)} %get-tuple-element.87), channel_id=1, source_target_pairs={{0,4},{1,5},{2,6},{3,7},{4,0},{5,1},{6,2},{7,3},{8,12},{9,13},{10,... | collective-permute-start | bytes 393224 | tf_op jit(solution)/shard_map/ppermute | solution.py:31
  59.0 18.3 %collective-permute-start.18 = (bf16[256,1024]{1,0:T(8,128)(2,1)S(1)}, bf16[256,1024]{1,0:T(8,128)(2,1)S(1)}, u32[]{:S(2)}, u32[]{:S(2)}) collective-permute-start(bf16[256,1024]{1,0:T(8,128)(2,1)S(1)} %get-tuple-element.97), channel_id=1, source_target_pairs={{0,2},{1,3},{2,0},{3,1},{4,6},{5,7},{6,4},{7,5},{8,10},{9,11},{10,... | collective-permute-start | bytes 1572872 | tf_op jit(solution)/shard_map/ppermute | solution.py:31
  60.2 5.5 %collective-permute-start.20 = (bf16[256,128]{1,0:T(8,128)(2,1)S(1)}, bf16[256,128]{1,0:T(8,128)(2,1)S(1)}, u32[]{:S(2)}, u32[]{:S(2)}) collective-permute-start(bf16[256,128]{1,0:T(8,128)(2,1)S(1)} %get-tuple-element.95), channel_id=1, source_target_pairs={{0,48},{16,32},{32,16},{48,0},{64,112},{80,96},{96,80},{112,64},{1... | collective-permute-start | bytes 196616 | tf_op jit(solution)/shard_map/ppermute | solution.py:31
  62.7 5.5 %collective-permute-start.21 = (bf16[256,128]{1,0:T(8,128)(2,1)S(1)}, bf16[256,128]{1,0:T(8,128)(2,1)S(1)}, u32[]{:S(2)}, u32[]{:S(2)}) collective-permute-start(bf16[256,128]{1,0:T(8,128)(2,1)S(1)} %get-tuple-element.102), channel_id=1, source_target_pairs={{0,12},{1,13},{2,14},{3,15},{4,8},{5,9},{6,10},{7,11},{8,4},{9,5},... | collective-permute-start | bytes 196616 | tf_op jit(solution)/shard_map/ppermute | solution.py:31
  68.2 5.7 %collective-permute-start.22 = (bf16[128,256]{1,0:T(8,128)(2,1)S(1)}, bf16[128,256]{1,0:T(8,128)(2,1)S(1)}, u32[]{:S(2)}, u32[]{:S(2)}) collective-permute-start(bf16[128,256]{1,0:T(8,128)(2,1)S(1)} %get-tuple-element.104), channel_id=1, source_target_pairs={{0,2},{1,3},{2,0},{3,1},{4,6},{5,7},{6,4},{7,5},{8,10},{9,11},{10,... | collective-permute-start | bytes 196616 | tf_op jit(solution)/shard_map/ppermute | solution.py:31
  74.0 5.8 %collective-permute-start.23 = (bf16[128,256]{1,0:T(8,128)(2,1)S(1)}, bf16[128,256]{1,0:T(8,128)(2,1)S(1)}, u32[]{:S(2)}, u32[]{:S(2)}) collective-permute-start(bf16[128,256]{1,0:T(8,128)(2,1)S(1)} %add_convert_fusion.2), channel_id=1, source_target_pairs={{0,64},{16,80},{32,96},{48,112},{64,0},{80,16},{96,32},{112,48},{1... | collective-permute-start | bytes 196616 | tf_op jit(solution)/shard_map/ppermute | solution.py:31
  77.3 5.8 %collective-permute-start.19 = (bf16[96,1024]{1,0:T(8,128)(2,1)S(1)}, bf16[96,1024]{1,0:T(8,128)(2,1)S(1)}, u32[]{:S(2)}, u32[]{:S(2)}) collective-permute-start(bf16[96,1024]{1,0:T(8,128)(2,1)S(1)} %get-tuple-element.99), channel_id=1, source_target_pairs={{0,4},{1,5},{2,6},{3,7},{4,0},{5,1},{6,2},{7,3},{8,12},{9,13},{10,... | collective-permute-start | bytes 589832 | tf_op jit(solution)/shard_map/ppermute | solution.py:31
  83.1 7.2 %collective-permute-start.24 = (bf16[128,256]{1,0:T(8,128)(2,1)S(1)}, bf16[128,256]{1,0:T(8,128)(2,1)S(1)}, u32[]{:S(2)}, u32[]{:S(2)}) collective-permute-start(bf16[128,256]{1,0:T(8,128)(2,1)S(1)} %add_convert_fusion.1), channel_id=1, source_target_pairs={{0,192},{16,208},{32,224},{48,240},{64,128},{80,144},{96,160},{112... | collective-permute-start | bytes 196616 | tf_op jit(solution)/shard_map/ppermute | solution.py:31
  86.8 5.5 %collective-permute-start.25 = (bf16[32,1024]{1,0:T(8,128)(2,1)S(1)}, bf16[32,1024]{1,0:T(8,128)(2,1)S(1)}, u32[]{:S(2)}, u32[]{:S(2)}) collective-permute-start(bf16[32,1024]{1,0:T(8,128)(2,1)S(1)} %shard_map.97), channel_id=1, source_target_pairs={{0,12},{1,13},{2,14},{3,15},{4,8},{5,9},{6,10},{7,11},{8,4},{9,5},... | collective-permute-start | bytes 196616 | tf_op jit(solution)/shard_map/ppermute | solution.py:31
  92.2 6.8 %collective-permute-start.26 = (bf16[128,256]{1,0:T(8,128)(2,1)S(1)}, bf16[128,256]{1,0:T(8,128)(2,1)S(1)}, u32[]{:S(2)}, u32[]{:S(2)}) collective-permute-start(bf16[128,256]{1,0:T(8,128)(2,1)S(1)} %add_convert_fusion.a), channel_id=1, source_target_pairs={{0,16},{16,0},{32,48},{48,32},{64,80},{80,64},{96,112},{112,96},{1... | collective-permute-start | bytes 196616 | tf_op jit(solution)/shard_map/ppermute | solution.py:31
  93.7 5.8 %collective-permute-start.27 = (bf16[128,256]{1,0:T(8,128)(2,1)S(1)}, bf16[128,256]{1,0:T(8,128)(2,1)S(1)}, u32[]{:S(2)}, u32[]{:S(2)}) collective-permute-start(bf16[128,256]{1,0:T(8,128)(2,1)S(1)} %add_convert_fusion.a), channel_id=1, source_target_pairs={{0,32},{16,48},{32,0},{48,16},{64,96},{80,112},{96,64},{112,80},{1... | collective-permute-start | bytes 196616 | tf_op jit(solution)/shard_map/ppermute | solution.py:31
  96.5 5.5 %collective-permute-start.28 = (bf16[128,256]{1,0:T(8,128)(2,1)S(1)}, bf16[128,256]{1,0:T(8,128)(2,1)S(1)}, u32[]{:S(2)}, u32[]{:S(2)}) collective-permute-start(bf16[128,256]{1,0:T(8,128)(2,1)S(1)} %add_convert_fusion.a), channel_id=1, source_target_pairs={{0,48},{16,32},{32,16},{48,0},{64,112},{80,96},{96,80},{112,64},{1... | collective-permute-start | bytes 196616 | tf_op jit(solution)/shard_map/ppermute | solution.py:31

commit v4 on v3

--- a/solution.py
+++ b/solution.py
@@ -23,7 +23,8 @@
 
 CORE, ZLO, Y1, Y2, Y3 = 1, 2, 4, 8, 12
 X1, X2, X3, ZH1, ZH3 = 1, 2, 3, 4, 12
-ORDER = (0, 3, 1, 2)
+ORDER_X = (0, 3, 1, 2)
+ORDER_Y = (0, 1, 3, 2)
 
 
 def swap(value, axis, mask):
@@ -92,7 +93,7 @@
     seq = lax.axis_index("seq")
     y, zl, c = seq >> 2, (seq >> 1) & 1, seq & 1
     for n in range(8):
-        jy, iz = ORDER[n // 2], n % 2
+        jy, iz = ORDER_Y[n // 2], n % 2
         base = (y ^ jy) * 4 + (zl ^ iz) * 2
         for ref, core in ((own_ref, c), (other_ref, 1 - c)):
             at = pl.multiple_of((base + core) * 128, 128)
@@ -226,7 +227,7 @@
 
     def heads(ref, half):
         blocks = []
-        for jx in ORDER:
+        for jx in ORDER_X:
             col = pl.multiple_of(((x ^ jx) * 2 + half) * 128, 128)
             blocks.append(ref[:, pl.ds(col, 128)])
         return jnp.concatenate(blocks, axis=1)
@@ -254,21 +255,57 @@
         out[...] = sum(r[rows, :].astype(F32) for r in ins[4:]).astype(out.dtype)
 
 
-def sum_second_kernel(in_x, got_x, in_y, got_y, keep_x, send_x, keep_y, send_y):
+def fold(rows, x):
+    parts = [x[n * rows : (n + 1) * rows] for n in range(x.shape[0] // rows)]
+    return jnp.concatenate(parts, axis=1)
+
+
+def unfold(cols, x):
+    parts = [x[:, n * cols : (n + 1) * cols] for n in range(x.shape[1] // cols)]
+    return jnp.concatenate(parts, axis=0)
+
+
+def sum_second_kernel(
+    in_x, got_x, in_y, got_y, keep_ref, rc_ref,
+    keep_x, send_x, keep_y, send_y, z_ref, b3_ref, b4_ref,
+):
     for n, out in enumerate((keep_x, send_x)):
         cols = slice(n * 128, (n + 1) * 128)
         out[...] = (in_x[:, cols] + got_x[:, cols].astype(F32)).astype(out.dtype)
-    for n, out in enumerate((keep_y, send_y)):
-        rows = slice(n * 256, (n + 1) * 256)
-        out[...] = (in_y[rows, :] + got_y[rows, :].astype(F32)).astype(out.dtype)
-
-
-def sum_third_kernel(in_x, got_x, in_y, got_y, keep_ref, send_ref):
-    for half, (own, got) in enumerate(((in_x, got_x), (in_y, got_y))):
-        cols = slice(half * 128, (half + 1) * 128)
-        total = own[...] + got[...].astype(F32)
-        keep_ref[:, cols] = total[0:128]
-        send_ref[:, cols] = total[128:256].astype(BF)
+    keep_y[...] = in_y[0:256, :] + got_y[0:256, :].astype(F32)
+    leaves = in_y[256:512, :] + got_y[256:512, :].astype(F32)
+    send_y[0:32, :] = fold(32, leaves).astype(BF)
+
+    def both(at, rows):
+        return keep_ref[at : at + rows, :] + rc_ref[256 + at : 256 + at + rows, :].astype(F32)
+
+    send_y[32:64, :] = both(192, 32).astype(BF)
+    send_y[64:96, :] = both(320, 32).astype(BF)
+    z_ref[0:128, :] = both(0, 128).astype(BF)
+    z_ref[128:192, :] = both(256, 64).astype(BF)
+    b3_ref[...] = both(128, 64)
+    b4_ref[0:32, :] = both(224, 32)
+    b4_ref[32:64, :] = both(352, 32)
+
+
+def sum_third_kernel(in_x, got_x, in_y, got_y, b4_ref, keep_ref, send_ref, s4_ref):
+    total_x = in_x[...] + got_x[...].astype(F32)
+    total_y = in_y[...] + unfold(128, got_y[0:32, :].astype(F32))
+    keep_ref[:, 0:128] = total_x[0:128]
+    keep_ref[:, 128:256] = total_y[0:128]
+    leaves = jnp.concatenate([total_x[128:256], total_y[128:256]], axis=1)
+    send_ref[0:32, :] = fold(32, leaves).astype(BF)
+    s4_ref[...] = b4_ref[0:32, :] + got_y[32:64, :].astype(F32)
+    send_ref[32:64, :] = (b4_ref[32:64, :] + got_y[64:96, :].astype(F32)).astype(BF)
+
+
+def sum_fourth_kernel(in_ref, got_ref, s4_ref, g_ref, r4_ref):
+    g_ref[...] = (in_ref[...] + unfold(256, got_ref[0:32, :].astype(F32))).astype(BF)
+    r4_ref[...] = (s4_ref[...] + got_ref[32:64, :].astype(F32)).astype(BF)
+
+
+def add_kernel(b3_ref, got_ref, out_ref):
+    out_ref[...] = (b3_ref[...] + got_ref[128:192, :].astype(F32)).astype(BF)
 
 
 def place_kernel(a, b, c, d, out_ref):
@@ -276,22 +313,6 @@
     for j, ref in enumerate((a, b, c, d)):
         col = pl.multiple_of((x ^ j) * 256, 256)
         out_ref[:, pl.ds(col, 256)] = ref[...].astype(F32)
-
-
-def add_first_kernel(keep_ref, got_ref, out_ref, rest_ref):
-    out_ref[0:128, :] = (keep_ref[256:384, :] + got_ref[512:640, :].astype(F32)).astype(BF)
-    out_ref[128:256, :] = (keep_ref[0:128, :] + got_ref[256:384, :].astype(F32)).astype(BF)
-    rest_ref[...] = keep_ref[128:256, :] + got_ref[384:512, :].astype(F32)
-
-
-def add_second_kernel(rest_ref, got_ref, send_ref, last_ref):
-    total = rest_ref[...] + got_ref[0:128, :].astype(F32)
-    send_ref[...] = total[0:96].astype(BF)
-    last_ref[...] = total[96:128]
-
-
-def add_third_kernel(last_ref, got_ref, out_ref):
-    out_ref[...] = (last_ref[...] + got_ref[64:96, :].astype(F32)).astype(BF)
 
 
 def finish_kernel(gk_ref, gv_ref, r1, r2, r3, r4, dk_ref, dv_ref, bufs):
@@ -384,7 +405,7 @@
         sum_first_kernel,
         [shape(256, 256, F32), shape(256, 256), shape(512, 128, F32), shape(512, 128)],
     )(
-        o[0], swap(o[1], "seq", Y3), swap(o[2], "seq", Y1), swap(o[3], "seq", Y2),
+        o[0], swap(o[1], "seq", Y1), swap(o[2], "seq", Y3), swap(o[3], "seq", Y2),
         o[4], swap(o[5], "dp", X3), swap(o[6], "dp", X1), swap(o[7], "dp", X2),
     )
     send, keep, gq = call(
@@ -397,10 +418,7 @@
     )(qx, a1, u, e, datt, att, lse)
     send, _ = lax.optimization_barrier((send, send_x))
 
-    halves = [shape(256, 128, F32), shape(256, 128)] * 2
-    keep_x, next_x, keep_y, next_y = call(sum_second_kernel, halves)(
-        keep_x, swap(send_x, "dp", X1), keep_y, swap(send_y, "seq", Y1)
-    )
+    rc = swap(send, "seq", CORE)
     dq, gk0, gv0 = call(
         local_back_kernel,
         flops=5e9,
@@ -410,41 +428,41 @@
         in_specs=[hs(ROWS)] * 7,
         out_specs=[hs(ROWS)] * 3,
     )(q, k, v, datt, att, lse, gq)
-    next_x, gk0 = lax.optimization_barrier((next_x, gk0))
-
-    rc = swap(send, "seq", CORE)
-    keep, _ = lax.optimization_barrier((keep, next_x))
-    out, rest = call(add_first_kernel, [shape(256, WIDTH), shape(128, WIDTH, F32)])(keep, rc)
-    rz = swap(out, "seq", ZLO)
-    ty, t4 = call(add_second_kernel, [shape(96, WIDTH), shape(32, WIDTH, F32)])(rest, rz)
-    ry = swap(ty, "seq", Y1)
-    r4 = call(add_third_kernel, shape(32, WIDTH))(t4, ry)
-
-    kept, sent = call(sum_third_kernel, [shape(128, 256, F32), shape(128, 256)])(
-        keep_x, swap(next_x, "dp", X3), keep_y, swap(next_y, "seq", Y3)
+    keep, gk0 = lax.optimization_barrier((keep, gk0))
+    keep_x, next_x, keep_y, next_y, out_z, b3, b4 = call(
+        sum_second_kernel,
+        [shape(256, 128, F32), shape(256, 128), shape(256, 128, F32), shape(96, WIDTH)]
+        + [shape(192, WIDTH), shape(64, WIDTH, F32), shape(64, WIDTH, F32)],
+    )(keep_x, swap(send_x, "dp", X1), keep_y, swap(send_y, "seq", Y3), keep, rc)
+    rz = swap(out_z, "seq", ZLO)
+    r3 = call(add_kernel, shape(64, WIDTH))(b3, rz)
+    kept, sent, s4 = call(
+        sum_third_kernel, [shape(128, 256, F32), shape(64, WIDTH), shape(32, WIDTH, F32)]
+    )(keep_x, swap(next_x, "dp", X3), keep_y, swap(next_y, "seq", Y1), b4)
+    g, r4 = call(sum_fourth_kernel, [shape(128, 256), shape(32, WIDTH)])(
+        kept, swap(sent, "seq", ZLO), s4
     )
-    g = (kept + swap(sent, "seq", ZLO).astype(F32)).astype(BF)
+    g, r3 = lax.optimization_barrier((g, r3))
+    r3, r4 = swap(r3, "seq", Y1), swap(r4, "seq", Y3)
     g = g.astype(F32) + swap(g, "dp", ZH1).astype(F32)
-    g, r4 = lax.optimization_barrier((g.astype(BF), r4))
-    r4 = swap(r4, "seq", Y3)
+    g = g.astype(BF)
     g = (g.astype(F32) + swap(g, "dp", ZH3).astype(F32)).astype(BF)
-    g, r4 = lax.optimization_barrier((g, r4))
-    lower = pl.BlockSpec((128, step), lambda i: (1, i))
     dk, dv = call(
         finish_kernel,
         flops=3e9,
         moved=8e6,
         out=[shape(ROWS, WIDTH)] * 2,
         grid=grid,
-        in_specs=[hs(ROWS)] * 2 + [hs(256), lower, hs(64), hs(32)],
+        in_specs=[hs(ROWS)] * 2 + [hs(256), hs(128), hs(64), hs(32)],
         out_specs=[hs(ROWS)] * 2,
         scratch_shapes=[pltpu.VMEM((4, ROWS, HDIM), F32)],
-    )(gk0, gv0, rc, rz, ry, r4)
+    )(gk0, gv0, rc, rz, r3, r4)
+    g2, dk = lax.optimization_barrier((swap(g, "dp", X2), dk))
     dw = call(
         place_kernel,
         shape(128, WIDTH, F32),
         in_specs=[pl.BlockSpec(memory_space=pltpu.VMEM)] * 4,
-    )(g, swap(g, "dp", X1), swap(g, "dp", X2), swap(g, "dp", X3))
+    )(g, swap(g, "dp", X1), g2, swap(g, "dp", X3))
     return dq[None], dk[None], dv[None], dw
 
 

time: 103 us -> 98 us (0.951)
  waiting for transfers between devices: 27.2 us -> 22.5 us
    ppermute x29, waiting for transfers between devices: 27.2 us -> 22.5 us  [swap(): return lax.ppermute(value, axis, pairs)]
  transfers between devices with their start and end apart: 29 -> 29, of which waited for: 15 -> 13; matrix products, arithmetic and copies ran while one was open for 0% -> 0% of each run, Pallas kernels for 25% -> 26%
where the time goes in v4:
time: 98 us; the launch traced here: 97.9 us
  starting transfers between devices  40.9 us (42%)
  Pallas kernels  29.1 us (30%)
  waiting for transfers between devices  22.5 us (23%)
  local copies, waits for them, and re-layouts  4.43 us (5%)
    ppermute x29, starting transfers between devices, swap(): return lax.ppermute(value, axis, pairs)  40.9 us
    ppermute x29, waiting for transfers between devices, swap(): return lax.ppermute(value, axis, pairs)  22.5 us
    pallas_call x1, Pallas kernels, per_device(): call(local_kernel, flops=8000000000.0, moved=20000000.0, out=[shape(4 * R...  6.17 us
    pallas_call x1, Pallas kernels, per_device(): call(back_kernel, [shape(640, WIDTH), shape(384, WIDTH, F32), shape(ROWS,...  5.88 us
    unnamed x16, local copies, waits for them, and re-layouts  4.41 us
    pallas_call x1, Pallas kernels, per_device(): call(local_back_kernel, flops=5000000000.0, moved=15000000.0, out=[shape(...  4.26 us
    pallas_call x1, Pallas kernels, per_device(): call(forward_kernel, [shape(ROWS, WIDTH), shape(ROWS, WIDTH, F32)], grid=...  4.14 us
    pallas_call x1, Pallas kernels, per_device(): call(project_kernel, shape(ROWS, WIDTH), grid=grid, in_specs=[whole(ROWS,...  2.42 us
  transfers between devices with their start and end apart: 29, of which 13 were waited for; matrix products, arithmetic and copies ran while one was open for 0% of the time, Pallas kernels for 26%

profile of v4, /device:TPU:32, one launch (start us, length us, event | category | flops | bytes accessed | tf_op | source)
XLA Modules:
  0.0 97.9 jit_solution(3163545028014565526)
XLA Ops:
  0.6 0.0 copy-start.2
  0.7 1.1 %copy-done.2 = bf16[1,256,1024]{2,1,0:T(8,128)(2,1)S(1)} copy-done((bf16[1,256,1024]{2,1,0:T(8,128)(2,1)S(1)}, bf16[1,256,1024]{2,1,0:T(8,128)(2,1)}, u32[]{:S(2)}) %copy-start.2) | copy-done | bytes 524312
  1.8 1.0 %copy-done.4 = bf16[1,256,1024]{2,1,0:T(8,128)(2,1)S(1)} copy-done((bf16[1,256,1024]{2,1,0:T(8,128)(2,1)S(1)}, bf16[1,256,1024]{2,1,0:T(8,128)(2,1)}, u32[]{:S(2)}) %copy-start.4) | copy-done | bytes 524312
  2.8 1.1 %shard_map.84 = (bf16[256,1024]{1,0:T(8,128)(2,1)S(1)}, bf16[128,1024]{1,0:T(8,128)(2,1)S(1)}, bf16[64,1024]{1,0:T(8,128)(2,1)S(1)}, bf16[32,1024]{1,0:T(8,128)(2,1)S(1)}) custom-call(bf16[256,1024]{1,0:T(8,128)(2,1)S(1)} %bitcast.9, bf16[256,1024]{1,0:T(8,128)(2,1)S(1)} %bitcast.12), custom_call_target="tpu_custom_call" | custom-call | flops 1 | bytes 1 | tf_op jit(solution)/shard_map/pallas_call | solution.py:353
  3.9 0.0 collective-permute-start.3
  3.9 1.7 %collective-permute-start = (bf16[64,1024]{1,0:T(8,128)(2,1)S(1)}, bf16[64,1024]{1,0:T(8,128)(2,1)S(1)}, u32[]{:S(2)}, u32[]{:S(2)}) collective-permute-start(bf16[64,1024]{1,0:T(8,128)(2,1)S(1)} %get-tuple-element.59), channel_id=1, source_target_pairs={{0,4},{1,5},{2,6},{3,7},{4,0},{5,1},{6,2},{7,3},{8,12},{9,13},{10,... | collective-permute-start | bytes 393224 | tf_op jit(solution)/shard_map/ppermute | solution.py:32
  5.6 2.2 %collective-permute-start.2 = (bf16[32,1024]{1,0:T(8,128)(2,1)S(1)}, bf16[32,1024]{1,0:T(8,128)(2,1)S(1)}, u32[]{:S(2)}, u32[]{:S(2)}) collective-permute-start(bf16[32,1024]{1,0:T(8,128)(2,1)S(1)} %get-tuple-element.60), channel_id=1, source_target_pairs={{0,12},{1,13},{2,14},{3,15},{4,8},{5,9},{6,10},{7,11},{8,4},{9,5},... | collective-permute-start | bytes 196616 | tf_op jit(solution)/shard_map/ppermute | solution.py:32
  7.8 0.7 collective-permute-start.1
  8.5 1.5 %collective-permute-start.4 = (bf16[128,1024]{1,0:T(8,128)(2,1)S(1)}, bf16[128,1024]{1,0:T(8,128)(2,1)S(1)}, u32[]{:S(2)}, u32[]{:S(2)}) collective-permute-start(bf16[128,1024]{1,0:T(8,128)(2,1)S(1)} %get-tuple-element.64), channel_id=1, source_target_pairs={{0,2},{1,3},{2,0},{3,1},{4,6},{5,7},{6,4},{7,5},{8,10},{9,11},{10,... | collective-permute-start | bytes 786440 | tf_op jit(solution)/shard_map/ppermute | solution.py:32
  10.0 2.2 %copy-done = bf16[2048,1024]{1,0:T(8,128)(2,1)S(1)} copy-done((bf16[2048,1024]{1,0:T(8,128)(2,1)S(1)}, bf16[2048,1024]{1,0:T(8,128)(2,1)}, u32[]{:S(2)}) %copy-start) | copy-done | bytes 4194328
  12.2 2.4 %shard_map.85.datt_ref = bf16[256,1024]{1,0:T(8,128)(2,1)S(1)} custom-call(bf16[256,2048]{1,0:T(8,128)(2,1)S(1)} %bitcast.7, bf16[2048,1024]{1,0:T(8,128)(2,1)S(1)} %copy-done), custom_call_target="tpu_custom_call" | custom-call | flops 1 | bytes 1 | tf_op jit(solution)/shard_map/pallas_call | solution.py:363
  14.6 0.0 collective-permute-done.2
  14.6 0.0 collective-permute-done
  14.6 0.7 collective-permute-start.5
  15.3 0.0 collective-permute-done.3.a_ref
  15.3 6.2 %shard_map.86 = (bf16[1024,1024]{1,0:T(8,128)(2,1)S(1)}, f32[256,1024]{1,0:T(8,128)S(1)}, f32[256,1024]{1,0:T(8,128)S(1)}, f32[256,1024]{1,0:T(8,128)S(1)}) custom-call(bf16[256,1024]{1,0:T(8,128)(2,1)S(1)} %bitcast.15, bf16[256,1024]{1,0:T(8,128)(2,1)S(1)} %bitcast.10, bf16[256,1024]{1,0:T(8,128)(2,1)S(1)} %bitcast.13, ...), custom_call_target="tpu_custom_call" | custom-call | flops 8000000000 | bytes 20000000 | tf_op jit(solution)/shard_map/pallas_call | solution.py:372
  21.6 0.7 collective-permute-done.5
  22.3 0.1 collective-permute-start.6
  22.4 0.3 shard_map.90
  22.7 0.6 collective-permute-start.7
  23.3 1.4 %collective-permute-done.6.e_ref = bf16[384,1024]{1,0:T(8,128)(2,1)S(1)} collective-permute-done((bf16[384,1024]{1,0:T(8,128)(2,1)S(1)}, bf16[384,1024]{1,0:T(8,128)(2,1)S(1)}, u32[]{:S(2)}, u32[]{:S(2)}) %collective-permute-start.6) | collective-permute-done | bytes 786464 | tf_op jit(solution)/shard_map/ppermute | solution.py:32
  24.7 4.1 %shard_map.87 = (bf16[256,1024]{1,0:T(8,128)(2,1)S(1)}, f32[256,1024]{1,0:T(8,128)S(1)}) custom-call(bf16[1024,1024]{1,0:T(8,128)(2,1)S(1)} %get-tuple-element.63.qx_ref, bf16[384,1024]{1,0:T(8,128)(2,1)S(1)} %constant_dynamic-update-slice_fusion.u_ref, bf16[384,1024]{1,0:T(8,128)(2,1)S(1)} %collective-permute-done.6.e_ref, ...), custom_call_target="tpu_custom_call" | custom-call | flops 1 | bytes 1 | tf_op jit(solution)/shard_map/pallas_call | solution.py:390
  28.8 0.2 collective-permute-start.8
  29.0 1.8 %collective-permute-done.8.attp_ref = bf16[256,1024]{1,0:T(8,128)(2,1)S(1)} collective-permute-done((bf16[256,1024]{1,0:T(8,128)(2,1)S(1)}, bf16[256,1024]{1,0:T(8,128)(2,1)S(1)}, u32[]{:S(2)}, u32[]{:S(2)}) %collective-permute-start.8) | collective-permute-done | bytes 524320 | tf_op jit(solution)/shard_map/ppermute | solution.py:32
  30.8 1.4 %shard_map.91 = (bf16[256,512]{1,0:T(8,128)(2,1)S(1)}, bf16[256,512]{1,0:T(8,128)(2,1)S(1)}, bf16[256,512]{1,0:T(8,128)(2,1)S(1)}, bf16[256,512]{1,0:T(8,128)(2,...) custom-call(bf16[1024,256]{1,0:T(8,128)(2,1)S(1)} %get-tuple-element, ...), custom_call_target="tpu_custom_call" | custom-call | flops 1 | bytes 1 | tf_op jit(solution)/shard_map/pallas_call | solution.py:399
  32.2 0.9 collective-permute-start.9
  33.2 2.2 %collective-permute-start.10 = (bf16[256,512]{1,0:T(8,128)(2,1)S(1)}, bf16[256,512]{1,0:T(8,128)(2,1)S(1)}, u32[]{:S(2)}, u32[]{:S(2)}) collective-permute-start(bf16[256,512]{1,0:T(8,128)(2,1)S(1)} %get-tuple-element.79), channel_id=1, source_target_pairs={{0,12},{1,13},{2,14},{3,15},{4,8},{5,9},{6,10},{7,11},{8,4},{9,5},... | collective-permute-start | bytes 786440 | tf_op jit(solution)/shard_map/ppermute | solution.py:32
  35.3 1.0 %collective-permute-start.11 = (bf16[256,512]{1,0:T(8,128)(2,1)S(1)}, bf16[256,512]{1,0:T(8,128)(2,1)S(1)}, u32[]{:S(2)}, u32[]{:S(2)}) collective-permute-start(bf16[256,512]{1,0:T(8,128)(2,1)S(1)} %get-tuple-element.80), channel_id=1, source_target_pairs={{0,8},{1,9},{2,10},{3,11},{4,12},{5,13},{6,14},{7,15},{8,0},{9,1},... | collective-permute-start | bytes 786440 | tf_op jit(solution)/shard_map/ppermute | solution.py:32
  36.4 2.7 %collective-permute-start.12 = (bf16[1024,128]{1,0:T(8,128)(2,1)S(1)}, bf16[1024,128]{1,0:T(8,128)(2,1)S(1)}, u32[]{:S(2)}, u32[]{:S(2)}) collective-permute-start(bf16[1024,128]{1,0:T(8,128)(2,1)S(1)} %get-tuple-element.82), channel_id=1, source_target_pairs={{0,48},{16,32},{32,16},{48,0},{64,112},{80,96},{96,80},{112,64},{1... | collective-permute-start | bytes 786440 | tf_op jit(solution)/shard_map/ppermute | solution.py:32
  39.1 0.2 collective-permute-start.13
  39.3 2.1 %collective-permute-done.9.refs_1_ = bf16[256,512]{1,0:T(8,128)(2,1)S(1)} collective-permute-done((bf16[256,512]{1,0:T(8,128)(2,1)S(1)}, bf16[256,512]{1,0:T(8,128)(2,1)S(1)}, u32[]{:S(2)}, u32[]{:S(2)}) %collective-permute-start.9) | collective-permute-done | bytes 262176 | tf_op jit(solution)/shard_map/ppermute | solution.py:32
  41.4 3.0 %collective-permute-start.14 = (bf16[1024,128]{1,0:T(8,128)(2,1)S(1)}, bf16[1024,128]{1,0:T(8,128)(2,1)S(1)}, u32[]{:S(2)}, u32[]{:S(2)}) collective-permute-start(bf16[1024,128]{1,0:T(8,128)(2,1)S(1)} %get-tuple-element.84), channel_id=1, source_target_pairs={{0,32},{16,48},{32,0},{48,16},{64,96},{80,112},{96,64},{112,80},{1... | collective-permute-start | bytes 786440 | tf_op jit(solution)/shard_map/ppermute | solution.py:32
  44.4 5.9 %shard_map.88 = (bf16[640,1024]{1,0:T(8,128)(2,1)S(1)}, f32[384,1024]{1,0:T(8,128)S(1)}, f32[256,1024]{1,0:T(8,128)S(1)}) custom-call(bf16[1024,1024]{1,0:T(8,128)(2,1)S(1)} %get-tuple-element.63.qx_ref, bf16[256,1024]{1,0:T(8,128)(2,1)S(1)} %collective-permute-done.3.a_ref, bf16[384,1024]{1,0:T(8,128)(2,1)S(1)} %constant_dynamic-update-slice_fusion.u_ref, ...), custom_call_target="tpu_custom_call" | custom-call | flops 1 | bytes 1 | tf_op jit(solution)/shard_map/pallas_call | solution.py:411
  50.3 0.0 copy-start.3
  50.3 0.0 copy-start.5
  50.3 0.0 collective-permute-done.11.refs_3_
  50.4 1.5 %collective-permute-done.14.refs_7_ = bf16[1024,128]{1,0:T(8,128)(2,1)S(1)} collective-permute-done((bf16[1024,128]{1,0:T(8,128)(2,1)S(1)}, bf16[1024,128]{1,0:T(8,128)(2,1)S(1)}, u32[]{:S(2)}, u32[]{:S(2)}) %collective-permute-start.14) | collective-permute-done | bytes 262176 | tf_op jit(solution)/shard_map/ppermute | solution.py:32
  51.9 0.2 shard_map.92
  52.2 0.1 collective-permute-start.17
  52.3 0.3 collective-permute-start.15
  52.6 2.3 %collective-permute-start.16 = (bf16[512,128]{1,0:T(8,128)(2,1)S(1)}, bf16[512,128]{1,0:T(8,128)(2,1)S(1)}, u32[]{:S(2)}, u32[]{:S(2)}) collective-permute-start(bf16[512,128]{1,0:T(8,128)(2,1)S(1)} %get-tuple-element.88), channel_id=1, source_target_pairs={{0,12},{1,13},{2,14},{3,15},{4,8},{5,9},{6,10},{7,11},{8,4},{9,5},... | collective-permute-start | bytes 393224 | tf_op jit(solution)/shard_map/ppermute | solution.py:32
  54.9 4.3 %shard_map.89 = (bf16[256,1024]{1,0:T(8,128)(2,1)}, f32[256,1024]{1,0:T(8,128)S(1)}, f32[256,1024]{1,0:T(8,128)S(1)}) custom-call(bf16[256,1024]{1,0:T(8,128)(2,1)S(1)} %bitcast.16, bf16[256,1024]{1,0:T(8,128)(2,1)S(1)} %bitcast.11, bf16[256,1024]{1,0:T(8,128)(2,1)S(1)} %bitcast.14, bf16[256,1024]{1,0:T(8,128)(2,1)S(1)} %shard_map.85.datt_ref, ...), custom_call_target="tpu_custom_call" | custom-call | flops 5000000000 | bytes 15000000 | tf_op jit(solution)/shard_map/pallas_call | solution.py:422
  59.2 0.0 collective-permute-done.15.got_x
  59.2 0.2 collective-permute-done.16.got_y
  59.4 0.0 collective-permute-done.17.rc_ref.r1
  59.4 0.2 shard_map.93
  59.6 1.2 %collective-permute-start.21 = (bf16[192,1024]{1,0:T(8,128)(2,1)S(1)}, bf16[192,1024]{1,0:T(8,128)(2,1)S(1)}, u32[]{:S(2)}, u32[]{:S(2)}) collective-permute-start(bf16[192,1024]{1,0:T(8,128)(2,1)S(1)} %get-tuple-element.104), channel_id=1, source_target_pairs={{0,2},{1,3},{2,0},{3,1},{4,6},{5,7},{6,4},{7,5},{8,10},{9,11},{10,... | collective-permute-start | bytes 1179656 | tf_op jit(solution)/shard_map/ppermute | solution.py:32
  60.8 2.5 %collective-permute-start.18 = (bf16[256,128]{1,0:T(8,128)(2,1)S(1)}, bf16[256,128]{1,0:T(8,128)(2,1)S(1)}, u32[]{:S(2)}, u32[]{:S(2)}) collective-permute-start(bf16[256,128]{1,0:T(8,128)(2,1)S(1)} %get-tuple-element.95), channel_id=1, source_target_pairs={{0,48},{16,32},{32,16},{48,0},{64,112},{80,96},{96,80},{112,64},{1... | collective-permute-start | bytes 196616 | tf_op jit(solution)/shard_map/ppermute | solution.py:32
  63.3 3.0 %collective-permute-done.18.got_x = bf16[256,128]{1,0:T(8,128)(2,1)S(1)} collective-permute-done((bf16[256,128]{1,0:T(8,128)(2,1)S(1)}, bf16[256,128]{1,0:T(8,128)(2,1)S(1)}, u32[]{:S(2)}, u32[]{:S(2)}) %collective-permute-start.18) | collective-permute-done | bytes 65568 | tf_op jit(solution)/shard_map/ppermute | solution.py:32
  66.2 0.6 collective-permute-done.19.got_y
  66.9 1.2 %collective-permute-start.20 = (bf16[64,1024]{1,0:T(8,128)(2,1)S(1)}, bf16[64,1024]{1,0:T(8,128)(2,1)S(1)}, u32[]{:S(2)}, u32[]{:S(2)}) collective-permute-start(bf16[64,1024]{1,0:T(8,128)(2,1)S(1)} %get-tuple-element.100), channel_id=1, source_target_pairs={{0,2},{1,3},{2,0},{3,1},{4,6},{5,7},{6,4},{7,5},{8,10},{9,11},{10,... | collective-permute-start | bytes 393224 | tf_op jit(solution)/shard_map/ppermute | solution.py:32
  68.0 5.1 %collective-permute-done.20.got_ref = bf16[64,1024]{1,0:T(8,128)(2,1)S(1)} collective-permute-done((bf16[64,1024]{1,0:T(8,128)(2,1)S(1)}, bf16[64,1024]{1,0:T(8,128)(2,1)S(1)}, u32[]{:S(2)}, u32[]{:S(2)}) %collective-permute-start.20) | collective-permute-done | bytes 131104 | tf_op jit(solution)/shard_map/ppermute | solution.py:32
  73.2 0.0 collective-permute-done.21.got_ref.r2
  73.2 3.4 %collective-permute-start.22 = (bf16[128,256]{1,0:T(8,128)(2,1)S(1)}, bf16[128,256]{1,0:T(8,128)(2,1)S(1)}, u32[]{:S(2)}, u32[]{:S(2)}) collective-permute-start(bf16[128,256]{1,0:T(8,128)(2,1)S(1)} %get-tuple-element.105), channel_id=1, source_target_pairs={{0,64},{16,80},{32,96},{48,112},{64,0},{80,16},{96,32},{112,48},{1... | collective-permute-start | bytes 196616 | tf_op jit(solution)/shard_map/ppermute | solution.py:32
  76.6 2.5 %collective-permute-done.22 = bf16[128,256]{1,0:T(8,128)(2,1)S(1)} collective-permute-done((bf16[128,256]{1,0:T(8,128)(2,1)S(1)}, bf16[128,256]{1,0:T(8,128)(2,1)S(1)}, u32[]{:S(2)}, u32[]{:S(2)}) %collective-permute-start.22) | collective-permute-done | bytes 65568 | tf_op jit(solution)/shard_map/ppermute | solution.py:32
  79.1 5.6 %collective-permute-start.23 = (bf16[128,256]{1,0:T(8,128)(2,1)S(1)}, bf16[128,256]{1,0:T(8,128)(2,1)S(1)}, u32[]{:S(2)}, u32[]{:S(2)}) collective-permute-start(bf16[128,256]{1,0:T(8,128)(2,1)S(1)} %add_convert_fusion.1), channel_id=1, source_target_pairs={{0,192},{16,208},{32,224},{48,240},{64,128},{80,144},{96,160},{112... | collective-permute-start | bytes 196616 | tf_op jit(solution)/shard_map/ppermute | solution.py:32
  84.7 1.9 %collective-permute-start.26 = (bf16[32,1024]{1,0:T(8,128)(2,1)S(1)}, bf16[32,1024]{1,0:T(8,128)(2,1)S(1)}, u32[]{:S(2)}, u32[]{:S(2)}) collective-permute-start(bf16[32,1024]{1,0:T(8,128)(2,1)S(1)} %get-tuple-element.109), channel_id=1, source_target_pairs={{0,12},{1,13},{2,14},{3,15},{4,8},{5,9},{6,10},{7,11},{8,4},{9,5},... | collective-permute-start | bytes 196616 | tf_op jit(solution)/shard_map/ppermute | solution.py:32
  86.6 0.9 collective-permute-done.23
  87.5 4.0 %collective-permute-start.24 = (bf16[128,256]{1,0:T(8,128)(2,1)S(1)}, bf16[128,256]{1,0:T(8,128)(2,1)S(1)}, u32[]{:S(2)}, u32[]{:S(2)}) collective-permute-start(bf16[128,256]{1,0:T(8,128)(2,1)S(1)} %add_convert_fusion.a), channel_id=1, source_target_pairs={{0,32},{16,48},{32,0},{48,16},{64,96},{80,112},{96,64},{112,80},{1... | collective-permute-start | bytes 196616 | tf_op jit(solution)/shard_map/ppermute | solution.py:32
  91.6 0.7 collective-permute-start.28
  92.2 2.1 %shard_map.97 = (bf16[256,1024]{1,0:T(8,128)(2,1)}, bf16[256,1024]{1,0:T(8,128)(2,1)}) custom-call(f32[256,1024]{1,0:T(8,128)S(1)} %get-tuple-element.106.gk_ref, f32[256,1024]{1,0:T(8,128)S(1)} %get-tuple-element.107.gv_ref, bf16[640,1024]{1,0:T(8,128)(2,1)S(1)} %collective-permute-done.17.rc_ref.r1, ...), custom_call_target="tpu_custom_call" | custom-call | flops 3000000000 | bytes 8000000 | tf_op jit(solution)/shard_map/pallas_call | solution.py:450
  94.3 1.5 %collective-permute-done.27.b = bf16[128,256]{1,0:T(8,128)(2,1)S(1)} collective-permute-done((bf16[128,256]{1,0:T(8,128)(2,1)S(1)}, bf16[128,256]{1,0:T(8,128)(2,1)S(1)}, u32[]{:S(2)}, u32[]{:S(2)}) %collective-permute-start.27) | collective-permute-done | bytes 65568 | tf_op jit(solution)/shard_map/ppermute | solution.py:32
  95.8 1.2 %collective-permute-done.28.d = bf16[128,256]{1,0:T(8,128)(2,1)S(1)} collective-permute-done((bf16[128,256]{1,0:T(8,128)(2,1)S(1)}, bf16[128,256]{1,0:T(8,128)(2,1)S(1)}, u32[]{:S(2)}, u32[]{:S(2)}) %collective-permute-start.28) | collective-permute-done | bytes 65568 | tf_op jit(solution)/shard_map/ppermute | solution.py:32
  97.0 0.8 shard_map.98
  (29 shorter events, 0.3 us)
Async XLA Ops:
  0.6 9.3 %copy-start.1 = (bf16[1,256,2048]{2,1,0:T(8,128)(2,1)S(1)}, bf16[1,256,2048]{2,1,0:T(8,128)(2,1)}, u32[]{:S(2)}) copy-start(bf16[1,256,2048]{2,1,0:T(8,128)(2,1)} %param.8) | copy-start | bytes 3145732
  0.6 1.1 %copy-start.2 = (bf16[1,256,1024]{2,1,0:T(8,128)(2,1)S(1)}, bf16[1,256,1024]{2,1,0:T(8,128)(2,1)}, u32[]{:S(2)}) copy-start(bf16[1,256,1024]{2,1,0:T(8,128)(2,1)} %param.6) | copy-start | bytes 1572868
  1.8 1.0 %copy-start.4 = (bf16[1,256,1024]{2,1,0:T(8,128)(2,1)S(1)}, bf16[1,256,1024]{2,1,0:T(8,128)(2,1)}, u32[]{:S(2)}) copy-start(bf16[1,256,1024]{2,1,0:T(8,128)(2,1)} %param.7) | copy-start | bytes 1572868
  3.9 11.4 %collective-permute-start.3 = (bf16[256,1024]{1,0:T(8,128)(2,1)S(1)}, bf16[256,1024]{1,0:T(8,128)(2,1)S(1)}, u32[]{:S(2)}, u32[]{:S(2)}) collective-permute-start(bf16[256,1024]{1,0:T(8,128)(2,1)S(1)} %get-tuple-element.62), channel_id=1, source_target_pairs={{0,1},{1,0},{2,3},{3,2},{4,5},{5,4},{6,7},{7,6},{8,9},{9,8},{10,11... | collective-permute-start | bytes 1572872 | tf_op jit(solution)/shard_map/ppermute | solution.py:32
  3.9 10.7 %collective-permute-start = (bf16[64,1024]{1,0:T(8,128)(2,1)S(1)}, bf16[64,1024]{1,0:T(8,128)(2,1)S(1)}, u32[]{:S(2)}, u32[]{:S(2)}) collective-permute-start(bf16[64,1024]{1,0:T(8,128)(2,1)S(1)} %get-tuple-element.59), channel_id=1, source_target_pairs={{0,4},{1,5},{2,6},{3,7},{4,0},{5,1},{6,2},{7,3},{8,12},{9,13},{10,... | collective-permute-start | bytes 393224 | tf_op jit(solution)/shard_map/ppermute | solution.py:32
  5.6 9.0 %collective-permute-start.2 = (bf16[32,1024]{1,0:T(8,128)(2,1)S(1)}, bf16[32,1024]{1,0:T(8,128)(2,1)S(1)}, u32[]{:S(2)}, u32[]{:S(2)}) collective-permute-start(bf16[32,1024]{1,0:T(8,128)(2,1)S(1)} %get-tuple-element.60), channel_id=1, source_target_pairs={{0,12},{1,13},{2,14},{3,15},{4,8},{5,9},{6,10},{7,11},{8,4},{9,5},... | collective-permute-start | bytes 196616 | tf_op jit(solution)/shard_map/ppermute | solution.py:32
  7.8 6.8 %collective-permute-start.1 = (bf16[32,1024]{1,0:T(8,128)(2,1)S(1)}, bf16[32,1024]{1,0:T(8,128)(2,1)S(1)}, u32[]{:S(2)}, u32[]{:S(2)}) collective-permute-start(bf16[32,1024]{1,0:T(8,128)(2,1)S(1)} %get-tuple-element.60), channel_id=1, source_target_pairs={{0,8},{1,9},{2,10},{3,11},{4,12},{5,13},{6,14},{7,15},{8,0},{9,1},... | collective-permute-start | bytes 196616 | tf_op jit(solution)/shard_map/ppermute | solution.py:32
  8.5 13.0 %collective-permute-start.4 = (bf16[128,1024]{1,0:T(8,128)(2,1)S(1)}, bf16[128,1024]{1,0:T(8,128)(2,1)S(1)}, u32[]{:S(2)}, u32[]{:S(2)}) collective-permute-start(bf16[128,1024]{1,0:T(8,128)(2,1)S(1)} %get-tuple-element.64), channel_id=1, source_target_pairs={{0,2},{1,3},{2,0},{3,1},{4,6},{5,7},{6,4},{7,5},{8,10},{9,11},{10,... | collective-permute-start | bytes 786440 | tf_op jit(solution)/shard_map/ppermute | solution.py:32
  10.0 2.2 %copy-start = (bf16[2048,1024]{1,0:T(8,128)(2,1)S(1)}, bf16[2048,1024]{1,0:T(8,128)(2,1)}, u32[]{:S(2)}) copy-start(bf16[2048,1024]{1,0:T(8,128)(2,1)} %w_ref.1) | copy-start | bytes 12582916
  12.2 3.2 %copy-start.6 = (bf16[1,256,1024]{2,1,0:T(8,128)(2,1)S(1)}, bf16[1,256,1024]{2,1,0:T(8,128)(2,1)}, u32[]{:S(2)}) copy-start(bf16[1,256,1024]{2,1,0:T(8,128)(2,1)} %param.5) | copy-start | bytes 1572868
  14.6 7.6 %collective-permute-start.5 = (bf16[128,1024]{1,0:T(8,128)(2,1)S(1)}, bf16[128,1024]{1,0:T(8,128)(2,1)S(1)}, u32[]{:S(2)}, u32[]{:S(2)}) collective-permute-start(bf16[128,1024]{1,0:T(8,128)(2,1)S(1)} %pad_maximum_fusion), channel_id=1, source_target_pairs={{0,2},{1,3},{2,0},{3,1},{4,6},{5,7},{6,4},{7,5},{8,10},{9,11},{10,... | collective-permute-start | bytes 786440 | tf_op jit(solution)/shard_map/ppermute | solution.py:32
  22.3 2.4 %collective-permute-start.6 = (bf16[384,1024]{1,0:T(8,128)(2,1)S(1)}, bf16[384,1024]{1,0:T(8,128)(2,1)S(1)}, u32[]{:S(2)}, u32[]{:S(2)}) collective-permute-start(bf16[384,1024]{1,0:T(8,128)(2,1)S(1)} %constant_dynamic-update-slice_fusion.u_ref), channel_id=1, source_target_pairs={{0,1},{1,0},{2,3},{3,2},{4,5},{5,4},{6,7},{7,6},{8,9},{9,8},{10,11... | collective-permute-start | bytes 2359304 | tf_op jit(solution)/shard_map/ppermute | solution.py:32
  22.7 6.3 %collective-permute-start.7 = (bf16[1024,256]{1,0:T(8,128)(2,1)S(1)}, bf16[1024,256]{1,0:T(8,128)(2,1)S(1)}, u32[]{:S(2)}, u32[]{:S(2)}) collective-permute-start(bf16[1024,256]{1,0:T(8,128)(2,1)S(1)} %get-tuple-element.76), channel_id=1, source_target_pairs={{0,1},{1,0},{2,3},{3,2},{4,5},{5,4},{6,7},{7,6},{8,9},{9,8},{10,11... | collective-permute-start | bytes 1572872 | tf_op jit(solution)/shard_map/ppermute | solution.py:32
  28.8 2.0 %collective-permute-start.8 = (bf16[256,1024]{1,0:T(8,128)(2,1)S(1)}, bf16[256,1024]{1,0:T(8,128)(2,1)S(1)}, u32[]{:S(2)}, u32[]{:S(2)}) collective-permute-start(bf16[256,1024]{1,0:T(8,128)(2,1)S(1)} %get-tuple-element.71.att_ref), channel_id=1, source_target_pairs={{0,1},{1,0},{2,3},{3,2},{4,5},{5,4},{6,7},{7,6},{8,9},{9,8},{10,11... | collective-permute-start | bytes 1572872 | tf_op jit(solution)/shard_map/ppermute | solution.py:32
  32.2 9.2 %collective-permute-start.9 = (bf16[256,512]{1,0:T(8,128)(2,1)S(1)}, bf16[256,512]{1,0:T(8,128)(2,1)S(1)}, u32[]{:S(2)}, u32[]{:S(2)}) collective-permute-start(bf16[256,512]{1,0:T(8,128)(2,1)S(1)} %get-tuple-element.78), channel_id=1, source_target_pairs={{0,4},{1,5},{2,6},{3,7},{4,0},{5,1},{6,2},{7,3},{8,12},{9,13},{10,... | collective-permute-start | bytes 786440 | tf_op jit(solution)/shard_map/ppermute | solution.py:32
  33.2 17.2 %collective-permute-start.10 = (bf16[256,512]{1,0:T(8,128)(2,1)S(1)}, bf16[256,512]{1,0:T(8,128)(2,1)S(1)}, u32[]{:S(2)}, u32[]{:S(2)}) collective-permute-start(bf16[256,512]{1,0:T(8,128)(2,1)S(1)} %get-tuple-element.79), channel_id=1, source_target_pairs={{0,12},{1,13},{2,14},{3,15},{4,8},{5,9},{6,10},{7,11},{8,4},{9,5},... | collective-permute-start | bytes 786440 | tf_op jit(solution)/shard_map/ppermute | solution.py:32
  35.3 15.0 %collective-permute-start.11 = (bf16[256,512]{1,0:T(8,128)(2,1)S(1)}, bf16[256,512]{1,0:T(8,128)(2,1)S(1)}, u32[]{:S(2)}, u32[]{:S(2)}) collective-permute-start(bf16[256,512]{1,0:T(8,128)(2,1)S(1)} %get-tuple-element.80), channel_id=1, source_target_pairs={{0,8},{1,9},{2,10},{3,11},{4,12},{5,13},{6,14},{7,15},{8,0},{9,1},... | collective-permute-start | bytes 786440 | tf_op jit(solution)/shard_map/ppermute | solution.py:32
  36.4 14.0 %collective-permute-start.12 = (bf16[1024,128]{1,0:T(8,128)(2,1)S(1)}, bf16[1024,128]{1,0:T(8,128)(2,1)S(1)}, u32[]{:S(2)}, u32[]{:S(2)}) collective-permute-start(bf16[1024,128]{1,0:T(8,128)(2,1)S(1)} %get-tuple-element.82), channel_id=1, source_target_pairs={{0,48},{16,32},{32,16},{48,0},{64,112},{80,96},{96,80},{112,64},{1... | collective-permute-start | bytes 786440 | tf_op jit(solution)/shard_map/ppermute | solution.py:32
  39.1 11.3 %collective-permute-start.13 = (bf16[1024,128]{1,0:T(8,128)(2,1)S(1)}, bf16[1024,128]{1,0:T(8,128)(2,1)S(1)}, u32[]{:S(2)}, u32[]{:S(2)}) collective-permute-start(bf16[1024,128]{1,0:T(8,128)(2,1)S(1)} %get-tuple-element.83), channel_id=1, source_target_pairs={{0,16},{16,0},{32,48},{48,32},{64,80},{80,64},{96,112},{112,96},{1... | collective-permute-start | bytes 786440 | tf_op jit(solution)/shard_map/ppermute | solution.py:32
  41.4 10.5 %collective-permute-start.14 = (bf16[1024,128]{1,0:T(8,128)(2,1)S(1)}, bf16[1024,128]{1,0:T(8,128)(2,1)S(1)}, u32[]{:S(2)}, u32[]{:S(2)}) collective-permute-start(bf16[1024,128]{1,0:T(8,128)(2,1)S(1)} %get-tuple-element.84), channel_id=1, source_target_pairs={{0,32},{16,48},{32,0},{48,16},{64,96},{80,112},{96,64},{112,80},{1... | collective-permute-start | bytes 786440 | tf_op jit(solution)/shard_map/ppermute | solution.py:32
  50.3 4.6 %copy-start.3 = (bf16[1,256,1024]{2,1,0:T(8,128)(2,1)S(1)}, bf16[1,256,1024]{2,1,0:T(8,128)(2,1)}, u32[]{:S(2)}) copy-start(bf16[1,256,1024]{2,1,0:T(8,128)(2,1)} %param.6) | copy-start | bytes 1572868
  50.3 4.6 %copy-start.5 = (bf16[1,256,1024]{2,1,0:T(8,128)(2,1)S(1)}, bf16[1,256,1024]{2,1,0:T(8,128)(2,1)}, u32[]{:S(2)}) copy-start(bf16[1,256,1024]{2,1,0:T(8,128)(2,1)} %param.7) | copy-start | bytes 1572868
  52.2 7.2 %collective-permute-start.17 = (bf16[640,1024]{1,0:T(8,128)(2,1)S(1)}, bf16[640,1024]{1,0:T(8,128)(2,1)S(1)}, u32[]{:S(2)}, u32[]{:S(2)}) collective-permute-start(bf16[640,1024]{1,0:T(8,128)(2,1)S(1)} %get-tuple-element.93), channel_id=1, source_target_pairs={{0,1},{1,0},{2,3},{3,2},{4,5},{5,4},{6,7},{7,6},{8,9},{9,8},{10,11... | collective-permute-start | bytes 3932168 | tf_op jit(solution)/shard_map/ppermute | solution.py:32
  52.3 6.9 %collective-permute-start.15 = (bf16[256,256]{1,0:T(8,128)(2,1)S(1)}, bf16[256,256]{1,0:T(8,128)(2,1)S(1)}, u32[]{:S(2)}, u32[]{:S(2)}) collective-permute-start(bf16[256,256]{1,0:T(8,128)(2,1)S(1)} %get-tuple-element.86), channel_id=1, source_target_pairs={{0,16},{16,0},{32,48},{48,32},{64,80},{80,64},{96,112},{112,96},{1... | collective-permute-start | bytes 393224 | tf_op jit(solution)/shard_map/ppermute | solution.py:32
  52.6 6.8 %collective-permute-start.16 = (bf16[512,128]{1,0:T(8,128)(2,1)S(1)}, bf16[512,128]{1,0:T(8,128)(2,1)S(1)}, u32[]{:S(2)}, u32[]{:S(2)}) collective-permute-start(bf16[512,128]{1,0:T(8,128)(2,1)S(1)} %get-tuple-element.88), channel_id=1, source_target_pairs={{0,12},{1,13},{2,14},{3,15},{4,8},{5,9},{6,10},{7,11},{8,4},{9,5},... | collective-permute-start | bytes 393224 | tf_op jit(solution)/shard_map/ppermute | solution.py:32
  59.6 13.7 %collective-permute-start.21 = (bf16[192,1024]{1,0:T(8,128)(2,1)S(1)}, bf16[192,1024]{1,0:T(8,128)(2,1)S(1)}, u32[]{:S(2)}, u32[]{:S(2)}) collective-permute-start(bf16[192,1024]{1,0:T(8,128)(2,1)S(1)} %get-tuple-element.104), channel_id=1, source_target_pairs={{0,2},{1,3},{2,0},{3,1},{4,6},{5,7},{6,4},{7,5},{8,10},{9,11},{10,... | collective-permute-start | bytes 1179656 | tf_op jit(solution)/shard_map/ppermute | solution.py:32
  60.8 6.0 %collective-permute-start.19 = (bf16[96,1024]{1,0:T(8,128)(2,1)S(1)}, bf16[96,1024]{1,0:T(8,128)(2,1)S(1)}, u32[]{:S(2)}, u32[]{:S(2)}) collective-permute-start(bf16[96,1024]{1,0:T(8,128)(2,1)S(1)} %get-tuple-element.97), channel_id=1, source_target_pairs={{0,4},{1,5},{2,6},{3,7},{4,0},{5,1},{6,2},{7,3},{8,12},{9,13},{10,... | collective-permute-start | bytes 589832 | tf_op jit(solution)/shard_map/ppermute | solution.py:32
  60.8 5.5 %collective-permute-start.18 = (bf16[256,128]{1,0:T(8,128)(2,1)S(1)}, bf16[256,128]{1,0:T(8,128)(2,1)S(1)}, u32[]{:S(2)}, u32[]{:S(2)}) collective-permute-start(bf16[256,128]{1,0:T(8,128)(2,1)S(1)} %get-tuple-element.95), channel_id=1, source_target_pairs={{0,48},{16,32},{32,16},{48,0},{64,112},{80,96},{96,80},{112,64},{1... | collective-permute-start | bytes 196616 | tf_op jit(solution)/shard_map/ppermute | solution.py:32
  66.9 6.3 %collective-permute-start.20 = (bf16[64,1024]{1,0:T(8,128)(2,1)S(1)}, bf16[64,1024]{1,0:T(8,128)(2,1)S(1)}, u32[]{:S(2)}, u32[]{:S(2)}) collective-permute-start(bf16[64,1024]{1,0:T(8,128)(2,1)S(1)} %get-tuple-element.100), channel_id=1, source_target_pairs={{0,2},{1,3},{2,0},{3,1},{4,6},{5,7},{6,4},{7,5},{8,10},{9,11},{10,... | collective-permute-start | bytes 393224 | tf_op jit(solution)/shard_map/ppermute | solution.py:32
  73.2 5.9 %collective-permute-start.22 = (bf16[128,256]{1,0:T(8,128)(2,1)S(1)}, bf16[128,256]{1,0:T(8,128)(2,1)S(1)}, u32[]{:S(2)}, u32[]{:S(2)}) collective-permute-start(bf16[128,256]{1,0:T(8,128)(2,1)S(1)} %get-tuple-element.105), channel_id=1, source_target_pairs={{0,64},{16,80},{32,96},{48,112},{64,0},{80,16},{96,32},{112,48},{1... | collective-permute-start | bytes 196616 | tf_op jit(solution)/shard_map/ppermute | solution.py:32
  79.1 8.4 %collective-permute-start.23 = (bf16[128,256]{1,0:T(8,128)(2,1)S(1)}, bf16[128,256]{1,0:T(8,128)(2,1)S(1)}, u32[]{:S(2)}, u32[]{:S(2)}) collective-permute-start(bf16[128,256]{1,0:T(8,128)(2,1)S(1)} %add_convert_fusion.1), channel_id=1, source_target_pairs={{0,192},{16,208},{32,224},{48,240},{64,128},{80,144},{96,160},{112... | collective-permute-start | bytes 196616 | tf_op jit(solution)/shard_map/ppermute | solution.py:32
  84.7 7.5 %collective-permute-start.26 = (bf16[32,1024]{1,0:T(8,128)(2,1)S(1)}, bf16[32,1024]{1,0:T(8,128)(2,1)S(1)}, u32[]{:S(2)}, u32[]{:S(2)}) collective-permute-start(bf16[32,1024]{1,0:T(8,128)(2,1)S(1)} %get-tuple-element.109), channel_id=1, source_target_pairs={{0,12},{1,13},{2,14},{3,15},{4,8},{5,9},{6,10},{7,11},{8,4},{9,5},... | collective-permute-start | bytes 196616 | tf_op jit(solution)/shard_map/ppermute | solution.py:32
  86.6 5.6 %collective-permute-start.25 = (bf16[64,1024]{1,0:T(8,128)(2,1)S(1)}, bf16[64,1024]{1,0:T(8,128)(2,1)S(1)}, u32[]{:S(2)}, u32[]{:S(2)}) collective-permute-start(bf16[64,1024]{1,0:T(8,128)(2,1)S(1)} %shard_map.96), channel_id=1, source_target_pairs={{0,4},{1,5},{2,6},{3,7},{4,0},{5,1},{6,2},{7,3},{8,12},{9,13},{10,... | collective-permute-start | bytes 393224 | tf_op jit(solution)/shard_map/ppermute | solution.py:32
  87.5 6.8 %collective-permute-start.24 = (bf16[128,256]{1,0:T(8,128)(2,1)S(1)}, bf16[128,256]{1,0:T(8,128)(2,1)S(1)}, u32[]{:S(2)}, u32[]{:S(2)}) collective-permute-start(bf16[128,256]{1,0:T(8,128)(2,1)S(1)} %add_convert_fusion.a), channel_id=1, source_target_pairs={{0,32},{16,48},{32,0},{48,16},{64,96},{80,112},{96,64},{112,80},{1... | collective-permute-start | bytes 196616 | tf_op jit(solution)/shard_map/ppermute | solution.py:32
  91.6 4.3 %collective-permute-start.27 = (bf16[128,256]{1,0:T(8,128)(2,1)S(1)}, bf16[128,256]{1,0:T(8,128)(2,1)S(1)}, u32[]{:S(2)}, u32[]{:S(2)}) collective-permute-start(bf16[128,256]{1,0:T(8,128)(2,1)S(1)} %add_convert_fusion.a), channel_id=1, source_target_pairs={{0,16},{16,0},{32,48},{48,32},{64,80},{80,64},{96,112},{112,96},{1... | collective-permute-start | bytes 196616 | tf_op jit(solution)/shard_map/ppermute | solution.py:32
  91.6 5.5 %collective-permute-start.28 = (bf16[128,256]{1,0:T(8,128)(2,1)S(1)}, bf16[128,256]{1,0:T(8,128)(2,1)S(1)}, u32[]{:S(2)}, u32[]{:S(2)}) collective-permute-start(bf16[128,256]{1,0:T(8,128)(2,1)S(1)} %add_convert_fusion.a), channel_id=1, source_target_pairs={{0,48},{16,32},{32,16},{48,0},{64,112},{80,96},{96,80},{112,64},{1... | collective-permute-start | bytes 196616 | tf_op jit(solution)/shard_map/ppermute | solution.py:32

commit v5 on v4

--- a/solution.py
+++ b/solution.py
@@ -19,7 +19,6 @@
 SPANS = {2: ((0, 64),), 3: ((128, 32), (256, 32)), 4: ((192, 16), (224, 16), (320, 16), (352, 16))}
 BF = jnp.bfloat16
 F32 = jnp.float32
-VMEM = pltpu.CompilerParams(vmem_limit_bytes=16 * 1024 * 1024)
 
 CORE, ZLO, Y1, Y2, Y3 = 1, 2, 4, 8, 12
 X1, X2, X3, ZH1, ZH3 = 1, 2, 3, 4, 12
@@ -339,9 +338,10 @@
     return pl.BlockSpec((rows, cols), lambda i: (0, 0))
 
 
-def call(kernel, out, flops=1, moved=1, **kw):
+def call(kernel, out, flops=1, moved=1, vmem=16, **kw):
     cost = pl.CostEstimate(flops=int(flops), bytes_accessed=int(moved), transcendentals=0)
-    return pl.pallas_call(kernel, out_shape=out, compiler_params=VMEM, cost_estimate=cost, **kw)
+    params = pltpu.CompilerParams(vmem_limit_bytes=vmem * 1024 * 1024)
+    return pl.pallas_call(kernel, out_shape=out, compiler_params=params, cost_estimate=cost, **kw)
 
 
 def per_device(queries, keys, values, d_out, w_out):
@@ -390,9 +390,9 @@
     att, lse = call(
         forward_kernel,
         [shape(ROWS, WIDTH), shape(ROWS, WIDTH, F32)],
-        grid=grid,
-        in_specs=[hs(4 * ROWS), hs(384), hs(384)] + [hs(ROWS)] * 3,
-        out_specs=[hs(ROWS), hs(ROWS)],
+        grid=(2,),
+        in_specs=[by_heads(n, 512) for n in (4 * ROWS, 384, 384, ROWS, ROWS, ROWS)],
+        out_specs=[by_heads(ROWS, 512)] * 2,
     )(qx, u, e, n0, m0, l0)
 
     attp = swap(att, "seq", CORE)
@@ -424,9 +424,9 @@
         flops=5e9,
         moved=15e6,
         out=[shape(ROWS, WIDTH)] + [shape(ROWS, WIDTH, F32)] * 2,
-        grid=grid,
-        in_specs=[hs(ROWS)] * 7,
-        out_specs=[hs(ROWS)] * 3,
+        grid=(2,),
+        in_specs=[by_heads(ROWS, 512)] * 7,
+        out_specs=[by_heads(ROWS, 512)] * 3,
     )(q, k, v, datt, att, lse, gq)
     keep, gk0 = lax.optimization_barrier((keep, gk0))
     keep_x, next_x, keep_y, next_y, out_z, b3, b4 = call(

time: 98 us -> 97.4 us (level)
  Pallas kernels: 29.1 us -> 27.8 us
  transfers between devices with their start and end apart: 29 -> 29, of which waited for: 13 -> 13; matrix products, arithmetic and copies ran while one was open for 0% -> 0% of each run, Pallas kernels for 26% -> 25%
where the time goes in v5:
time: 97.4 us; the launch traced here: 96.9 us
  starting transfers between devices  40.9 us (42%)
  Pallas kernels  27.8 us (29%)
  waiting for transfers between devices  22.8 us (23%)
  local copies, waits for them, and re-layouts  4.43 us (5%)
    ppermute x29, starting transfers between devices, swap(): return lax.ppermute(value, axis, pairs)  40.9 us
    ppermute x29, waiting for transfers between devices, swap(): return lax.ppermute(value, axis, pairs)  22.8 us
    pallas_call x1, Pallas kernels, per_device(): call(local_kernel, flops=8000000000.0, moved=20000000.0, out=[shape(4 * R...  6.17 us
    pallas_call x1, Pallas kernels, per_device(): call(back_kernel, [shape(640, WIDTH), shape(384, WIDTH, F32), shape(ROWS,...  5.89 us
    unnamed x16, local copies, waits for them, and re-layouts  4.41 us
    pallas_call x1, Pallas kernels, per_device(): call(forward_kernel, [shape(ROWS, WIDTH), shape(ROWS, WIDTH, F32)], grid=...  3.56 us
    pallas_call x1, Pallas kernels, per_device(): call(local_back_kernel, flops=5000000000.0, moved=15000000.0, out=[shape(...  3.5 us
    pallas_call x1, Pallas kernels, per_device(): call(project_kernel, shape(ROWS, WIDTH), grid=grid, in_specs=[whole(ROWS,...  2.42 us
  transfers between devices with their start and end apart: 29, of which 13 were waited for; matrix products, arithmetic and copies ran while one was open for 0% of the time, Pallas kernels for 25%

profile of v5, /device:TPU:32, one launch (start us, length us, event | category | flops | bytes accessed | tf_op | source)
XLA Modules:
  0.0 96.9 jit_solution(6359168001622666612)
XLA Ops:
  0.6 0.0 copy-start.2
  0.7 1.1 %copy-done.2 = bf16[1,256,1024]{2,1,0:T(8,128)(2,1)S(1)} copy-done((bf16[1,256,1024]{2,1,0:T(8,128)(2,1)S(1)}, bf16[1,256,1024]{2,1,0:T(8,128)(2,1)}, u32[]{:S(2)}) %copy-start.2) | copy-done | bytes 524312
  1.8 1.0 %copy-done.4 = bf16[1,256,1024]{2,1,0:T(8,128)(2,1)S(1)} copy-done((bf16[1,256,1024]{2,1,0:T(8,128)(2,1)S(1)}, bf16[1,256,1024]{2,1,0:T(8,128)(2,1)}, u32[]{:S(2)}) %copy-start.4) | copy-done | bytes 524312
  2.8 1.1 %shard_map.84 = (bf16[256,1024]{1,0:T(8,128)(2,1)S(1)}, bf16[128,1024]{1,0:T(8,128)(2,1)S(1)}, bf16[64,1024]{1,0:T(8,128)(2,1)S(1)}, bf16[32,1024]{1,0:T(8,128)(2,1)S(1)}) custom-call(bf16[256,1024]{1,0:T(8,128)(2,1)S(1)} %bitcast.9, bf16[256,1024]{1,0:T(8,128)(2,1)S(1)} %bitcast.12), custom_call_target="tpu_custom_call" | custom-call | flops 1 | bytes 1 | tf_op jit(solution)/shard_map/pallas_call | solution.py:353
  3.9 1.7 %collective-permute-start = (bf16[64,1024]{1,0:T(8,128)(2,1)S(1)}, bf16[64,1024]{1,0:T(8,128)(2,1)S(1)}, u32[]{:S(2)}, u32[]{:S(2)}) collective-permute-start(bf16[64,1024]{1,0:T(8,128)(2,1)S(1)} %get-tuple-element.59), channel_id=1, source_target_pairs={{0,4},{1,5},{2,6},{3,7},{4,0},{5,1},{6,2},{7,3},{8,12},{9,13},{10,... | collective-permute-start | bytes 393224 | tf_op jit(solution)/shard_map/ppermute | solution.py:31
  5.6 2.2 %collective-permute-start.2 = (bf16[32,1024]{1,0:T(8,128)(2,1)S(1)}, bf16[32,1024]{1,0:T(8,128)(2,1)S(1)}, u32[]{:S(2)}, u32[]{:S(2)}) collective-permute-start(bf16[32,1024]{1,0:T(8,128)(2,1)S(1)} %get-tuple-element.60), channel_id=1, source_target_pairs={{0,12},{1,13},{2,14},{3,15},{4,8},{5,9},{6,10},{7,11},{8,4},{9,5},... | collective-permute-start | bytes 196616 | tf_op jit(solution)/shard_map/ppermute | solution.py:31
  7.8 0.7 collective-permute-start.1
  8.5 1.5 %collective-permute-start.4 = (bf16[128,1024]{1,0:T(8,128)(2,1)S(1)}, bf16[128,1024]{1,0:T(8,128)(2,1)S(1)}, u32[]{:S(2)}, u32[]{:S(2)}) collective-permute-start(bf16[128,1024]{1,0:T(8,128)(2,1)S(1)} %get-tuple-element.64), channel_id=1, source_target_pairs={{0,2},{1,3},{2,0},{3,1},{4,6},{5,7},{6,4},{7,5},{8,10},{9,11},{10,... | collective-permute-start | bytes 786440 | tf_op jit(solution)/shard_map/ppermute | solution.py:31
  10.0 2.2 %copy-done = bf16[2048,1024]{1,0:T(8,128)(2,1)S(1)} copy-done((bf16[2048,1024]{1,0:T(8,128)(2,1)S(1)}, bf16[2048,1024]{1,0:T(8,128)(2,1)}, u32[]{:S(2)}) %copy-start) | copy-done | bytes 4194328
  12.2 2.4 %shard_map.85.datt_ref = bf16[256,1024]{1,0:T(8,128)(2,1)S(1)} custom-call(bf16[256,2048]{1,0:T(8,128)(2,1)S(1)} %bitcast.7, bf16[2048,1024]{1,0:T(8,128)(2,1)S(1)} %copy-done), custom_call_target="tpu_custom_call" | custom-call | flops 1 | bytes 1 | tf_op jit(solution)/shard_map/pallas_call | solution.py:363
  14.6 0.0 collective-permute-done.2
  14.6 0.0 collective-permute-done.1
  14.6 0.7 collective-permute-start.5
  15.3 6.2 %shard_map.86 = (bf16[1024,1024]{1,0:T(8,128)(2,1)S(1)}, f32[256,1024]{1,0:T(8,128)S(1)}, f32[256,1024]{1,0:T(8,128)S(1)}, f32[256,1024]{1,0:T(8,128)S(1)}) custom-call(bf16[256,1024]{1,0:T(8,128)(2,1)S(1)} %bitcast.15, bf16[256,1024]{1,0:T(8,128)(2,1)S(1)} %bitcast.10, bf16[256,1024]{1,0:T(8,128)(2,1)S(1)} %bitcast.13, ...), custom_call_target="tpu_custom_call" | custom-call | flops 8000000000 | bytes 20000000 | tf_op jit(solution)/shard_map/pallas_call | solution.py:372
  21.5 0.0 collective-permute-done.4
  21.6 0.7 collective-permute-done.5
  22.3 0.1 collective-permute-start.6
  22.4 0.3 shard_map.90
  22.7 0.6 collective-permute-start.7
  23.3 1.4 %collective-permute-done.6.e_ref = bf16[384,1024]{1,0:T(8,128)(2,1)S(1)} collective-permute-done((bf16[384,1024]{1,0:T(8,128)(2,1)S(1)}, bf16[384,1024]{1,0:T(8,128)(2,1)S(1)}, u32[]{:S(2)}, u32[]{:S(2)}) %collective-permute-start.6) | collective-permute-done | bytes 786464 | tf_op jit(solution)/shard_map/ppermute | solution.py:31
  24.7 3.6 %shard_map.87 = (bf16[256,1024]{1,0:T(8,128)(2,1)S(1)}, f32[256,1024]{1,0:T(8,128)S(1)}) custom-call(bf16[1024,1024]{1,0:T(8,128)(2,1)S(1)} %get-tuple-element.63.qx_ref, bf16[384,1024]{1,0:T(8,128)(2,1)S(1)} %constant_dynamic-update-slice_fusion.u_ref, bf16[384,1024]{1,0:T(8,128)(2,1)S(1)} %collective-permute-done.6.e_ref, ...), custom_call_target="tpu_custom_call" | custom-call | flops 1 | bytes 1 | tf_op jit(solution)/shard_map/pallas_call | solution.py:390
  28.2 0.2 collective-permute-start.8
  28.5 1.8 %collective-permute-done.8.attp_ref = bf16[256,1024]{1,0:T(8,128)(2,1)S(1)} collective-permute-done((bf16[256,1024]{1,0:T(8,128)(2,1)S(1)}, bf16[256,1024]{1,0:T(8,128)(2,1)S(1)}, u32[]{:S(2)}, u32[]{:S(2)}) %collective-permute-start.8) | collective-permute-done | bytes 524320 | tf_op jit(solution)/shard_map/ppermute | solution.py:31
  30.2 1.4 %shard_map.91 = (bf16[256,512]{1,0:T(8,128)(2,1)S(1)}, bf16[256,512]{1,0:T(8,128)(2,1)S(1)}, bf16[256,512]{1,0:T(8,128)(2,1)S(1)}, bf16[256,512]{1,0:T(8,128)(2,...) custom-call(bf16[1024,256]{1,0:T(8,128)(2,1)S(1)} %get-tuple-element, ...), custom_call_target="tpu_custom_call" | custom-call | flops 1 | bytes 1 | tf_op jit(solution)/shard_map/pallas_call | solution.py:399
  31.6 1.0 collective-permute-start.9
  32.6 2.2 %collective-permute-start.10 = (bf16[256,512]{1,0:T(8,128)(2,1)S(1)}, bf16[256,512]{1,0:T(8,128)(2,1)S(1)}, u32[]{:S(2)}, u32[]{:S(2)}) collective-permute-start(bf16[256,512]{1,0:T(8,128)(2,1)S(1)} %get-tuple-element.79), channel_id=1, source_target_pairs={{0,12},{1,13},{2,14},{3,15},{4,8},{5,9},{6,10},{7,11},{8,4},{9,5},... | collective-permute-start | bytes 786440 | tf_op jit(solution)/shard_map/ppermute | solution.py:31
  34.8 1.0 %collective-permute-start.11 = (bf16[256,512]{1,0:T(8,128)(2,1)S(1)}, bf16[256,512]{1,0:T(8,128)(2,1)S(1)}, u32[]{:S(2)}, u32[]{:S(2)}) collective-permute-start(bf16[256,512]{1,0:T(8,128)(2,1)S(1)} %get-tuple-element.80), channel_id=1, source_target_pairs={{0,8},{1,9},{2,10},{3,11},{4,12},{5,13},{6,14},{7,15},{8,0},{9,1},... | collective-permute-start | bytes 786440 | tf_op jit(solution)/shard_map/ppermute | solution.py:31
  35.8 2.7 %collective-permute-start.12 = (bf16[1024,128]{1,0:T(8,128)(2,1)S(1)}, bf16[1024,128]{1,0:T(8,128)(2,1)S(1)}, u32[]{:S(2)}, u32[]{:S(2)}) collective-permute-start(bf16[1024,128]{1,0:T(8,128)(2,1)S(1)} %get-tuple-element.82), channel_id=1, source_target_pairs={{0,48},{16,32},{32,16},{48,0},{64,112},{80,96},{96,80},{112,64},{1... | collective-permute-start | bytes 786440 | tf_op jit(solution)/shard_map/ppermute | solution.py:31
  38.5 0.2 collective-permute-start.13
  38.8 2.1 %collective-permute-done.9.refs_1_ = bf16[256,512]{1,0:T(8,128)(2,1)S(1)} collective-permute-done((bf16[256,512]{1,0:T(8,128)(2,1)S(1)}, bf16[256,512]{1,0:T(8,128)(2,1)S(1)}, u32[]{:S(2)}, u32[]{:S(2)}) %collective-permute-start.9) | collective-permute-done | bytes 262176 | tf_op jit(solution)/shard_map/ppermute | solution.py:31
  40.9 3.0 %collective-permute-start.14 = (bf16[1024,128]{1,0:T(8,128)(2,1)S(1)}, bf16[1024,128]{1,0:T(8,128)(2,1)S(1)}, u32[]{:S(2)}, u32[]{:S(2)}) collective-permute-start(bf16[1024,128]{1,0:T(8,128)(2,1)S(1)} %get-tuple-element.84), channel_id=1, source_target_pairs={{0,32},{16,48},{32,0},{48,16},{64,96},{80,112},{96,64},{112,80},{1... | collective-permute-start | bytes 786440 | tf_op jit(solution)/shard_map/ppermute | solution.py:31
  43.9 5.9 %shard_map.88 = (bf16[640,1024]{1,0:T(8,128)(2,1)S(1)}, f32[384,1024]{1,0:T(8,128)S(1)}, f32[256,1024]{1,0:T(8,128)S(1)}) custom-call(bf16[1024,1024]{1,0:T(8,128)(2,1)S(1)} %get-tuple-element.63.qx_ref, bf16[256,1024]{1,0:T(8,128)(2,1)S(1)} %collective-permute-done.3.a_ref, bf16[384,1024]{1,0:T(8,128)(2,1)S(1)} %constant_dynamic-update-slice_fusion.u_ref, ...), custom_call_target="tpu_custom_call" | custom-call | flops 1 | bytes 1 | tf_op jit(solution)/shard_map/pallas_call | solution.py:411
  49.8 0.0 copy-start.3
  49.8 0.0 copy-start.5
  49.8 0.0 collective-permute-done.11.refs_3_
  49.8 1.5 %collective-permute-done.14.refs_7_ = bf16[1024,128]{1,0:T(8,128)(2,1)S(1)} collective-permute-done((bf16[1024,128]{1,0:T(8,128)(2,1)S(1)}, bf16[1024,128]{1,0:T(8,128)(2,1)S(1)}, u32[]{:S(2)}, u32[]{:S(2)}) %collective-permute-start.14) | collective-permute-done | bytes 262176 | tf_op jit(solution)/shard_map/ppermute | solution.py:31
  51.3 0.2 shard_map.92
  51.6 0.1 collective-permute-start.17
  51.7 0.3 collective-permute-start.15
  52.0 2.3 %collective-permute-start.16 = (bf16[512,128]{1,0:T(8,128)(2,1)S(1)}, bf16[512,128]{1,0:T(8,128)(2,1)S(1)}, u32[]{:S(2)}, u32[]{:S(2)}) collective-permute-start(bf16[512,128]{1,0:T(8,128)(2,1)S(1)} %get-tuple-element.88), channel_id=1, source_target_pairs={{0,12},{1,13},{2,14},{3,15},{4,8},{5,9},{6,10},{7,11},{8,4},{9,5},... | collective-permute-start | bytes 393224 | tf_op jit(solution)/shard_map/ppermute | solution.py:31
  54.4 3.5 %shard_map.89 = (bf16[256,1024]{1,0:T(8,128)(2,1)}, f32[256,1024]{1,0:T(8,128)S(1)}, f32[256,1024]{1,0:T(8,128)S(1)}) custom-call(bf16[256,1024]{1,0:T(8,128)(2,1)S(1)} %bitcast.16, bf16[256,1024]{1,0:T(8,128)(2,1)S(1)} %bitcast.11, bf16[256,1024]{1,0:T(8,128)(2,1)S(1)} %bitcast.14, bf16[256,1024]{1,0:T(8,128)(2,1)S(1)} %shard_map.85.datt_ref, ...), custom_call_target="tpu_custom_call" | custom-call | flops 5000000000 | bytes 15000000 | tf_op jit(solution)/shard_map/pallas_call | solution.py:422
  57.9 0.9 collective-permute-done.16.got_y
  58.8 0.0 collective-permute-done.17.rc_ref.r1
  58.8 0.2 shard_map.93
  59.0 1.2 %collective-permute-start.21 = (bf16[192,1024]{1,0:T(8,128)(2,1)S(1)}, bf16[192,1024]{1,0:T(8,128)(2,1)S(1)}, u32[]{:S(2)}, u32[]{:S(2)}) collective-permute-start(bf16[192,1024]{1,0:T(8,128)(2,1)S(1)} %get-tuple-element.104), channel_id=1, source_target_pairs={{0,2},{1,3},{2,0},{3,1},{4,6},{5,7},{6,4},{7,5},{8,10},{9,11},{10,... | collective-permute-start | bytes 1179656 | tf_op jit(solution)/shard_map/ppermute | solution.py:31
  60.2 0.0 collective-permute-start.19
  60.2 2.5 %collective-permute-start.18 = (bf16[256,128]{1,0:T(8,128)(2,1)S(1)}, bf16[256,128]{1,0:T(8,128)(2,1)S(1)}, u32[]{:S(2)}, u32[]{:S(2)}) collective-permute-start(bf16[256,128]{1,0:T(8,128)(2,1)S(1)} %get-tuple-element.95), channel_id=1, source_target_pairs={{0,48},{16,32},{32,16},{48,0},{64,112},{80,96},{96,80},{112,64},{1... | collective-permute-start | bytes 196616 | tf_op jit(solution)/shard_map/ppermute | solution.py:31
  62.7 3.0 %collective-permute-done.18.got_x = bf16[256,128]{1,0:T(8,128)(2,1)S(1)} collective-permute-done((bf16[256,128]{1,0:T(8,128)(2,1)S(1)}, bf16[256,128]{1,0:T(8,128)(2,1)S(1)}, u32[]{:S(2)}, u32[]{:S(2)}) %collective-permute-start.18) | collective-permute-done | bytes 65568 | tf_op jit(solution)/shard_map/ppermute | solution.py:31
  65.7 0.6 collective-permute-done.19.got_y
  66.3 0.8 collective-permute-start.20
  67.1 5.1 %collective-permute-done.20.got_ref = bf16[64,1024]{1,0:T(8,128)(2,1)S(1)} collective-permute-done((bf16[64,1024]{1,0:T(8,128)(2,1)S(1)}, bf16[64,1024]{1,0:T(8,128)(2,1)S(1)}, u32[]{:S(2)}, u32[]{:S(2)}) %collective-permute-start.20) | collective-permute-done | bytes 131104 | tf_op jit(solution)/shard_map/ppermute | solution.py:31
  72.3 0.0 collective-permute-done.21.got_ref.r2
  72.3 3.3 %collective-permute-start.22 = (bf16[128,256]{1,0:T(8,128)(2,1)S(1)}, bf16[128,256]{1,0:T(8,128)(2,1)S(1)}, u32[]{:S(2)}, u32[]{:S(2)}) collective-permute-start(bf16[128,256]{1,0:T(8,128)(2,1)S(1)} %get-tuple-element.105), channel_id=1, source_target_pairs={{0,64},{16,80},{32,96},{48,112},{64,0},{80,16},{96,32},{112,48},{1... | collective-permute-start | bytes 196616 | tf_op jit(solution)/shard_map/ppermute | solution.py:31
  75.6 2.5 %collective-permute-done.22 = bf16[128,256]{1,0:T(8,128)(2,1)S(1)} collective-permute-done((bf16[128,256]{1,0:T(8,128)(2,1)S(1)}, bf16[128,256]{1,0:T(8,128)(2,1)S(1)}, u32[]{:S(2)}, u32[]{:S(2)}) %collective-permute-start.22) | collective-permute-done | bytes 65568 | tf_op jit(solution)/shard_map/ppermute | solution.py:31
  78.2 5.6 %collective-permute-start.23 = (bf16[128,256]{1,0:T(8,128)(2,1)S(1)}, bf16[128,256]{1,0:T(8,128)(2,1)S(1)}, u32[]{:S(2)}, u32[]{:S(2)}) collective-permute-start(bf16[128,256]{1,0:T(8,128)(2,1)S(1)} %add_convert_fusion.1), channel_id=1, source_target_pairs={{0,192},{16,208},{32,224},{48,240},{64,128},{80,144},{96,160},{112... | collective-permute-start | bytes 196616 | tf_op jit(solution)/shard_map/ppermute | solution.py:31
  83.7 2.3 %collective-permute-start.26 = (bf16[32,1024]{1,0:T(8,128)(2,1)S(1)}, bf16[32,1024]{1,0:T(8,128)(2,1)S(1)}, u32[]{:S(2)}, u32[]{:S(2)}) collective-permute-start(bf16[32,1024]{1,0:T(8,128)(2,1)S(1)} %get-tuple-element.109), channel_id=1, source_target_pairs={{0,12},{1,13},{2,14},{3,15},{4,8},{5,9},{6,10},{7,11},{8,4},{9,5},... | collective-permute-start | bytes 196616 | tf_op jit(solution)/shard_map/ppermute | solution.py:31
  86.1 0.4 collective-permute-done.23
  86.5 4.0 %collective-permute-start.24 = (bf16[128,256]{1,0:T(8,128)(2,1)S(1)}, bf16[128,256]{1,0:T(8,128)(2,1)S(1)}, u32[]{:S(2)}, u32[]{:S(2)}) collective-permute-start(bf16[128,256]{1,0:T(8,128)(2,1)S(1)} %add_convert_fusion.a), channel_id=1, source_target_pairs={{0,32},{16,48},{32,0},{48,16},{64,96},{80,112},{96,64},{112,80},{1... | collective-permute-start | bytes 196616 | tf_op jit(solution)/shard_map/ppermute | solution.py:31
  90.6 0.7 collective-permute-start.28
  91.2 0.0 collective-permute-done.26.r4
  91.2 2.1 %shard_map.97 = (bf16[256,1024]{1,0:T(8,128)(2,1)}, bf16[256,1024]{1,0:T(8,128)(2,1)}) custom-call(f32[256,1024]{1,0:T(8,128)S(1)} %get-tuple-element.106.gk_ref, f32[256,1024]{1,0:T(8,128)S(1)} %get-tuple-element.107.gv_ref, bf16[640,1024]{1,0:T(8,128)(2,1)S(1)} %collective-permute-done.17.rc_ref.r1, ...), custom_call_target="tpu_custom_call" | custom-call | flops 3000000000 | bytes 8000000 | tf_op jit(solution)/shard_map/pallas_call | solution.py:450
  93.3 1.5 %collective-permute-done.27.b = bf16[128,256]{1,0:T(8,128)(2,1)S(1)} collective-permute-done((bf16[128,256]{1,0:T(8,128)(2,1)S(1)}, bf16[128,256]{1,0:T(8,128)(2,1)S(1)}, u32[]{:S(2)}, u32[]{:S(2)}) %collective-permute-start.27) | collective-permute-done | bytes 65568 | tf_op jit(solution)/shard_map/ppermute | solution.py:31
  94.8 1.2 %collective-permute-done.28.d = bf16[128,256]{1,0:T(8,128)(2,1)S(1)} collective-permute-done((bf16[128,256]{1,0:T(8,128)(2,1)S(1)}, bf16[128,256]{1,0:T(8,128)(2,1)S(1)}, u32[]{:S(2)}, u32[]{:S(2)}) %collective-permute-start.28) | collective-permute-done | bytes 65568 | tf_op jit(solution)/shard_map/ppermute | solution.py:31
  96.1 0.8 shard_map.98
  (29 shorter events, 0.3 us)
Async XLA Ops:
  0.6 9.3 %copy-start.1 = (bf16[1,256,2048]{2,1,0:T(8,128)(2,1)S(1)}, bf16[1,256,2048]{2,1,0:T(8,128)(2,1)}, u32[]{:S(2)}) copy-start(bf16[1,256,2048]{2,1,0:T(8,128)(2,1)} %param.8) | copy-start | bytes 3145732
  0.6 1.1 %copy-start.2 = (bf16[1,256,1024]{2,1,0:T(8,128)(2,1)S(1)}, bf16[1,256,1024]{2,1,0:T(8,128)(2,1)}, u32[]{:S(2)}) copy-start(bf16[1,256,1024]{2,1,0:T(8,128)(2,1)} %param.6) | copy-start | bytes 1572868
  1.8 1.0 %copy-start.4 = (bf16[1,256,1024]{2,1,0:T(8,128)(2,1)S(1)}, bf16[1,256,1024]{2,1,0:T(8,128)(2,1)}, u32[]{:S(2)}) copy-start(bf16[1,256,1024]{2,1,0:T(8,128)(2,1)} %param.7) | copy-start | bytes 1572868
  3.9 11.4 %collective-permute-start.3 = (bf16[256,1024]{1,0:T(8,128)(2,1)S(1)}, bf16[256,1024]{1,0:T(8,128)(2,1)S(1)}, u32[]{:S(2)}, u32[]{:S(2)}) collective-permute-start(bf16[256,1024]{1,0:T(8,128)(2,1)S(1)} %get-tuple-element.62), channel_id=1, source_target_pairs={{0,1},{1,0},{2,3},{3,2},{4,5},{5,4},{6,7},{7,6},{8,9},{9,8},{10,11... | collective-permute-start | bytes 1572872 | tf_op jit(solution)/shard_map/ppermute | solution.py:31
  3.9 10.7 %collective-permute-start = (bf16[64,1024]{1,0:T(8,128)(2,1)S(1)}, bf16[64,1024]{1,0:T(8,128)(2,1)S(1)}, u32[]{:S(2)}, u32[]{:S(2)}) collective-permute-start(bf16[64,1024]{1,0:T(8,128)(2,1)S(1)} %get-tuple-element.59), channel_id=1, source_target_pairs={{0,4},{1,5},{2,6},{3,7},{4,0},{5,1},{6,2},{7,3},{8,12},{9,13},{10,... | collective-permute-start | bytes 393224 | tf_op jit(solution)/shard_map/ppermute | solution.py:31
  5.6 9.0 %collective-permute-start.2 = (bf16[32,1024]{1,0:T(8,128)(2,1)S(1)}, bf16[32,1024]{1,0:T(8,128)(2,1)S(1)}, u32[]{:S(2)}, u32[]{:S(2)}) collective-permute-start(bf16[32,1024]{1,0:T(8,128)(2,1)S(1)} %get-tuple-element.60), channel_id=1, source_target_pairs={{0,12},{1,13},{2,14},{3,15},{4,8},{5,9},{6,10},{7,11},{8,4},{9,5},... | collective-permute-start | bytes 196616 | tf_op jit(solution)/shard_map/ppermute | solution.py:31
  7.8 6.8 %collective-permute-start.1 = (bf16[32,1024]{1,0:T(8,128)(2,1)S(1)}, bf16[32,1024]{1,0:T(8,128)(2,1)S(1)}, u32[]{:S(2)}, u32[]{:S(2)}) collective-permute-start(bf16[32,1024]{1,0:T(8,128)(2,1)S(1)} %get-tuple-element.60), channel_id=1, source_target_pairs={{0,8},{1,9},{2,10},{3,11},{4,12},{5,13},{6,14},{7,15},{8,0},{9,1},... | collective-permute-start | bytes 196616 | tf_op jit(solution)/shard_map/ppermute | solution.py:31
  8.5 13.0 %collective-permute-start.4 = (bf16[128,1024]{1,0:T(8,128)(2,1)S(1)}, bf16[128,1024]{1,0:T(8,128)(2,1)S(1)}, u32[]{:S(2)}, u32[]{:S(2)}) collective-permute-start(bf16[128,1024]{1,0:T(8,128)(2,1)S(1)} %get-tuple-element.64), channel_id=1, source_target_pairs={{0,2},{1,3},{2,0},{3,1},{4,6},{5,7},{6,4},{7,5},{8,10},{9,11},{10,... | collective-permute-start | bytes 786440 | tf_op jit(solution)/shard_map/ppermute | solution.py:31
  10.0 2.2 %copy-start = (bf16[2048,1024]{1,0:T(8,128)(2,1)S(1)}, bf16[2048,1024]{1,0:T(8,128)(2,1)}, u32[]{:S(2)}) copy-start(bf16[2048,1024]{1,0:T(8,128)(2,1)} %w_ref.1) | copy-start | bytes 12582916
  12.2 3.2 %copy-start.6 = (bf16[1,256,1024]{2,1,0:T(8,128)(2,1)S(1)}, bf16[1,256,1024]{2,1,0:T(8,128)(2,1)}, u32[]{:S(2)}) copy-start(bf16[1,256,1024]{2,1,0:T(8,128)(2,1)} %param.5) | copy-start | bytes 1572868
  14.6 7.6 %collective-permute-start.5 = (bf16[128,1024]{1,0:T(8,128)(2,1)S(1)}, bf16[128,1024]{1,0:T(8,128)(2,1)S(1)}, u32[]{:S(2)}, u32[]{:S(2)}) collective-permute-start(bf16[128,1024]{1,0:T(8,128)(2,1)S(1)} %pad_maximum_fusion), channel_id=1, source_target_pairs={{0,2},{1,3},{2,0},{3,1},{4,6},{5,7},{6,4},{7,5},{8,10},{9,11},{10,... | collective-permute-start | bytes 786440 | tf_op jit(solution)/shard_map/ppermute | solution.py:31
  22.3 2.4 %collective-permute-start.6 = (bf16[384,1024]{1,0:T(8,128)(2,1)S(1)}, bf16[384,1024]{1,0:T(8,128)(2,1)S(1)}, u32[]{:S(2)}, u32[]{:S(2)}) collective-permute-start(bf16[384,1024]{1,0:T(8,128)(2,1)S(1)} %constant_dynamic-update-slice_fusion.u_ref), channel_id=1, source_target_pairs={{0,1},{1,0},{2,3},{3,2},{4,5},{5,4},{6,7},{7,6},{8,9},{9,8},{10,11... | collective-permute-start | bytes 2359304 | tf_op jit(solution)/shard_map/ppermute | solution.py:31
  22.7 5.7 %collective-permute-start.7 = (bf16[1024,256]{1,0:T(8,128)(2,1)S(1)}, bf16[1024,256]{1,0:T(8,128)(2,1)S(1)}, u32[]{:S(2)}, u32[]{:S(2)}) collective-permute-start(bf16[1024,256]{1,0:T(8,128)(2,1)S(1)} %get-tuple-element.76), channel_id=1, source_target_pairs={{0,1},{1,0},{2,3},{3,2},{4,5},{5,4},{6,7},{7,6},{8,9},{9,8},{10,11... | collective-permute-start | bytes 1572872 | tf_op jit(solution)/shard_map/ppermute | solution.py:31
  28.2 2.0 %collective-permute-start.8 = (bf16[256,1024]{1,0:T(8,128)(2,1)S(1)}, bf16[256,1024]{1,0:T(8,128)(2,1)S(1)}, u32[]{:S(2)}, u32[]{:S(2)}) collective-permute-start(bf16[256,1024]{1,0:T(8,128)(2,1)S(1)} %get-tuple-element.71.att_ref), channel_id=1, source_target_pairs={{0,1},{1,0},{2,3},{3,2},{4,5},{5,4},{6,7},{7,6},{8,9},{9,8},{10,11... | collective-permute-start | bytes 1572872 | tf_op jit(solution)/shard_map/ppermute | solution.py:31
  31.6 9.2 %collective-permute-start.9 = (bf16[256,512]{1,0:T(8,128)(2,1)S(1)}, bf16[256,512]{1,0:T(8,128)(2,1)S(1)}, u32[]{:S(2)}, u32[]{:S(2)}) collective-permute-start(bf16[256,512]{1,0:T(8,128)(2,1)S(1)} %get-tuple-element.78), channel_id=1, source_target_pairs={{0,4},{1,5},{2,6},{3,7},{4,0},{5,1},{6,2},{7,3},{8,12},{9,13},{10,... | collective-permute-start | bytes 786440 | tf_op jit(solution)/shard_map/ppermute | solution.py:31
  32.6 17.2 %collective-permute-start.10 = (bf16[256,512]{1,0:T(8,128)(2,1)S(1)}, bf16[256,512]{1,0:T(8,128)(2,1)S(1)}, u32[]{:S(2)}, u32[]{:S(2)}) collective-permute-start(bf16[256,512]{1,0:T(8,128)(2,1)S(1)} %get-tuple-element.79), channel_id=1, source_target_pairs={{0,12},{1,13},{2,14},{3,15},{4,8},{5,9},{6,10},{7,11},{8,4},{9,5},... | collective-permute-start | bytes 786440 | tf_op jit(solution)/shard_map/ppermute | solution.py:31
  34.8 15.0 %collective-permute-start.11 = (bf16[256,512]{1,0:T(8,128)(2,1)S(1)}, bf16[256,512]{1,0:T(8,128)(2,1)S(1)}, u32[]{:S(2)}, u32[]{:S(2)}) collective-permute-start(bf16[256,512]{1,0:T(8,128)(2,1)S(1)} %get-tuple-element.80), channel_id=1, source_target_pairs={{0,8},{1,9},{2,10},{3,11},{4,12},{5,13},{6,14},{7,15},{8,0},{9,1},... | collective-permute-start | bytes 786440 | tf_op jit(solution)/shard_map/ppermute | solution.py:31
  35.8 14.0 %collective-permute-start.12 = (bf16[1024,128]{1,0:T(8,128)(2,1)S(1)}, bf16[1024,128]{1,0:T(8,128)(2,1)S(1)}, u32[]{:S(2)}, u32[]{:S(2)}) collective-permute-start(bf16[1024,128]{1,0:T(8,128)(2,1)S(1)} %get-tuple-element.82), channel_id=1, source_target_pairs={{0,48},{16,32},{32,16},{48,0},{64,112},{80,96},{96,80},{112,64},{1... | collective-permute-start | bytes 786440 | tf_op jit(solution)/shard_map/ppermute | solution.py:31
  38.5 11.3 %collective-permute-start.13 = (bf16[1024,128]{1,0:T(8,128)(2,1)S(1)}, bf16[1024,128]{1,0:T(8,128)(2,1)S(1)}, u32[]{:S(2)}, u32[]{:S(2)}) collective-permute-start(bf16[1024,128]{1,0:T(8,128)(2,1)S(1)} %get-tuple-element.83), channel_id=1, source_target_pairs={{0,16},{16,0},{32,48},{48,32},{64,80},{80,64},{96,112},{112,96},{1... | collective-permute-start | bytes 786440 | tf_op jit(solution)/shard_map/ppermute | solution.py:31
  40.9 10.5 %collective-permute-start.14 = (bf16[1024,128]{1,0:T(8,128)(2,1)S(1)}, bf16[1024,128]{1,0:T(8,128)(2,1)S(1)}, u32[]{:S(2)}, u32[]{:S(2)}) collective-permute-start(bf16[1024,128]{1,0:T(8,128)(2,1)S(1)} %get-tuple-element.84), channel_id=1, source_target_pairs={{0,32},{16,48},{32,0},{48,16},{64,96},{80,112},{96,64},{112,80},{1... | collective-permute-start | bytes 786440 | tf_op jit(solution)/shard_map/ppermute | solution.py:31
  49.8 4.6 %copy-start.3 = (bf16[1,256,1024]{2,1,0:T(8,128)(2,1)S(1)}, bf16[1,256,1024]{2,1,0:T(8,128)(2,1)}, u32[]{:S(2)}) copy-start(bf16[1,256,1024]{2,1,0:T(8,128)(2,1)} %param.6) | copy-start | bytes 1572868
  49.8 4.6 %copy-start.5 = (bf16[1,256,1024]{2,1,0:T(8,128)(2,1)S(1)}, bf16[1,256,1024]{2,1,0:T(8,128)(2,1)}, u32[]{:S(2)}) copy-start(bf16[1,256,1024]{2,1,0:T(8,128)(2,1)} %param.7) | copy-start | bytes 1572868
  51.6 7.2 %collective-permute-start.17 = (bf16[640,1024]{1,0:T(8,128)(2,1)S(1)}, bf16[640,1024]{1,0:T(8,128)(2,1)S(1)}, u32[]{:S(2)}, u32[]{:S(2)}) collective-permute-start(bf16[640,1024]{1,0:T(8,128)(2,1)S(1)} %get-tuple-element.93), channel_id=1, source_target_pairs={{0,1},{1,0},{2,3},{3,2},{4,5},{5,4},{6,7},{7,6},{8,9},{9,8},{10,11... | collective-permute-start | bytes 3932168 | tf_op jit(solution)/shard_map/ppermute | solution.py:31
  51.7 6.2 %collective-permute-start.15 = (bf16[256,256]{1,0:T(8,128)(2,1)S(1)}, bf16[256,256]{1,0:T(8,128)(2,1)S(1)}, u32[]{:S(2)}, u32[]{:S(2)}) collective-permute-start(bf16[256,256]{1,0:T(8,128)(2,1)S(1)} %get-tuple-element.86), channel_id=1, source_target_pairs={{0,16},{16,0},{32,48},{48,32},{64,80},{80,64},{96,112},{112,96},{1... | collective-permute-start | bytes 393224 | tf_op jit(solution)/shard_map/ppermute | solution.py:31
  52.0 6.8 %collective-permute-start.16 = (bf16[512,128]{1,0:T(8,128)(2,1)S(1)}, bf16[512,128]{1,0:T(8,128)(2,1)S(1)}, u32[]{:S(2)}, u32[]{:S(2)}) collective-permute-start(bf16[512,128]{1,0:T(8,128)(2,1)S(1)} %get-tuple-element.88), channel_id=1, source_target_pairs={{0,12},{1,13},{2,14},{3,15},{4,8},{5,9},{6,10},{7,11},{8,4},{9,5},... | collective-permute-start | bytes 393224 | tf_op jit(solution)/shard_map/ppermute | solution.py:31
  59.0 13.3 %collective-permute-start.21 = (bf16[192,1024]{1,0:T(8,128)(2,1)S(1)}, bf16[192,1024]{1,0:T(8,128)(2,1)S(1)}, u32[]{:S(2)}, u32[]{:S(2)}) collective-permute-start(bf16[192,1024]{1,0:T(8,128)(2,1)S(1)} %get-tuple-element.104), channel_id=1, source_target_pairs={{0,2},{1,3},{2,0},{3,1},{4,6},{5,7},{6,4},{7,5},{8,10},{9,11},{10,... | collective-permute-start | bytes 1179656 | tf_op jit(solution)/shard_map/ppermute | solution.py:31
  60.2 6.0 %collective-permute-start.19 = (bf16[96,1024]{1,0:T(8,128)(2,1)S(1)}, bf16[96,1024]{1,0:T(8,128)(2,1)S(1)}, u32[]{:S(2)}, u32[]{:S(2)}) collective-permute-start(bf16[96,1024]{1,0:T(8,128)(2,1)S(1)} %get-tuple-element.97), channel_id=1, source_target_pairs={{0,4},{1,5},{2,6},{3,7},{4,0},{5,1},{6,2},{7,3},{8,12},{9,13},{10,... | collective-permute-start | bytes 589832 | tf_op jit(solution)/shard_map/ppermute | solution.py:31
  60.2 5.5 %collective-permute-start.18 = (bf16[256,128]{1,0:T(8,128)(2,1)S(1)}, bf16[256,128]{1,0:T(8,128)(2,1)S(1)}, u32[]{:S(2)}, u32[]{:S(2)}) collective-permute-start(bf16[256,128]{1,0:T(8,128)(2,1)S(1)} %get-tuple-element.95), channel_id=1, source_target_pairs={{0,48},{16,32},{32,16},{48,0},{64,112},{80,96},{96,80},{112,64},{1... | collective-permute-start | bytes 196616 | tf_op jit(solution)/shard_map/ppermute | solution.py:31
  66.3 6.0 %collective-permute-start.20 = (bf16[64,1024]{1,0:T(8,128)(2,1)S(1)}, bf16[64,1024]{1,0:T(8,128)(2,1)S(1)}, u32[]{:S(2)}, u32[]{:S(2)}) collective-permute-start(bf16[64,1024]{1,0:T(8,128)(2,1)S(1)} %get-tuple-element.100), channel_id=1, source_target_pairs={{0,2},{1,3},{2,0},{3,1},{4,6},{5,7},{6,4},{7,5},{8,10},{9,11},{10,... | collective-permute-start | bytes 393224 | tf_op jit(solution)/shard_map/ppermute | solution.py:31
  72.3 5.8 %collective-permute-start.22 = (bf16[128,256]{1,0:T(8,128)(2,1)S(1)}, bf16[128,256]{1,0:T(8,128)(2,1)S(1)}, u32[]{:S(2)}, u32[]{:S(2)}) collective-permute-start(bf16[128,256]{1,0:T(8,128)(2,1)S(1)} %get-tuple-element.105), channel_id=1, source_target_pairs={{0,64},{16,80},{32,96},{48,112},{64,0},{80,16},{96,32},{112,48},{1... | collective-permute-start | bytes 196616 | tf_op jit(solution)/shard_map/ppermute | solution.py:31
  78.2 8.4 %collective-permute-start.23 = (bf16[128,256]{1,0:T(8,128)(2,1)S(1)}, bf16[128,256]{1,0:T(8,128)(2,1)S(1)}, u32[]{:S(2)}, u32[]{:S(2)}) collective-permute-start(bf16[128,256]{1,0:T(8,128)(2,1)S(1)} %add_convert_fusion.1), channel_id=1, source_target_pairs={{0,192},{16,208},{32,224},{48,240},{64,128},{80,144},{96,160},{112... | collective-permute-start | bytes 196616 | tf_op jit(solution)/shard_map/ppermute | solution.py:31
  83.7 7.5 %collective-permute-start.26 = (bf16[32,1024]{1,0:T(8,128)(2,1)S(1)}, bf16[32,1024]{1,0:T(8,128)(2,1)S(1)}, u32[]{:S(2)}, u32[]{:S(2)}) collective-permute-start(bf16[32,1024]{1,0:T(8,128)(2,1)S(1)} %get-tuple-element.109), channel_id=1, source_target_pairs={{0,12},{1,13},{2,14},{3,15},{4,8},{5,9},{6,10},{7,11},{8,4},{9,5},... | collective-permute-start | bytes 196616 | tf_op jit(solution)/shard_map/ppermute | solution.py:31
  86.1 5.2 %collective-permute-start.25 = (bf16[64,1024]{1,0:T(8,128)(2,1)S(1)}, bf16[64,1024]{1,0:T(8,128)(2,1)S(1)}, u32[]{:S(2)}, u32[]{:S(2)}) collective-permute-start(bf16[64,1024]{1,0:T(8,128)(2,1)S(1)} %shard_map.96), channel_id=1, source_target_pairs={{0,4},{1,5},{2,6},{3,7},{4,0},{5,1},{6,2},{7,3},{8,12},{9,13},{10,... | collective-permute-start | bytes 393224 | tf_op jit(solution)/shard_map/ppermute | solution.py:31
  86.5 6.8 %collective-permute-start.24 = (bf16[128,256]{1,0:T(8,128)(2,1)S(1)}, bf16[128,256]{1,0:T(8,128)(2,1)S(1)}, u32[]{:S(2)}, u32[]{:S(2)}) collective-permute-start(bf16[128,256]{1,0:T(8,128)(2,1)S(1)} %add_convert_fusion.a), channel_id=1, source_target_pairs={{0,32},{16,48},{32,0},{48,16},{64,96},{80,112},{96,64},{112,80},{1... | collective-permute-start | bytes 196616 | tf_op jit(solution)/shard_map/ppermute | solution.py:31
  90.6 4.3 %collective-permute-start.27 = (bf16[128,256]{1,0:T(8,128)(2,1)S(1)}, bf16[128,256]{1,0:T(8,128)(2,1)S(1)}, u32[]{:S(2)}, u32[]{:S(2)}) collective-permute-start(bf16[128,256]{1,0:T(8,128)(2,1)S(1)} %add_convert_fusion.a), channel_id=1, source_target_pairs={{0,16},{16,0},{32,48},{48,32},{64,80},{80,64},{96,112},{112,96},{1... | collective-permute-start | bytes 196616 | tf_op jit(solution)/shard_map/ppermute | solution.py:31
  90.6 5.5 %collective-permute-start.28 = (bf16[128,256]{1,0:T(8,128)(2,1)S(1)}, bf16[128,256]{1,0:T(8,128)(2,1)S(1)}, u32[]{:S(2)}, u32[]{:S(2)}) collective-permute-start(bf16[128,256]{1,0:T(8,128)(2,1)S(1)} %add_convert_fusion.a), channel_id=1, source_target_pairs={{0,48},{16,32},{32,16},{48,0},{64,112},{80,96},{96,80},{112,64},{1... | collective-permute-start | bytes 196616 | tf_op jit(solution)/shard_map/ppermute | solution.py:31
